TPU v7x, 32 devices: a whole 2x2x4 slice. The times are simulated.
32 devices in a mesh: fsdp: 8 (over z, core), seq: 4 (over y, x).
Axes of the slice: x: 2, y: 2, z: 4, core: 2. Of those that a mesh axis runs over, the one named last changes fastest.
Arguments:
- inputs: bfloat16 [8, 2048, 2048], P('fsdp', 'seq'), may hold values from -6 to 6
- cotangent: bfloat16 [8, 2048, 2048], P('fsdp', 'seq'), may hold values from -6 to 6
- segments: int32 [8, 2048], P('fsdp', 'seq'), may hold values from 0 to 10, as said below
- valid_mask: int32 [8, 2048], P('fsdp', 'seq'), may hold values from 0 to 1, as said below
- query_weight: bfloat16 [2048, 2048], P('fsdp'), may hold values from -0.125 to 0.125
- key_weight: bfloat16 [2048, 512], P('fsdp'), may hold values from -0.125 to 0.125
- value_weight: bfloat16 [2048, 512], P('fsdp'), may hold values from -0.125 to 0.125
- out_weight: bfloat16 [2048, 2048], P(None, 'fsdp'), may hold values from -2 to 2
- gate_weight: bfloat16 [2048, 8192], P('fsdp'), may hold values from -0.125 to 0.125
- up_weight: bfloat16 [2048, 8192], P('fsdp'), may hold values from -0.125 to 0.125
- down_weight: bfloat16 [8192, 2048], P(None, 'fsdp'), may hold values from -0.0625 to 0.0625
- attn_gain: bfloat16 [2048], P('fsdp'), may hold values from 0.5 to 1.5
- mlp_gain: bfloat16 [2048], P('fsdp'), may hold values from 0.5 to 1.5
Outputs:
- outputs: bfloat16 [8, 2048, 2048], P('fsdp', 'seq')
- input_grad: bfloat16 [8, 2048, 2048], P('fsdp', 'seq')
- query_grad: float32 [2048, 2048], P('fsdp')
- key_grad: float32 [2048, 512], P('fsdp')
- value_grad: float32 [2048, 512], P('fsdp')
- out_grad: float32 [2048, 2048], P(None, 'fsdp')
- gate_grad: float32 [2048, 8192], P('fsdp')
- up_grad: float32 [2048, 8192], P('fsdp')
- down_grad: float32 [8192, 2048], P(None, 'fsdp')
- attn_gain_grad: float32 [2048], P('fsdp')
- mlp_gain_grad: float32 [2048], P('fsdp')
- rms_stats: float32 [8, 5], P('fsdp')
Inputs may be any that keep to these rules, and one draw needn't show every extreme that they name: `segments`: in each sequence the numbers start at 0, never fall and rise by one where a new document begins; every document but the last of its sequence holds 204 tokens or more. `valid_mask`: in each sequence the pads, if any, are its last tokens; most tokens are valid.
All inputs are finite; a program needn't handle non-finite values.
Results may differ from a plain program's by a relative error of at most 0.02.
Values may be sent and summed in bfloat16 or wider, within the bound.
No kernel may reach another device: no remote copies, remote signals or barrier semaphores. Data moves between devices by JAX's collectives and lax.ppermute only.
A program may use at most 704 MiB of HBM per device.

v0:
```python
import jax
import jax.numpy as jnp
from jax import lax
from jax.sharding import PartitionSpec as P

D = 2048
HEADS = 32
KV_HEADS = 8
HEAD_DIM = 64
FF = 8192


EPSILON = 1e-05
ROPE_BASE = 500000.0
NEGATIVE = -1e30
CONTRACT_COLS = (((1,), (1,)), ((), ()))


def norm_scale(values):
    return lax.rsqrt(jnp.mean(values * values, axis=-1, keepdims=True) + EPSILON)


def norm_back(grad_normed, values, inv_rms, gain_row):
    unit_rows = values * inv_rms
    scaled = grad_normed * gain_row
    return inv_rms * (scaled - unit_rows * jnp.mean(scaled * unit_rows, axis=-1, keepdims=True))


def doc_positions(segment_ids):
    length = segment_ids.shape[0]
    places = jnp.arange(length, dtype=jnp.int32)
    boundary = jnp.concatenate([jnp.ones((1,), jnp.bool_), segment_ids[1:] != segment_ids[:-1]])
    starts = lax.cummax(jnp.where(boundary, places, 0), axis=0)
    return places - starts


def rotate(values, places, head_count, direction):
    length = values.shape[0]
    half_dim = HEAD_DIM // 2
    per_head = values.reshape(length, head_count, HEAD_DIM)
    frequency = ROPE_BASE ** (-2.0 * jnp.arange(half_dim, dtype=jnp.float32) / HEAD_DIM)
    angles = places.astype(jnp.float32)[:, None] * frequency[None, :]
    cosine = jnp.cos(angles)[:, None, :]
    sine_part = direction * jnp.sin(angles)[:, None, :]
    first_half = per_head[..., :half_dim]
    second_half = per_head[..., half_dim:]
    turned = jnp.concatenate(
        [
            first_half * cosine - second_half * sine_part,
            second_half * cosine + first_half * sine_part,
        ],
        axis=-1,
    )
    return turned.reshape(length, head_count * HEAD_DIM)


def visible(block_start, block_rows, segment_ids, valid_ids):
    length = segment_ids.shape[0]
    query_pos = block_start + jnp.arange(block_rows, dtype=jnp.int32)
    key_pos = jnp.arange(length, dtype=jnp.int32)
    query_seg = lax.dynamic_slice_in_dim(segment_ids, block_start, block_rows, 0)
    query_valid = lax.dynamic_slice_in_dim(valid_ids, block_start, block_rows, 0)
    allowed = (
        (query_seg[:, None] == segment_ids[None, :])
        & (key_pos[None, :] <= query_pos[:, None])
        & (query_valid[:, None] == 1)
    )
    return allowed | (key_pos[None, :] == query_pos[:, None])


def split_heads(query_heads, pair_heads):
    length = query_heads.shape[0]
    kv_local = pair_heads.shape[1] // (2 * HEAD_DIM)
    group = HEADS // KV_HEADS
    query_four = query_heads.reshape(length, kv_local, group, HEAD_DIM)
    pair_four = pair_heads.reshape(length, kv_local, 2, HEAD_DIM)
    return (query_four, pair_four[:, :, 0], pair_four[:, :, 1])


def block_scores(query_block, key_three, block_start, segment_ids, valid_ids):
    block_rows = query_block.shape[0]
    scores = jnp.einsum(
        "qkgd,skd->kgqs", query_block, key_three, preferred_element_type=jnp.float32
    ) * HEAD_DIM ** (-0.5)
    allowed = visible(block_start, block_rows, segment_ids, valid_ids)
    return jnp.where(allowed[None, None], scores, NEGATIVE)


def attend_forward(query_heads, pair_heads, segment_ids, valid_ids):
    length = query_heads.shape[0]
    query_four, key_three, value_three = split_heads(query_heads, pair_heads)
    block_rows = min(512, length)

    def one_block(index):
        block_start = index * block_rows
        query_block = lax.dynamic_slice_in_dim(query_four, block_start, block_rows, 0)
        scores = block_scores(query_block, key_three, block_start, segment_ids, valid_ids)
        peak = jnp.max(scores, axis=-1, keepdims=True)
        expo = jnp.exp(scores - peak)
        total = jnp.sum(expo, axis=-1, keepdims=True)
        probs_low = (expo / total).astype(jnp.bfloat16)
        block_out = jnp.einsum(
            "kgqs,skd->qkgd", probs_low, value_three, preferred_element_type=jnp.float32
        )
        return (block_out.astype(jnp.bfloat16), (peak + jnp.log(total))[..., 0])

    block_outs, log_totals = lax.map(one_block, jnp.arange(length // block_rows, dtype=jnp.int32))
    return (block_outs.reshape(length, query_heads.shape[1]), log_totals)


def attend_backward(query_heads, pair_heads, grad_heads, log_totals, segment_ids, valid_ids):
    length = query_heads.shape[0]
    query_four, key_three, value_three = split_heads(query_heads, pair_heads)
    grad_four = grad_heads.reshape(query_four.shape)
    block_rows = min(512, length)

    def step(carry, items):
        key_sum, value_sum = carry
        index, block_totals = items
        block_start = index * block_rows
        query_block = lax.dynamic_slice_in_dim(query_four, block_start, block_rows, 0)
        grad_block = lax.dynamic_slice_in_dim(grad_four, block_start, block_rows, 0)
        scores = block_scores(query_block, key_three, block_start, segment_ids, valid_ids)
        probs = jnp.exp(scores - block_totals[..., None])
        probs_low = probs.astype(jnp.bfloat16)
        value_sum = value_sum + jnp.einsum(
            "kgqs,qkgd->skd", probs_low, grad_block, preferred_element_type=jnp.float32
        )
        grad_probs = jnp.einsum(
            "qkgd,skd->kgqs", grad_block, value_three, preferred_element_type=jnp.float32
        )
        inner = jnp.sum(probs * grad_probs, axis=-1, keepdims=True)
        grad_scores = (probs * (grad_probs - inner)).astype(jnp.bfloat16)
        query_part = jnp.einsum(
            "kgqs,skd->qkgd", grad_scores, key_three, preferred_element_type=jnp.float32
        ) * HEAD_DIM ** (-0.5)
        key_sum = key_sum + jnp.einsum(
            "kgqs,qkgd->skd", grad_scores, query_block, preferred_element_type=jnp.float32
        ) * HEAD_DIM ** (-0.5)
        return ((key_sum, value_sum), query_part.astype(jnp.bfloat16))

    start_sums = (
        jnp.zeros(key_three.shape, jnp.float32),
        jnp.zeros(value_three.shape, jnp.float32),
    )
    indices = jnp.arange(length // block_rows, dtype=jnp.int32)
    (key_sum, value_sum), query_parts = lax.scan(step, start_sums, (indices, log_totals))
    grad_query_heads = query_parts.reshape(length, query_heads.shape[1])
    grad_pair_heads = (
        jnp.stack([key_sum, value_sum], axis=2)
        .astype(jnp.bfloat16)
        .reshape(length, pair_heads.shape[1])
    )
    return (grad_query_heads, grad_pair_heads)


def block_term(pairs, count, group_count, seq_parts, shard_rows):
    block_count = count // shard_rows
    token_rows = pairs[0][0].shape[0]
    group_span = min(group_count, (block_count + 2 * seq_parts - 2) // seq_parts)
    pieces = []
    for left_side, right_side in pairs:
        left_cols = left_side
        left_cols = left_cols.reshape(token_rows, group_span, shard_rows)
        right_parts = right_side.reshape(token_rows, seq_parts, right_side.shape[1] // seq_parts)
        pieces.append(
            jnp.einsum("tfr,tsc->fsrc", left_cols, right_parts, preferred_element_type=jnp.float32)
        )
    full_term = jnp.concatenate(pieces, axis=3)
    full_term = full_term.reshape(group_span * seq_parts * shard_rows, full_term.shape[3])
    return full_term


def body(
    inputs,
    cotangent,
    segments,
    valid_mask,
    query_weight,
    key_weight,
    value_weight,
    out_weight,
    gate_weight,
    up_weight,
    down_weight,
    attn_gain,
    mlp_gain,
):
    fsdp_count = lax.axis_size("fsdp")
    seq_index = lax.axis_index("seq")
    fsdp_index = lax.axis_index("fsdp")
    local_rows = inputs.shape[1]
    query_width = HEADS * HEAD_DIM
    pair_width = KV_HEADS * HEAD_DIM
    segment_all, valid_all = (
        lax.all_gather(segments[0], "seq", axis=0, tiled=True),
        lax.all_gather(valid_mask[0], "seq", axis=0, tiled=True),
    )
    places = lax.dynamic_slice_in_dim(
        doc_positions(segment_all), seq_index * local_rows, local_rows, 0
    )
    valid_rows = valid_mask[0].astype(jnp.float32)
    valid_col = valid_rows[:, None]
    query_full, key_full, value_full, out_full, attn_gain_full = (
        lax.all_gather(query_weight, "fsdp", axis=0, tiled=True),
        lax.all_gather(key_weight, "fsdp", axis=0, tiled=True),
        lax.all_gather(value_weight, "fsdp", axis=0, tiled=True),
        lax.all_gather(out_weight, "fsdp", axis=1, tiled=True),
        lax.all_gather(attn_gain, "fsdp", axis=0, tiled=True),
    )
    tokens = inputs[0].astype(jnp.float32)
    inv_one = norm_scale(tokens)
    gain_one = attn_gain_full.astype(jnp.float32)
    normed_one = (tokens * inv_one * gain_one).astype(jnp.bfloat16)
    query_lin = jnp.dot(normed_one, query_full, preferred_element_type=jnp.float32)
    key_lin = jnp.dot(normed_one, key_full, preferred_element_type=jnp.float32)
    value_lin = jnp.dot(normed_one, value_full, preferred_element_type=jnp.float32)
    query_low = rotate(query_lin, places, HEADS, 1.0).astype(jnp.bfloat16)
    key_low = (
        rotate(key_lin, places, KV_HEADS, 1.0)
        .astype(jnp.bfloat16)
        .reshape(local_rows, KV_HEADS, HEAD_DIM)
    )
    value_low = value_lin.astype(jnp.bfloat16).reshape(local_rows, KV_HEADS, HEAD_DIM)
    pair_low = jnp.stack([key_low, value_low], axis=2).reshape(local_rows, 2 * pair_width)
    query_heads, pair_heads = (
        lax.all_to_all(query_low, "seq", split_axis=1, concat_axis=0, tiled=True),
        lax.all_to_all(pair_low, "seq", split_axis=1, concat_axis=0, tiled=True),
    )
    heads_out, log_totals = attend_forward(query_heads, pair_heads, segment_all, valid_all)
    heads_tokens = lax.all_to_all(heads_out, "seq", split_axis=0, concat_axis=1, tiled=True)
    attn_branch = jnp.dot(heads_tokens, out_full, preferred_element_type=jnp.float32)
    middle = tokens + attn_branch
    gate_full, up_full, down_full, mlp_gain_full = (
        lax.all_gather(gate_weight, "fsdp", axis=0, tiled=True),
        lax.all_gather(up_weight, "fsdp", axis=0, tiled=True),
        lax.all_gather(down_weight, "fsdp", axis=1, tiled=True),
        lax.all_gather(mlp_gain, "fsdp", axis=0, tiled=True),
    )
    inv_two = norm_scale(middle)
    gain_two = mlp_gain_full.astype(jnp.float32)
    normed_two = (middle * inv_two * gain_two).astype(jnp.bfloat16)
    gate_lin = jnp.dot(normed_two, gate_full, preferred_element_type=jnp.float32)
    up_lin = jnp.dot(normed_two, up_full, preferred_element_type=jnp.float32)
    sigmoid_gate = jax.nn.sigmoid(gate_lin)
    silu_gate = gate_lin * sigmoid_gate
    activated = (silu_gate * up_lin).astype(jnp.bfloat16)
    mlp_branch = jnp.dot(activated, down_full, preferred_element_type=jnp.float32)
    final = middle + mlp_branch
    outputs = final.astype(jnp.bfloat16)[None]
    squares = [
        jnp.sum(valid_col * branch_part * branch_part)
        for branch_part in (tokens, middle, final, attn_branch, mlp_branch)
    ]
    stat_row = jnp.stack([jnp.sum(valid_rows)] + squares)
    grad_final = cotangent[0].astype(jnp.float32) * valid_col
    grad_mlp_low = grad_final.astype(jnp.bfloat16)
    grad_act = lax.dot_general(
        grad_mlp_low, down_full, CONTRACT_COLS, preferred_element_type=jnp.float32
    )
    grad_gate_low = (
        grad_act * up_lin * sigmoid_gate * (1.0 + gate_lin * (1.0 - sigmoid_gate))
    ).astype(jnp.bfloat16)
    grad_up_low = (grad_act * silu_gate).astype(jnp.bfloat16)
    grad_normed_two = lax.dot_general(
        grad_gate_low, gate_full, CONTRACT_COLS, preferred_element_type=jnp.float32
    ) + lax.dot_general(grad_up_low, up_full, CONTRACT_COLS, preferred_element_type=jnp.float32)
    gain_two_term = jnp.sum(grad_normed_two * middle * inv_two, axis=0)
    grad_middle = grad_final + norm_back(grad_normed_two, middle, inv_two, gain_two)
    gate_up_low = jnp.concatenate([grad_gate_low, grad_up_low], axis=1)
    grad_attn_low = grad_middle.astype(jnp.bfloat16)
    grad_heads_tokens = lax.dot_general(
        grad_attn_low, out_full, CONTRACT_COLS, preferred_element_type=jnp.float32
    ).astype(jnp.bfloat16)
    grad_heads = lax.all_to_all(grad_heads_tokens, "seq", split_axis=1, concat_axis=0, tiled=True)
    grad_query_heads, grad_pair_heads = attend_backward(
        query_heads, pair_heads, grad_heads, log_totals, segment_all, valid_all
    )
    grad_query_tokens, grad_pair_tokens = (
        lax.all_to_all(grad_query_heads, "seq", split_axis=0, concat_axis=1, tiled=True),
        lax.all_to_all(grad_pair_heads, "seq", split_axis=0, concat_axis=1, tiled=True),
    )
    grad_pair_split = grad_pair_tokens.reshape(local_rows, KV_HEADS, 2, HEAD_DIM)
    grad_key_rot = grad_pair_split[:, :, 0].reshape(local_rows, pair_width)
    grad_value_low = grad_pair_split[:, :, 1].reshape(local_rows, pair_width)
    grad_query_low = rotate(grad_query_tokens.astype(jnp.float32), places, HEADS, -1.0).astype(
        jnp.bfloat16
    )
    grad_key_low = rotate(grad_key_rot.astype(jnp.float32), places, KV_HEADS, -1.0).astype(
        jnp.bfloat16
    )
    grad_normed_one = lax.dot_general(
        grad_query_low, query_full, CONTRACT_COLS, preferred_element_type=jnp.float32
    )
    grad_normed_one = grad_normed_one + lax.dot_general(
        grad_key_low, key_full, CONTRACT_COLS, preferred_element_type=jnp.float32
    )
    grad_normed_one = grad_normed_one + lax.dot_general(
        grad_value_low, value_full, CONTRACT_COLS, preferred_element_type=jnp.float32
    )
    gain_one_term = jnp.sum(grad_normed_one * tokens * inv_one, axis=0)
    input_grad = (grad_middle + norm_back(grad_normed_one, tokens, inv_one, gain_one)).astype(
        jnp.bfloat16
    )[None]
    projected_low = jnp.concatenate([grad_query_low, grad_key_low, grad_value_low], axis=1)
    attn_pairs = ((normed_one, projected_low), (grad_attn_low, heads_tokens))
    mlp_pairs = ((normed_two, gate_up_low), (grad_mlp_low, activated))
    shard_rows = D // fsdp_count
    attn_part = lax.psum_scatter(
        block_term(
            attn_pairs, lax.axis_size("fsdp") * shard_rows, fsdp_count, 1, shard_rows
        ).astype(jnp.bfloat16),
        "fsdp",
        scatter_dimension=0,
        tiled=True,
    )
    mlp_part = lax.psum_scatter(
        block_term(mlp_pairs, lax.axis_size("fsdp") * shard_rows, fsdp_count, 1, shard_rows).astype(
            jnp.bfloat16
        ),
        "fsdp",
        scatter_dimension=0,
        tiled=True,
    )
    attn_total, mlp_total = (
        lax.psum(attn_part, "seq").astype(jnp.float32),
        lax.psum(mlp_part, "seq").astype(jnp.float32),
    )
    stat_table = (
        jax.nn.one_hot(fsdp_index, fsdp_count, dtype=jnp.float32)[:, None] * stat_row[None, :]
    )
    gain_one_sum, gain_two_sum, stat_sum = lax.psum(
        (gain_one_term, gain_two_term, stat_table), ("fsdp", "seq")
    )
    query_grad = attn_total[:, :query_width]
    key_grad = attn_total[:, query_width : query_width + pair_width]
    value_grad = attn_total[:, query_width + pair_width : query_width + 2 * pair_width]
    out_grad = attn_total[:, query_width + 2 * pair_width :].T
    gate_grad = mlp_total[:, :FF]
    up_grad = mlp_total[:, FF : 2 * FF]
    down_grad = mlp_total[:, 2 * FF :].T
    attn_gain_grad = lax.dynamic_slice_in_dim(gain_one_sum, fsdp_index * shard_rows, shard_rows, 0)
    mlp_gain_grad = lax.dynamic_slice_in_dim(gain_two_sum, fsdp_index * shard_rows, shard_rows, 0)
    own_stats = lax.dynamic_slice_in_dim(stat_sum, fsdp_index, 1, 0)
    rms_stats = jnp.sqrt(own_stats[:, 1:] / (own_stats[:, :1] * D))
    return (
        outputs,
        input_grad,
        query_grad,
        key_grad,
        value_grad,
        out_grad,
        gate_grad,
        up_grad,
        down_grad,
        attn_gain_grad,
        mlp_gain_grad,
        rms_stats,
    )


def solution(mesh):
    placed = (
        P("fsdp", "seq", None),
        P("fsdp", "seq", None),
        P("fsdp", "seq"),
        P("fsdp", "seq"),
        P("fsdp", None),
        P("fsdp", None),
        P("fsdp", None),
        P(None, "fsdp"),
        P("fsdp", None),
        P("fsdp", None),
        P(None, "fsdp"),
        P("fsdp"),
        P("fsdp"),
    )
    return jax.shard_map(
        body,
        mesh=mesh,
        in_specs=placed,
        out_specs=(
            P("fsdp", "seq", None),
            P("fsdp", "seq", None),
            P("fsdp", None),
            P("fsdp", None),
            P("fsdp", None),
            P(None, "fsdp"),
            P("fsdp", None),
            P("fsdp", None),
            P(None, "fsdp"),
            P("fsdp"),
            P("fsdp"),
            P("fsdp", None),
        ),
        check_vma=False,
    )
```

profile of v0, /device:TPU:0, one launch (start us, length us, event | category | flops | bytes accessed | tf_op | source)
XLA Modules:
  0.0 3359.9 jit_solution(3193061748657249352)
XLA Ops:
  79.5 75.4 %all-gather.12.cloned.1.call-done = bf16[2048,2048]{1,0:T(8,128)(2,1)} async-done(((bf16[256,2048]{1,0:T(8,128)(2,1)}), bf16[2048,2048]{1,0:T(8,128)(2,1)}) %all-gather.12.cloned.1.call-update) | async-done | bytes 8388624 | tf_op jit(solution)/shard_map/all_gather | solution.py:205
  181.3 28.7 all-gather.1
  222.3 202.4 %while.27 = (s32[]{:T(128)}, bf16[4,512,2,4,64]{1,4,3,2,0:T(8,128)(2,1)}, f32[4,2,4,512]{3,2,1,0:T(4,128)}, s32[4]{0:T(128)S(1)}, s32[2048]{0:T(1024)S(1)}, /*in...) while((s32[]{:T(128)}, ...), condition=%wide.region_6.7_spmd, body=%wide.region_3.6_spmd.sunk | while | flops 2254697472 | bytes 107107536 | solution.py:107
  468.0 57.8 %all-gather.22.cloned.1.call-done = bf16[2048,8192]{1,0:T(8,128)(2,1)} async-done(((bf16[256,8192]{1,0:T(8,128)(2,1)}), bf16[2048,8192]{1,0:T(8,128)(2,1)}) %all-gather.22.cloned.1.call-update) | async-done | bytes 33554448 | tf_op jit(solution)/shard_map/all_gather | solution.py:236
  525.8 26.6 fusion.123
  552.5 261.6 %all-gather.20.cloned.1.call-done = bf16[2048,8192]{1,0:T(8,128)(2,1)} async-done(((bf16[256,8192]{1,0:T(8,128)(2,1)}), bf16[2048,8192]{1,0:T(8,128)(2,1)}) %all-gather.20.cloned.1.call-update) | async-done | bytes 33554448 | tf_op jit(solution)/shard_map/all_gather | solution.py:235
  814.1 27.9 fusion.122
  842.0 262.4 %all-gather.24.cloned.1.call-done = bf16[8192,2048]{1,0:T(8,128)(2,1)} async-done(((bf16[8192,256]{1,0:T(8,128)(2,1)}), bf16[8192,2048]{1,0:T(8,128)(2,1)}) %all-gather.24.cloned.1.call-update) | async-done | bytes 33554448 | tf_op jit(solution)/shard_map/all_gather | solution.py:237
  1104.3 38.0 %multiply_convert_fusion = (bf16[512,8192]{1,0:T(8,128)(2,1)}, bf16[512,8192]{1,0:T(8,128)(2,1)}, bf16[512,8192]{1,0:T(8,128)(2,1)}) fusion(f32[512,8192]{1,0:T(8,128)} %fusion.122, f32[512,8192]{1,0:T(8,128)} %fusion.123, bf16[8192,2048]{1,0:T(8,128)(2,1)} %all-gather.24.cloned.1.call-done, bf16[1,512,2048]{2,1,0:T(8,128)(2,1)S(1)} %copy-done.12, ...), kind=kOutput, calls=%fused_computation.75 | convolution fusion | flops 17245929472 | bytes 94373888 | tf_op jit(solution)/shard_map/dot_general | solution.py:258
  1193.0 28.8 fusion.66
  1239.9 25.6 all-to-all-done.3
  1276.2 411.3 %while.28 = (s32[]{:T(128)}, f32[2048,2,64]{0,2,1:T(8,128)S(1)}, f32[2048,2,64]{0,2,1:T(8,128)}, bf16[4,512,2,4,64]{1,4,3,2,0:T(8,128)(2,1)}, s32[4]{0:T(128)S(1...) while((s32[]{:T(128)}, f32[2048,2,64]{0,2,1:T(8,128)S(1)}, ...), condition=%wide.region_11.12_spmd.clone, body=%wide.region_9.11_spmd.clone.sunk | while | flops 5502661632 | bytes 348263776 | solution.py:147
  1334.9 27.8 fusion.189
  1437.5 27.8 fusion.189
  1540.2 27.8 fusion.189
  1642.9 27.8 fusion.189
  1768.5 26.0 copy.91
  1797.3 26.2 convert_bitcast_fusion.1
  1823.5 42.1 %convert_bitcast_fusion = bf16[8,1,256,16384]{2,3,0,1:T(8,128)(2,1)} fusion(bf16[512,8192]{1,0:T(8,128)(2,1)} %get-tuple-element.295, bf16[512,8192]{1,0:T(8,128)(2,1)} %get-tuple-element.296, bf16[64,8,8,256]{3,2,1,0:T(8,128)(2,1)S(1)} %bitcast.383), kind=kOutput, calls=%fused_computation.69 | convolution fusion | flops 34426847232 | bytes 85983232 | tf_op jit(solution)/shard_map/tfr,tsc->fsrc/dot_general | solution.py:167
  1865.5 72.6 %pad_maximum_fusion = bf16[8,1,256,24576]{2,3,0,1:T(8,128)(2,1)} fusion(bf16[8,1,256,8192]{2,3,0,1:T(8,128)(2,1)} %convert_bitcast_fusion.1, bf16[8,1,256,16384]{2,3,0,1:T(8,128)(2,1)} %convert_bitcast_fusion), kind=kLoop, calls=%fused_computation.68 | loop fusion | flops 201326592 | bytes 201326592 | tf_op jit(solution)/shard_map/concatenate | solution.py:169
  1938.2 120.1 %copy.96 = bf16[8,1,256,24576]{3,2,0,1:T(8,128)(2,1)} copy(bf16[8,1,256,24576]{2,3,0,1:T(8,128)(2,1)} %pad_maximum_fusion) | data formatting | bytes 201326592 | tf_op jit(solution)/shard_map/concatenate | solution.py:169
  2058.8 954.7 %reduce-scatter.7.cloned.1.call-done = bf16[256,24576]{1,0:T(8,128)(2,1)} async-done(((bf16[2048,24576]{1,0:T(8,128)(2,1)}), bf16[256,24576]{1,0:T(8,128)(2,1)}) %reduce-scatter.7.cloned.1.call-update) | async-done | bytes 12582928
  3034.2 38.4 %all-reduce.1 = (f32[2048]{0:T(1024)S(1)}, f32[2048]{0:T(1024)S(1)}, f32[8,6]{1,0:T(8,128)S(1)}) all-reduce(f32[2048]{0:T(1024)S(1)} %get-tuple-element.230, f32[2048]{0:T(1024)S(1)} %copy-done.52, f32[8,6]{1,0:T(8,128)S(1)} %broadcast_multiply_fusion.1), channel_id=1, replica_groups=mesh['fsdp'=8,'seq'=4] {'fsdp','seq'}, use_global_device_ids=true, to_apply=%region_18.19 | all-reduce | flops 4144 | bytes 33152 | tf_op jit(solution)/shard_map/psum | solution.py:332
  3080.4 219.9 %all-reduce.5.cloned.1.call-done = (bf16[256,5120]{1,0:T(8,128)(2,1)}, bf16[256,24576]{1,0:T(8,128)(2,1)}) async-done(((bf16[256,5120]{1,0:T(8,128)(2,1)}, bf16[256,24576]{1,0:T(8,128)(2,1)}), (bf16[256,5120]{1,0:T(8,128)(2,1)}, bf16[256,24576]{1,0:T(8,128)(2,1)})) %all-reduce.5.cloned.1.call-update) | async-done | bytes 15204368 | tf_op jit(solution)/shard_map/psum | solution.py:326
  (344 shorter events, 894.7 us)
Async XLA Ops:
  7.2 34.3 %all-gather.14.cloned.1.call-start = ((), (), s32[]{:S(2)}) async-start(), calls=%async_computation.9 | async-start | bytes 2359296 | tf_op jit(solution)/shard_map/all_gather | solution.py:206
  7.9 63.8 %all-gather.16.cloned.1.call-start = ((), (), s32[]{:S(2)}) async-start(), calls=%async_computation.10 | async-start | bytes 2359296 | tf_op jit(solution)/shard_map/all_gather | solution.py:207
  8.7 146.3 %all-gather.12.cloned.1.call-start = ((), (), s32[]{:S(2)}) async-start(), calls=%async_computation.8 | async-start | bytes 9437184 | tf_op jit(solution)/shard_map/all_gather | solution.py:205
  9.4 428.7 %all-gather.18.cloned.1.call-start = ((), (), s32[]{:S(2)}) async-start(), calls=%async_computation.11 | async-start | bytes 9437184 | tf_op jit(solution)/shard_map/all_gather | solution.py:208
  10.0 515.8 %all-gather.22.cloned.1.call-start = ((), (), s32[]{:S(2)}) async-start(), calls=%async_computation.13 | async-start | bytes 37748736 | tf_op jit(solution)/shard_map/all_gather | solution.py:236
  10.6 803.5 %all-gather.20.cloned.1.call-start = ((), (), s32[]{:S(2)}) async-start(), calls=%async_computation.12 | async-start | bytes 37748736 | tf_op jit(solution)/shard_map/all_gather | solution.py:235
  11.2 1093.2 %all-gather.24.cloned.1.call-start = ((), (), s32[]{:S(2)}) async-start(), calls=%async_computation.14 | async-start | bytes 37748736 | tf_op jit(solution)/shard_map/all_gather | solution.py:237
  34.3 133.0 %copy-start.34 = (f32[8,1,256]{2,1,0:T(1,128)}, f32[8,1,256]{2,1,0:T(1,128)S(1)}, u32[]{:S(2)}) copy-start(f32[8,1,256]{2,1,0:T(1,128)S(1)} %convert_element_type.237) | copy-start | bytes 24580
  37.6 136.9 %copy-start.27 = (f32[512,32]{0,1:T(8,128)}, f32[512,32]{0,1:T(8,128)S(1)}, u32[]{:S(2)}) copy-start(f32[512,32]{0,1:T(8,128)S(1)} %get-tuple-element.317) | copy-start | bytes 196612
  75.8 100.9 %all-to-all-start.1 = ((bf16[512,4,256]{0,2,1:T(8,128)(2,1)}), bf16[512,4,256]{0,2,1:T(8,128)(2,1)S(1)}, u32[]{:S(2)}, u32[]{:S(2)}) async-start(bf16[512,4,256]{0,2,1:T(8,128)(2,1)} %bitcast.380), calls=%async_computation.1 | async-start | bytes 2097152 | tf_op jit(solution)/shard_map/all_to_all | solution.py:228
  176.7 34.9 %all-to-all-start = ((bf16[512,4,512]{0,2,1:T(8,128)(2,1)}), bf16[512,4,512]{0,2,1:T(8,128)(2,1)}, u32[]{:S(2)}, u32[]{:S(2)}) async-start(bf16[512,4,512]{0,2,1:T(8,128)(2,1)} %bitcast.19), calls=%async_computation | async-start | bytes 4194304 | tf_op jit(solution)/shard_map/all_to_all | solution.py:227
  424.7 40.9 %copy-start.8 = (bf16[2048,2,64]{0,2,1:T(8,128)(2,1)}, bf16[2048,2,64]{0,2,1:T(8,128)(2,1)S(1)}, u32[]{:S(2)}) copy-start(bf16[2048,2,64]{0,2,1:T(8,128)(2,1)S(1)} %get-tuple-element.564) | copy-start | bytes 1572868
  424.7 40.9 %copy-start.25 = (s32[2048]{0:T(1024)}, s32[2048]{0:T(1024)S(1)}, u32[]{:S(2)}) copy-start(s32[2048]{0:T(1024)S(1)} %get-tuple-element.592) | copy-start | bytes 24580
  424.7 40.9 %copy-start.33 = (s32[2048]{0:T(1024)}, s32[2048]{0:T(1024)S(1)}, u32[]{:S(2)}) copy-start(s32[2048]{0:T(1024)S(1)} %get-tuple-element.601) | copy-start | bytes 24580
  424.7 28.9 all-to-all-start.2
  468.0 57.8 %copy-start.19 = (bf16[512,2048]{1,0:T(8,128)(2,1)}, bf16[512,2048]{1,0:T(8,128)(2,1)S(1)}, u32[]{:S(2)}) copy-start(bf16[512,2048]{1,0:T(8,128)(2,1)S(1)} %multiply_convert_fusion.3) | copy-start | bytes 6291460
  552.5 551.9 %copy-start.12 = (bf16[1,512,2048]{2,1,0:T(8,128)(2,1)S(1)}, bf16[1,512,2048]{2,1,0:T(8,128)(2,1)}, u32[]{:S(2)}) copy-start(bf16[1,512,2048]{2,1,0:T(8,128)(2,1)} %param.18) | copy-start | bytes 6291460
  552.5 551.9 %copy-start.41 = (f32[1,512]{1,0:T(1,128)S(1)}, f32[1,512]{1,0:T(1,128)}, u32[]{:S(2)}) copy-start(f32[1,512]{1,0:T(1,128)} %copy-done.40) | copy-start | bytes 6148
  1235.5 30.1 all-to-all-start.3
  1693.1 17.0 all-to-all-start.5
  1710.1 27.9 all-to-all-start.4
  1713.7 345.1 %reduce-scatter.5.cloned.1.call-start = ((), (), s32[]{:S(2)}) async-start(), calls=%async_computation.15 | async-start | bytes 23592960 | tf_op jit(solution)/shard_map/reduce_scatter | solution.py:309
  1794.6 1218.9 %reduce-scatter.7.cloned.1.call-start = ((), (), s32[]{:S(2)}) async-start(), calls=%async_computation.16 | async-start | bytes 113246208
  2058.4 1241.9 %all-reduce.5.cloned.1.call-start = ((), (), s32[]{:S(2)}) async-start(), calls=%async_computation.17 | async-start | bytes 30408704 | tf_op jit(solution)/shard_map/psum | solution.py:326
  (60 other events, 720.1 us)
Sparse Core Ops, SparseCore 0:
  9.6 31.8 all-gather.13
  43.1 28.5 all-gather.15
  73.3 81.5 all-gather.11
  156.4 81.0 all-gather.17
  238.9 286.8 all-gather.21
  527.3 286.7 all-gather.19
  815.7 288.6 all-gather.23
  1794.7 207.8 reduce-scatter.4
  2058.5 954.9 reduce-scatter.6
  3017.6 282.6 all-reduce.4
where the time goes:
time: 3370 us; the launch traced here: 3360 us
  waiting for transfers between devices  1930 us (57%)
  matrix products  706 us (21%)
  other arithmetic  323 us (10%)
  local copies, waits for them, and re-layouts  260 us (8%)
  blocking collectives  97.4 us (3%)
    unnamed x11, waiting for transfers between devices  959 us
    all_gather x1, waiting for transfers between devices, body(): lax.all_gather(down_weight, 'fsdp', axis=1, tiled=True)  262 us
    all_gather x1, waiting for transfers between devices, body(): lax.all_gather(gate_weight, 'fsdp', axis=0, tiled=True)  262 us
    psum x1, waiting for transfers between devices, body(): lax.psum(attn_part, 'seq').astype(jnp.float32)  220 us
    concatenate x2, local copies, waits for them, and re-layouts, block_term(): full_term = jnp.concatenate(pieces, axis=3)  146 us
    dot_general x8, matrix products, block_scores(): jnp.einsum('qkgd,skd->kgqs', query_block, key_three, preferred_element_ty...  117 us
    convert_element_type x4, other arithmetic, step(): grad_scores = (probs * (grad_probs - inner)).astype(jnp.bfloat16)  111 us
    dot_general x4, matrix products, step(): jnp.einsum('qkgd,skd->kgqs', grad_block, value_three, preferred_element_t...  96.8 us
  transfers between devices with their start and end apart: 16, of which 12 were waited for; matrix products, arithmetic and copies ran while one was open for 18% of the time, Pallas kernels for 0%

commit v1 on v0

v1 whole, which is shorter than its diff:
```python
import functools

import jax
import jax.numpy as jnp
from jax import lax
from jax.experimental import pallas as pl
from jax.experimental.pallas import tpu as pltpu
from jax.sharding import PartitionSpec as P

D = 2048
HEADS = 32
KV_HEADS = 8
HEAD_DIM = 64
GROUP = HEADS // KV_HEADS
FF = 8192
EPSILON = 1e-05
ROPE_BASE = 500000.0
NEGATIVE = -1e30
SCALE = HEAD_DIM**-0.5
BF = jnp.bfloat16
F32 = jnp.float32
LANES = 128
VMEM_LIMIT = 60 * 1024 * 1024
NT = (((1,), (1,)), ((), ()))
NN = (((1,), (0,)), ((), ()))
TN = (((0,), (0,)), ((), ()))


def dot(left, right, dims=NN):
    return lax.dot_general(left, right, dims, preferred_element_type=F32)


def params(grid_rank):
    return pltpu.CompilerParams(
        dimension_semantics=("arbitrary",) * grid_rank, vmem_limit_bytes=VMEM_LIMIT
    )


def swap(values, bit):
    count = lax.axis_size("seq")
    return lax.ppermute(values, "seq", [(i, i ^ bit) for i in range(count)])


def bit_orders():
    bits = [1 << b for b in range(lax.axis_size("seq").bit_length() - 1)]
    return bits, bits[::-1]


def gather_stream(block, order):
    held, owners = block[None], [0]
    for bit in order:
        held = jnp.concatenate([held, swap(held, bit)], axis=0)
        owners = owners + [k ^ bit for k in owners]
    return [held[owners.index(k)] for k in range(len(owners))]


def gather_seq(block):
    half = block.shape[-1] // 2
    low_order, high_order = bit_orders()
    low = gather_stream(block[..., :half], low_order)
    high = gather_stream(block[..., half:], high_order)
    return [jnp.concatenate(pair, axis=-1) for pair in zip(low, high)]


def reduce_stream(blocks, order):
    held = {k: b for k, b in enumerate(blocks)}
    for bit in order:
        away = sorted(k for k in held if k & bit)
        sent = swap(jnp.stack([held[k].astype(BF) for k in away]), bit)
        held = {
            k: held[k].astype(F32) + sent[away.index(k ^ bit)].astype(F32)
            for k in held
            if not k & bit
        }
    return held[0]


def reduce_seq(blocks):
    half = blocks[0].shape[-1] // 2
    low_order, high_order = bit_orders()
    low = reduce_stream([b[..., :half] for b in blocks], low_order)
    high = reduce_stream([b[..., half:] for b in blocks], high_order)
    return jnp.concatenate([low, high], axis=-1)


def exchange_seq(blocks):
    return [b if k == 0 else swap(b, k) for k, b in enumerate(blocks)]


def gather_fsdp(shard):
    return lax.all_gather(shard, "fsdp", axis=0, tiled=True)


def scatter_fsdp(values):
    return lax.psum_scatter(values, "fsdp", scatter_dimension=0, tiled=True)


def turn(values, cosine, sine):
    lane = lax.broadcasted_iota(jnp.int32, values.shape, 1)
    half = HEAD_DIM // 2
    ahead = pltpu.roll(values, LANES - half, 1)
    behind = pltpu.roll(values, half, 1)
    return values * cosine + jnp.where(lane % HEAD_DIM < half, ahead, behind) * sine


def project_kernel(kv_local, x_ref, gain_ref, w_ref, cos_ref, sin_ref, normed_ref, q_ref, k_ref, v_ref):
    x = x_ref[...].astype(F32)
    inv = lax.rsqrt(jnp.mean(x * x, axis=-1, keepdims=True) + EPSILON)
    normed = (x * inv * gain_ref[...]).astype(BF)
    normed_ref[...] = normed
    q_width = kv_local * GROUP * HEAD_DIM
    kv_width = kv_local * HEAD_DIM
    lin = dot(normed, w_ref[:, : q_width + 2 * kv_width])
    cosine, sine = cos_ref[...], sin_ref[...]
    for start in range(0, q_width, LANES):
        part = turn(lin[:, start : start + LANES], cosine, sine) * SCALE
        q_ref[:, start : start + LANES] = part.astype(BF)
    for start in range(0, kv_width, LANES):
        part = turn(lin[:, q_width + start : q_width + start + LANES], cosine, sine)
        for at in range(0, min(LANES, kv_width - start), HEAD_DIM):
            k_ref[(start + at) // HEAD_DIM] = part[:, at : at + HEAD_DIM].astype(BF)
    for head in range(kv_local):
        start = q_width + kv_width + head * HEAD_DIM
        v_ref[head] = lin[:, start : start + HEAD_DIM].astype(BF)


def project(x, gain_row, weight, cosine, sine, kv_local):
    rows = x.shape[0]
    block = 256
    q_width = kv_local * GROUP * HEAD_DIM
    by_row = lambda i: (i, 0)
    whole = lambda i: (0, 0)
    by_head = lambda i: (0, i, 0)
    return pl.pallas_call(
        functools.partial(project_kernel, kv_local),
        grid=(rows // block,),
        in_specs=[
            pl.BlockSpec((block, D), by_row),
            pl.BlockSpec((1, D), whole),
            pl.BlockSpec(weight.shape, whole),
            pl.BlockSpec((block, LANES), by_row),
            pl.BlockSpec((block, LANES), by_row),
        ],
        out_specs=[
            pl.BlockSpec((block, D), by_row),
            pl.BlockSpec((block, q_width), by_row),
            pl.BlockSpec((kv_local, block, HEAD_DIM), by_head),
            pl.BlockSpec((kv_local, block, HEAD_DIM), by_head),
        ],
        out_shape=[
            jax.ShapeDtypeStruct((rows, D), BF),
            jax.ShapeDtypeStruct((rows, q_width), BF),
            jax.ShapeDtypeStruct((kv_local, rows, HEAD_DIM), BF),
            jax.ShapeDtypeStruct((kv_local, rows, HEAD_DIM), BF),
        ],
        compiler_params=params(1),
        cost_estimate=pl.CostEstimate(
            flops=2 * rows * D * weight.shape[1], bytes_accessed=rows * D * 6, transcendentals=0
        ),
        name="project",
    )(x, gain_row, weight, cosine, sine)


def pair_bias(rows, query_index, key_index, query_row, key_col):
    key_pos = key_index * rows + lax.broadcasted_iota(jnp.int32, (rows, rows), 0)
    query_pos = query_index * rows + lax.broadcasted_iota(jnp.int32, (rows, rows), 1)
    allowed = ((key_col == query_row) & (key_pos <= query_pos)) | (key_pos == query_pos)
    return jnp.where(allowed, 0.0, NEGATIVE)


def attend_kernel(rows, me_ref, q_ref, k_ref, v_ref, query_row_ref, key_col_ref, out_ref, total_ref, v_t, peak, total, acc):
    index = pl.program_id(1)
    me = me_ref[0]

    @pl.when(index == 0)
    def _():
        v_t[...] = v_ref[0].astype(F32).T.astype(BF)

    peak[...] = jnp.full(peak.shape, NEGATIVE, F32)
    total[...] = jnp.zeros(total.shape, F32)
    acc[...] = jnp.zeros(acc.shape, F32)

    def step(j, _):
        at = pl.multiple_of((j ^ me) * rows, rows)
        keys = k_ref[0, pl.ds(at, rows), :]
        values_t = v_t[:, pl.ds(at, rows)]
        bias = pair_bias(rows, index, j, query_row_ref[...], key_col_ref[pl.ds(at, rows), :])
        for head in range(GROUP):
            query = q_ref[:, head * HEAD_DIM : (head + 1) * HEAD_DIM]
            scores = dot(keys, query, NT) + bias
            old = peak[head : head + 1, :]
            new = jnp.maximum(old, jnp.max(scores, axis=0, keepdims=True))
            expo = jnp.exp(scores - new)
            fade = jnp.exp(old - new)
            peak[head : head + 1, :] = new
            total[head : head + 1, :] = total[head : head + 1, :] * fade + jnp.sum(expo, axis=0, keepdims=True)
            acc[head] = acc[head] * fade + dot(values_t, expo.astype(BF))
        return 0

    lax.fori_loop(0, index + 1, step, 0)
    for head in range(GROUP):
        out = acc[head] / total[head : head + 1, :]
        out_ref[:, head * HEAD_DIM : (head + 1) * HEAD_DIM] = out.T.astype(BF)
    total_ref[0] = peak[...] + jnp.log(total[...])


def attend(me, q, k, v, query_row, key_col, rows):
    kv_local, length = k.shape[0], k.shape[1]
    count = length // rows
    width = GROUP * HEAD_DIM
    return pl.pallas_call(
        functools.partial(attend_kernel, rows),
        grid_spec=pltpu.PrefetchScalarGridSpec(
            num_scalar_prefetch=1,
            grid=(kv_local, count),
            in_specs=[
                pl.BlockSpec((rows, width), lambda g, i, me: (i ^ me[0], g)),
                pl.BlockSpec((1, length, HEAD_DIM), lambda g, i, me: (g, 0, 0)),
                pl.BlockSpec((1, length, HEAD_DIM), lambda g, i, me: (g, 0, 0)),
                pl.BlockSpec((1, rows), lambda g, i, me: (0, i ^ me[0])),
                pl.BlockSpec((length, 1), lambda g, i, me: (0, 0)),
            ],
            out_specs=[
                pl.BlockSpec((rows, width), lambda g, i, me: (i ^ me[0], g)),
                pl.BlockSpec((1, GROUP, rows), lambda g, i, me: (g, 0, i ^ me[0])),
            ],
            scratch_shapes=[
                pltpu.VMEM((HEAD_DIM, length), BF),
                pltpu.VMEM((GROUP, rows), F32),
                pltpu.VMEM((GROUP, rows), F32),
                pltpu.VMEM((GROUP, HEAD_DIM, rows), F32),
            ],
        ),
        out_shape=[
            jax.ShapeDtypeStruct((length, kv_local * width), BF),
            jax.ShapeDtypeStruct((kv_local, GROUP, length), F32),
        ],
        compiler_params=params(2),
        cost_estimate=pl.CostEstimate(
            flops=kv_local * GROUP * length * length * HEAD_DIM * 8, bytes_accessed=1 << 24, transcendentals=0
        ),
        name="attend",
    )(me, q, k, v, query_row, key_col)


def attend_back_kernel(
    rows, count, me_ref, q_ref, k_ref, v_ref, out_ref, grad_ref, total_ref, query_row_ref, key_col_ref,
    cos_ref, sin_ref, cos_t_ref, sin_t_ref, dq_ref, dk_ref, dv_ref, k_t, inner, dq_t, dk_acc, dv_acc,
):
    me = me_ref[0]
    half = HEAD_DIM // 2
    k_t[...] = k_ref[0].astype(F32).T.astype(BF)
    dq_t[...] = jnp.zeros(dq_t.shape, F32)

    def prepare(i, _):
        here = pl.ds(pl.multiple_of(i * rows, rows), rows)
        for head in range(GROUP):
            cols = slice(head * HEAD_DIM, (head + 1) * HEAD_DIM)
            both = out_ref[here, cols].astype(F32) * grad_ref[here, cols].astype(F32)
            inner[head : head + 1, here] = jnp.sum(both.T, axis=0, keepdims=True)
        return 0

    lax.fori_loop(0, count, prepare, 0)

    def key_step(j, _):
        key_at = pl.ds(pl.multiple_of((j ^ me) * rows, rows), rows)
        keys, values = k_ref[0, key_at, :], v_ref[0, key_at, :]
        keys_t = k_t[:, key_at]
        key_col = key_col_ref[key_at, :]
        dk_acc[...] = jnp.zeros(dk_acc.shape, F32)
        dv_acc[...] = jnp.zeros(dv_acc.shape, F32)

        def query_step(i, _):
            at = pl.ds(pl.multiple_of((i ^ me) * rows, rows), rows)
            bias = pair_bias(rows, i, j, query_row_ref[:, at], key_col)
            for head in range(GROUP):
                cols = slice(head * HEAD_DIM, (head + 1) * HEAD_DIM)
                query, grad = q_ref[at, cols], grad_ref[at, cols]
                probs = jnp.exp(dot(keys, query, NT) + bias - total_ref[0, head : head + 1, at])
                dv_acc[...] += dot(probs.astype(BF), grad)
                grad_probs = dot(values, grad, NT)
                grad_scores = (probs * (grad_probs - inner[head : head + 1, at])).astype(BF)
                dk_acc[...] += dot(grad_scores, query)
                dq_t[head, :, at] += dot(keys_t, grad_scores)
            return 0

        lax.fori_loop(j, count, query_step, 0)
        dk = dk_acc[...]
        low, high = dk[:, :half], dk[:, half:]
        cosine, sine = cos_ref[key_at, :half], sin_ref[key_at, half:HEAD_DIM]
        dk_ref[0, key_at, :] = jnp.concatenate(
            [low * cosine + high * sine, high * cosine - low * sine], axis=1
        ).astype(BF)
        dv_ref[0, key_at, :] = dv_acc[...].astype(BF)
        return 0

    lax.fori_loop(0, count, key_step, 0)

    def finish(i, _):
        here = pl.ds(pl.multiple_of(i * rows, rows), rows)
        cosine, sine = cos_t_ref[:, here], sin_t_ref[:, here]
        for head in range(GROUP):
            low, high = dq_t[head, :half, here], dq_t[head, half:, here]
            turned = jnp.concatenate([low * cosine + high * sine, high * cosine - low * sine], axis=0) * SCALE
            dq_ref[here, head * HEAD_DIM : (head + 1) * HEAD_DIM] = turned.T.astype(BF)
        return 0

    lax.fori_loop(0, count, finish, 0)


def attend_back(me, q, k, v, out, grad, totals, query_row, key_col, cosine, sine, cosine_t, sine_t, rows):
    kv_local, length = k.shape[0], k.shape[1]
    width = GROUP * HEAD_DIM
    by_group = pl.BlockSpec((length, width), lambda g, me: (0, g))
    by_head = pl.BlockSpec((1, length, HEAD_DIM), lambda g, me: (g, 0, 0))
    whole = lambda shape: pl.BlockSpec(shape, lambda g, me: (0, 0))
    return pl.pallas_call(
        functools.partial(attend_back_kernel, rows, length // rows),
        grid_spec=pltpu.PrefetchScalarGridSpec(
            num_scalar_prefetch=1,
            grid=(kv_local,),
            in_specs=[
                by_group,
                by_head,
                by_head,
                by_group,
                by_group,
                pl.BlockSpec((1, GROUP, length), lambda g, me: (g, 0, 0)),
                whole((1, length)),
                whole((length, 1)),
                whole((length, LANES)),
                whole((length, LANES)),
                whole((HEAD_DIM // 2, length)),
                whole((HEAD_DIM // 2, length)),
            ],
            out_specs=[by_group, by_head, by_head],
            scratch_shapes=[
                pltpu.VMEM((HEAD_DIM, length), BF),
                pltpu.VMEM((GROUP, length), F32),
                pltpu.VMEM((GROUP, HEAD_DIM, length), F32),
                pltpu.VMEM((rows, HEAD_DIM), F32),
                pltpu.VMEM((rows, HEAD_DIM), F32),
            ],
        ),
        out_shape=[
            jax.ShapeDtypeStruct((length, kv_local * width), BF),
            jax.ShapeDtypeStruct((kv_local, length, HEAD_DIM), BF),
            jax.ShapeDtypeStruct((kv_local, length, HEAD_DIM), BF),
        ],
        compiler_params=params(1),
        cost_estimate=pl.CostEstimate(
            flops=kv_local * GROUP * length * length * HEAD_DIM * 20, bytes_accessed=1 << 24, transcendentals=0
        ),
        name="attend_back",
    )(me, q, k, v, out, grad, totals, query_row, key_col, cosine, sine, cosine_t, sine_t)


def norm_scale(values):
    return lax.rsqrt(jnp.mean(values * values, axis=-1, keepdims=True) + EPSILON)


def norm_back(grad_normed, values, inv_rms, gain_row):
    unit_rows = values * inv_rms
    scaled = grad_normed * gain_row
    return inv_rms * (scaled - unit_rows * jnp.mean(scaled * unit_rows, axis=-1, keepdims=True))


def blocks_of(values, count):
    rows = values.shape[0] // count
    return [values[k * rows : (k + 1) * rows] for k in range(count)]


def whole_columns(blocks, me):
    stacked = jnp.stack(blocks)
    ordered = [
        lax.dynamic_index_in_dim(stacked, p ^ me, 0, keepdims=False) for p in range(len(blocks))
    ]
    return jnp.concatenate(ordered, axis=1).astype(F32)


def body(
    inputs, cotangent, segments, valid_mask, query_weight, key_weight, value_weight, out_weight,
    gate_weight, up_weight, down_weight, attn_gain, mlp_gain,
):
    count = lax.axis_size("seq")
    me = lax.axis_index("seq")
    me_row = me.reshape(1).astype(jnp.int32)
    rows = inputs.shape[1]
    length = rows * count
    kv_local = KV_HEADS // count
    q_width = kv_local * GROUP * HEAD_DIM
    kv_width = kv_local * HEAD_DIM
    ff_local = FF // count
    shard_rows = gate_weight.shape[0]

    def mine(weight, width, axis=1):
        return lax.dynamic_slice_in_dim(weight, me * width, width, axis)

    gains = jnp.pad(jnp.stack([attn_gain, mlp_gain], axis=1), ((0, 0), (0, LANES - 2)))
    qkv_shard = jnp.concatenate(
        [mine(query_weight, q_width), mine(key_weight, kv_width), mine(value_weight, kv_width), gains], axis=1
    )
    qkv_full = gather_fsdp(qkv_shard)
    out_slice = gather_fsdp(mine(out_weight, q_width, 0).T)
    down_t = gather_fsdp(mine(down_weight, ff_local, 0).T)
    gate_up = gather_fsdp(jnp.concatenate([mine(gate_weight, ff_local), mine(up_weight, ff_local)], axis=1))
    gain_one = qkv_full[:, q_width + 2 * kv_width].astype(F32).reshape(1, D)
    gain_two = qkv_full[:, q_width + 2 * kv_width + 1].astype(F32).reshape(1, D)
    qkv_weight = qkv_full[:, : q_width + 2 * kv_width]

    marks = jnp.stack([segments[0], valid_mask[0]])
    marks_all = jnp.stack(gather_stream(marks, bit_orders()[0]))
    segment_all = marks_all[:, 0].reshape(length)
    valid_all = marks_all[:, 1].reshape(length)
    x_all = jnp.concatenate(gather_seq(inputs[0]), axis=0)
    valid_col = valid_mask[0].astype(F32)[:, None]
    grad_final = cotangent[0].astype(F32) * valid_col
    grad_mlp = jnp.concatenate(gather_seq(grad_final.astype(BF)), axis=0)

    position = (
        (jnp.arange(count, dtype=jnp.int32) ^ me)[:, None] * rows + jnp.arange(rows, dtype=jnp.int32)[None, :]
    ).reshape(length)
    same = (segment_all[:, None] == segment_all[None, :]) & (position[None, :] < position[:, None])
    places = jnp.sum(same.astype(jnp.int32), axis=1).astype(F32)
    half = HEAD_DIM // 2
    frequency = ROPE_BASE ** (-2.0 * jnp.arange(half, dtype=F32) / HEAD_DIM)
    angles_t = frequency[:, None] * places[None, :]
    cosine_t, sine_t = jnp.cos(angles_t), jnp.sin(angles_t)
    cosine = jnp.tile(cosine_t.T, (1, LANES // half))
    sign = jnp.tile(jnp.repeat(jnp.array([-1.0, 1.0], F32), half), LANES // HEAD_DIM)
    sine = jnp.tile(sine_t.T, (1, LANES // half)) * sign[None, :]
    query_row = jnp.where(valid_all == 1, segment_all, -1).reshape(1, length)
    key_col = segment_all.reshape(length, 1)

    normed_one, q, k, v = project(x_all, gain_one, qkv_full, cosine, sine, kv_local)
    heads_own, totals = attend(me_row, q, k, v, query_row, key_col, rows)

    heads_blocks = gather_seq(heads_own)
    heads_all = jnp.concatenate(
        [
            jnp.concatenate([blocks_of(heads_blocks[k], count)[i ^ k] for i in range(count)], axis=0)
            for k in range(count)
        ],
        axis=1,
    )
    out_blocks = gather_seq(out_slice)
    out_t = jnp.concatenate(out_blocks, axis=1)
    attn_all = dot(heads_all, out_t, NT)
    middle_all = x_all.astype(F32) + attn_all
    normed_two = (middle_all * norm_scale(middle_all) * gain_two).astype(BF)
    tokens = inputs[0].astype(F32)
    attn_branch = attn_all[:rows]
    middle = tokens + attn_branch
    inv_two = norm_scale(middle)

    gate_full, up_full = gate_up[:, :ff_local], gate_up[:, ff_local:]
    gate_lin = dot(normed_two, gate_full)
    up_lin = dot(normed_two, up_full)
    sigmoid_gate = jax.nn.sigmoid(gate_lin)
    silu_gate = gate_lin * sigmoid_gate
    activated = (silu_gate * up_lin).astype(BF)
    grad_act = dot(grad_mlp, down_t)
    grad_gate = (grad_act * up_lin * sigmoid_gate * (1.0 + gate_lin * (1.0 - sigmoid_gate))).astype(BF)
    grad_up = (grad_act * silu_gate).astype(BF)
    mlp_part = dot(activated, down_t, NT).astype(BF)
    grad_both = jnp.concatenate([grad_gate, grad_up], axis=1)
    grad_two_part = dot(grad_both, gate_up, NT).astype(BF)
    grad_normed_two = reduce_seq(blocks_of(grad_two_part, count))
    mlp_branch = reduce_seq(blocks_of(mlp_part, count))
    final = middle + mlp_branch
    outputs = final.astype(BF)[None]

    gate_up_grad = scatter_fsdp(dot(normed_two, grad_both, TN).astype(BF))
    down_grad_t = scatter_fsdp(dot(grad_mlp, activated, TN).astype(BF))

    grad_middle = grad_final + norm_back(grad_normed_two, middle, inv_two, gain_two)
    grad_attn = grad_middle.astype(BF)
    grad_heads = jnp.concatenate(
        exchange_seq([dot(grad_attn, b).astype(BF) for b in out_blocks]), axis=0
    )
    grad_attn_all = jnp.concatenate(gather_seq(grad_attn), axis=0)
    out_grad_t = scatter_fsdp(dot(grad_attn_all, heads_own, TN).astype(BF))

    dq, dk, dv = attend_back(
        me_row, q, k, v, heads_own, grad_heads, totals, query_row, key_col, cosine, sine, cosine_t, sine_t, rows
    )
    dqkv = jnp.concatenate([dq] + [dk[g] for g in range(kv_local)] + [dv[g] for g in range(kv_local)], axis=1)
    qkv_grad = scatter_fsdp(dot(normed_one, dqkv, TN).astype(BF))
    weight_blocks = gather_seq(qkv_weight)
    parts = exchange_seq(blocks_of(dqkv, count))
    grad_normed_one = dot(jnp.concatenate(parts, axis=1), jnp.concatenate(weight_blocks, axis=1), NT)
    inv_one = norm_scale(tokens)
    input_grad = (grad_middle + norm_back(grad_normed_one, tokens, inv_one, gain_one)).astype(BF)[None]

    gate_up_blocks = gather_seq(gate_up_grad)
    gate_grad = whole_columns([b[:, :ff_local] for b in gate_up_blocks], me)
    up_grad = whole_columns([b[:, ff_local:] for b in gate_up_blocks], me)
    down_grad = whole_columns(gather_seq(down_grad_t), me).T
    out_grad = whole_columns(gather_seq(out_grad_t), me).T
    qkv_blocks = gather_seq(qkv_grad)
    query_grad = whole_columns([b[:, :q_width] for b in qkv_blocks], me)
    key_grad = whole_columns([b[:, q_width : q_width + kv_width] for b in qkv_blocks], me)
    value_grad = whole_columns([b[:, q_width + kv_width :] for b in qkv_blocks], me)

    def rows_dot(weight, grad):
        return jnp.sum(weight.astype(F32) * grad, axis=1)

    attn_gain_grad = (
        rows_dot(query_weight, query_grad) + rows_dot(key_weight, key_grad) + rows_dot(value_weight, value_grad)
    ) / attn_gain.astype(F32)
    mlp_gain_grad = (rows_dot(gate_weight, gate_grad) + rows_dot(up_weight, up_grad)) / mlp_gain.astype(F32)

    squares = [jnp.sum(valid_col * part * part) for part in (tokens, middle, final, attn_branch, mlp_branch)]
    stats = jnp.stack([jnp.sum(valid_col)] + squares)
    stats = jnp.broadcast_to(jnp.pad(stats, (0, LANES - 6))[None, :], (8, LANES))
    for bit in bit_orders()[0]:
        stats = stats + swap(stats, bit)
    rms_stats = jnp.sqrt(stats[:1, 1:6] / (stats[:1, :1] * D))
    return (
        outputs, input_grad, query_grad, key_grad, value_grad, out_grad, gate_grad, up_grad, down_grad,
        attn_gain_grad, mlp_gain_grad, rms_stats,
    )


def solution(mesh):
    rows_in = P("fsdp", None)
    columns_in = P(None, "fsdp")
    placed = (
        P("fsdp", "seq", None), P("fsdp", "seq", None), P("fsdp", "seq"), P("fsdp", "seq"),
        rows_in, rows_in, rows_in, columns_in, rows_in, rows_in, columns_in, P("fsdp"), P("fsdp"),
    )
    return jax.shard_map(
        body,
        mesh=mesh,
        in_specs=placed,
        out_specs=(
            P("fsdp", "seq", None), P("fsdp", "seq", None), rows_in, rows_in, rows_in, columns_in,
            rows_in, rows_in, columns_in, P("fsdp"), P("fsdp"), P("fsdp", None),
        ),
        check_vma=False,
    )
```

time: 3370 us -> 1460 us (0.43)
  waiting for transfers between devices: 1930 us -> 540 us
  matrix products: 706 us -> 367 us
  Pallas kernels: 0 us -> 150 us
  other arithmetic: 323 us -> 185 us
  local copies, waits for them, and re-layouts: 260 us -> 131 us
  blocking collectives: 97.4 us -> 0 us
    unnamed x11 -> x8, waiting for transfers between devices: 959 us -> 0.13 us
    all_gather x7 -> x4, waiting for transfers between devices: 684 us -> 0.03 us  [gather_fsdp(): return lax.all_gather(shard, 'fsdp', axis=0, tiled=True)]
    ppermute x0 -> x58, waiting for transfers between devices: none -> 540 us  [swap(): return lax.ppermute(values, 'seq', [(i, i ^ bit) for i in range(count)])]
    dot_general x46 -> x15, matrix products: 706 us -> 367 us  [dot(): return lax.dot_general(left, right, dims, preferred_element_type=F32)]
    psum x1 -> x0, waiting for transfers between devices: 220 us -> none  [body(): lax.psum(attn_part, 'seq').astype(jnp.float32)]
    pallas_call x0 -> x3, Pallas kernels: none -> 150 us  [the longest x1 75.4 us: attend_back(): pl.pallas_call(functools.partial(attend_back_kernel, rows, length // rows...]
    concatenate x2 -> x3, local copies, waits for them, and re-layouts: 146 us -> 10.8 us  [the longest x1 6.47 us: body(): jnp.concatenate([dq] + [dk[g] for g in range(kv_local)] + [dv[g] for g in...]
    convert_element_type x15 -> x6, other arithmetic: 131 us -> 62.2 us  [the longest x1 54.4 us: body(): normed_two = (middle_all * norm_scale(middle_all) * gain_two).astype(BF)]
  transfers between devices with their start and end apart: 16 -> 66, of which waited for: 12 -> 31; matrix products, arithmetic and copies ran while one was open for 18% -> 37% of each run, Pallas kernels for 0% -> 10%
where the time goes in v1:
time: 1460 us; the launch traced here: 1450 us
  waiting for transfers between devices  540 us (37%)
  matrix products  367 us (25%)
  other arithmetic  185 us (13%)
  Pallas kernels  150 us (10%)
  local copies, waits for them, and re-layouts  131 us (9%)
  starting transfers between devices  56.7 us (4%)
  between operations  16.3 us (1%)
    ppermute x58, waiting for transfers between devices, swap(): return lax.ppermute(values, 'seq', [(i, i ^ bit) for i in range(count)])  540 us
    dot_general x15, matrix products, dot(): return lax.dot_general(left, right, dims, preferred_element_type=F32)  367 us
    pallas_call x1, Pallas kernels, attend_back(): pl.pallas_call(functools.partial(attend_back_kernel, rows, length // rows...  75.4 us
    pallas_call x1, Pallas kernels, attend(): pl.pallas_call(functools.partial(attend_kernel, rows), grid_spec=pltpu.Pr...  58.4 us
    ppermute x58, starting transfers between devices, swap(): return lax.ppermute(values, 'seq', [(i, i ^ bit) for i in range(count)])  56.4 us
    convert_element_type x1, other arithmetic, body(): normed_two = (middle_all * norm_scale(middle_all) * gain_two).astype(BF)  54.4 us
    unnamed x175, local copies, waits for them, and re-layouts  45.7 us
  transfers between devices with their start and end apart: 66, of which 31 were waited for; matrix products, arithmetic and copies ran while one was open for 37% of the time, Pallas kernels for 10%

profile of v1, /device:TPU:0, one launch (start us, length us, event | category | flops | bytes accessed | tf_op | source)
XLA Modules:
  0.0 1445.9 jit_solution(15513280752068980840)
XLA Ops:
  47.0 19.3 %collective-permute-done.5 = s32[2,2,512]{2,1,0:T(2,128)S(1)} collective-permute-done((s32[2,2,512]{2,1,0:T(2,128)S(1)}, s32[2,2,512]{2,1,0:T(2,128)S(1)}, u32[]{:S(2)}, u32[]{:S(2)}) %collective-permute-start.5) | collective-permute-done | bytes 8224 | tf_op jit(solution)/shard_map/ppermute | solution.py:41
  99.0 18.9 %collective-permute-done.2 = bf16[2,512,1024]{2,1,0:T(8,128)(2,1)} collective-permute-done((bf16[2,512,1024]{2,1,0:T(8,128)(2,1)}, bf16[2,512,1024]{2,1,0:T(8,128)(2,1)}, u32[]{:S(2)}, u32[]{:S(2)}) %collective-permute-start.2) | collective-permute-done | bytes 2097184 | tf_op jit(solution)/shard_map/ppermute | solution.py:41
  130.5 26.9 %maximum_maximum_fusion.x_ref = bf16[2048,2048]{1,0:T(8,128)(2,1)} fusion(bf16[512,1024]{1,0:T(8,128)(2,1)S(1)} %copy-done.7, bf16[512,1024]{1,0:T(8,128)(2,1)S(1)} %copy-done.11, bf16[512,1024]{1,0:T(8,128)(2,1)S(1)} %bitcast.397, bf16[512,1024]{1,0:T(8,128)(2,1)S(1)} %copy-done.9, bf16[512,1024]{1,0:T(8,128)(2,1)S(1)} %copy-done.5, ...), kind=kLoop, calls=%fused_computation.42 | loop fusion | flops 58720256 | bytes 16777216 | tf_op jit(solution)/shard_map/concatenate | solution.py:415
  212.9 58.4 %attend.1 = (bf16[2048,512]{1,0:T(8,128)(2,1)}, f32[2,4,2048]{2,1,0:T(4,128)}) custom-call(s32[1]{0:T(128)} %bitcast.1.me_ref, bf16[2048,512]{1,0:T(8,128)(2,1)} %get-tuple-element.21.q_ref, bf16[2,2048,64]{2,1,0:T(8,128)(2,1)} %get-tuple-element.22.k_ref, bf16[2,2048,64]{2,1,0:T(8,128)(2,1)} %get-tuple-element.23.v_ref, s32[1,2048]{1,0:T(1,128)} %bitcast.425, ...), custom_call_target="tpu_custom_call" | custom-call | flops 17179869184 | bytes 16777216 | tf_op jit(solution)/shard_map/attend/pallas_call | solution.py:211
  277.1 18.6 %collective-permute-done.6 = bf16[1,2048,256]{2,1,0:T(8,128)(2,1)S(1)} collective-permute-done((bf16[1,2048,256]{2,1,0:T(8,128)(2,1)S(1)}, bf16[1,2048,256]{2,1,0:T(8,128)(2,1)S(1)}, u32[]{:S(2)}, u32[]{:S(2)}) %collective-permute-start.6) | collective-permute-done | bytes 1048608 | tf_op jit(solution)/shard_map/ppermute | solution.py:41
  302.3 40.0 %collective-permute-done.9 = bf16[2,2048,256]{2,1,0:T(8,128)(2,1)S(1)} collective-permute-done((bf16[2,2048,256]{2,1,0:T(8,128)(2,1)S(1)}, bf16[2,2048,256]{2,1,0:T(8,128)(2,1)S(1)}, u32[]{:S(2)}, u32[]{:S(2)}) %collective-permute-start.9) | collective-permute-done | bytes 2097184 | tf_op jit(solution)/shard_map/ppermute | solution.py:41
  347.8 87.4 %multiply_reduce_fusion = (f32[2048]{0:T(1024)S(1)}, f32[2048,2048]{1,0:T(8,128)}) fusion(bf16[2048,2048]{0,1:T(8,128)(2,1)} %copy-done.54, bf16[2048,256]{1,0:T(8,128)(2,1)} %copy-done.27, bf16[2048,256]{1,0:T(8,128)(2,1)} %copy-done.25, bf16[2048,256]{1,0:T(8,128)(2,1)S(1)} %bitcast.405, bf16[2048,256]{1,0:T(8,128)(2,1)} %copy-done.24, ...), kind=kOutput, calls=%fused_computation.13 | convolution fusion | flops 17406359552 | bytes 46145536 | tf_op jit(solution)/shard_map/dot_general | solution.py:30
  435.2 54.4 %multiply_convert_fusion.3 = bf16[2048,2048]{1,0:T(8,128)(2,1)} fusion(f32[2048,2048]{1,0:T(8,128)} %get-tuple-element.218, f32[2048]{0:T(1024)S(1)} %get-tuple-element.70, f32[2048]{0:T(1024)S(1)} %add_rsqrt_fusion, bf16[512,1024]{1,0:T(8,128)(2,1)S(1)} %copy-done.8, bf16[512,1024]{1,0:T(8,128)(2,1)S(1)} %copy-done.12, bf16[512,1024]{1,0:T(8,128)(2,1)S(1)} %bitcast.399, ...), kind=kLoop, calls=%fused_computation.12 | loop fusion | flops 75497472 | bytes 33570816 | tf_op jit(solution)/shard_map/convert_element_type | solution.py:450
  489.7 30.2 %fusion.144 = f32[2048,2048]{0,1:T(8,128)} fusion(bf16[2048,2048]{0,1:T(8,128)(2,1)} %all-gather.11.cloned.1.call-done, bf16[512,1024]{1,0:T(8,128)(2,1)} %get-tuple-element.140, bf16[512,1024]{1,0:T(8,128)(2,1)} %get-tuple-element.142, bf16[512,1024]{1,0:T(8,128)(2,1)} %bitcast.54, bf16[512,1024]{1,0:T(8,128)(2,1)} %get-tuple-element.141, ...), kind=kOutput, calls=%fused_computation.403 | convolution fusion | flops 17238589440 | bytes 33554432 | tf_op jit(solution)/shard_map/dot_general | solution.py:30
  519.9 24.8 %fusion.17 = f32[2048,2048]{0,1:T(8,128)} fusion(bf16[2048,2048]{1,0:T(8,128)(2,1)} %multiply_convert_fusion.3, bf16[2048,4096]{1,0:T(8,128)(2,1)} %all-gather.9.cloned.1.call-done), kind=kOutput, calls=%fused_computation.27 | convolution fusion | flops 17179869184 | bytes 33554432 | tf_op jit(solution)/shard_map/dot_general | solution.py:30
  544.7 36.6 %multiply_convert_fusion.1 = (bf16[2048,2048]{0,1:T(8,128)(2,1)}, bf16[2048,2048]{0,1:T(8,128)(2,1)}, bf16[2048,2048]{0,1:T(8,128)(2,1)}) fusion(f32[2048,2048]{0,1:T(8,128)} %fusion.144, f32[2048,2048]{0,1:T(8,128)} %fusion.17, bf16[2048,2048]{1,0:T(8,128)(2,1)} %multiply_convert_fusion.3, bf16[2048,4096]{1,0:T(8,128)(2,1)} %all-gather.9.cloned.1.call-done), kind=kOutput, calls=%fused_computation.8 | convolution fusion | flops 17242783744 | bytes 75497472 | tf_op jit(solution)/shard_map/dot_general | solution.py:30
  581.3 44.2 %fusion.58 = bf16[2048,2048]{1,0:T(8,128)(2,1)} fusion(bf16[2048,4096]{1,0:T(8,128)(2,1)} %all-gather.9.cloned.1.call-done, bf16[2048,2048]{0,1:T(8,128)(2,1)} %get-tuple-element.92, bf16[2048,2048]{0,1:T(8,128)(2,1)} %get-tuple-element.91), kind=kOutput, calls=%fused_computation.80 | convolution fusion | flops 34397487104 | bytes 41943040 | tf_op jit(solution)/shard_map/dot_general | solution.py:30
  629.1 22.4 %convolution_convert_fusion.2 = bf16[2048,2048]{1,0:T(8,128)(2,1)S(1)} fusion(bf16[2048,2048]{0,1:T(8,128)(2,1)} %get-tuple-element.93, bf16[2048,2048]{0,1:T(8,128)(2,1)} %all-gather.11.cloned.1.call-done), kind=kOutput, calls=%fused_computation.79 | convolution fusion | flops 17184063488 | bytes 25165824 | tf_op jit(solution)/shard_map/dot_general | solution.py:30
  658.1 18.9 %collective-permute-done.22 = bf16[2,512,1024]{2,1,0:T(8,128)(2,1)S(1)} collective-permute-done((bf16[2,512,1024]{2,1,0:T(8,128)(2,1)S(1)}, bf16[2,512,1024]{2,1,0:T(8,128)(2,1)S(1)}, u32[]{:S(2)}, u32[]{:S(2)}) %collective-permute-start.22) | collective-permute-done | bytes 2097184 | tf_op jit(solution)/shard_map/ppermute | solution.py:41
  679.2 39.5 %collective-permute-done.14 = bf16[2,512,1024]{2,1,0:T(8,128)(2,1)S(1)} collective-permute-done((bf16[2,512,1024]{2,1,0:T(8,128)(2,1)S(1)}, bf16[2,512,1024]{2,1,0:T(8,128)(2,1)S(1)}, u32[]{:S(2)}, u32[]{:S(2)}) %collective-permute-start.14) | collective-permute-done | bytes 2097184 | tf_op jit(solution)/shard_map/ppermute | solution.py:41
  725.8 44.1 %collective-permute-done.23 = bf16[1,512,1024]{2,1,0:T(8,128)(2,1)S(1)} collective-permute-done((bf16[1,512,1024]{2,1,0:T(8,128)(2,1)S(1)}, bf16[1,512,1024]{2,1,0:T(8,128)(2,1)S(1)}, u32[]{:S(2)}, u32[]{:S(2)}) %collective-permute-start.23) | collective-permute-done | bytes 1048608 | tf_op jit(solution)/shard_map/ppermute | solution.py:41
  858.5 75.4 %attend_back.1 = (bf16[2048,512]{1,0:T(8,128)(2,1)}, bf16[2,2048,64]{2,1,0:T(8,128)(2,1)}, bf16[2,2048,64]{2,1,0:T(8,128)(2,1)}) custom-call(s32[1]{0:T(128)} %bitcast.1.me_ref, bf16[2048,512]{1,0:T(8,128)(2,1)} %get-tuple-element.21.q_ref, bf16[2,2048,64]{2,1,0:T(8,128)(2,1)} %get-tuple-element.22.k_ref, bf16[2,2048,64]{2,1,0:T(8,128)(2,1)} %get-tuple-element.23.v_ref, ...), custom_call_target="tpu_custom_call" | custom-call | flops 42949672960 | bytes 16777216 | tf_op jit(solution)/shard_map/attend_back/pallas_call | solution.py:317
  959.1 22.6 %collective-permute-done.41 = bf16[1,512,1024]{2,1,0:T(8,128)(2,1)S(1)} collective-permute-done((bf16[1,512,1024]{2,1,0:T(8,128)(2,1)S(1)}, bf16[1,512,1024]{2,1,0:T(8,128)(2,1)S(1)}, u32[]{:S(2)}, u32[]{:S(2)}) %collective-permute-start.41) | collective-permute-done | bytes 1048608 | tf_op jit(solution)/shard_map/ppermute | solution.py:41
  982.4 37.1 %collective-permute-done.43 = bf16[2,512,1024]{2,1,0:T(8,128)(2,1)S(1)} collective-permute-done((bf16[2,512,1024]{2,1,0:T(8,128)(2,1)S(1)}, bf16[2,512,1024]{2,1,0:T(8,128)(2,1)S(1)}, u32[]{:S(2)}, u32[]{:S(2)}) %collective-permute-start.43) | collective-permute-done | bytes 2097184 | tf_op jit(solution)/shard_map/ppermute | solution.py:41
  1036.2 33.5 %convolution_convert_fusion.1 = bf16[2048,2048]{1,0:T(8,128)(2,1)} fusion(bf16[2048,2048]{0,1:T(8,128)(2,1)} %get-tuple-element.93, bf16[512,1024]{1,0:T(8,128)(2,1)} %get-tuple-element.140, bf16[512,1024]{1,0:T(8,128)(2,1)S(1)} %copy-done.47, bf16[512,1024]{1,0:T(8,128)(2,1)} %bitcast.54, bf16[512,1024]{1,0:T(8,128)(2,1)S(1)} %copy-done.46, ...), kind=kOutput, calls=%fused_computation.78 | convolution fusion | flops 17242783744 | bytes 25165824 | tf_op jit(solution)/shard_map/dot_general | solution.py:30
  1069.8 43.9 %convolution_convert_fusion = bf16[2048,4096]{1,0:T(8,128)(2,1)} fusion(bf16[2048,2048]{1,0:T(8,128)(2,1)} %multiply_convert_fusion.3, bf16[2048,2048]{0,1:T(8,128)(2,1)} %get-tuple-element.92, bf16[2048,2048]{0,1:T(8,128)(2,1)} %get-tuple-element.91), kind=kOutput, calls=%fused_computation.17 | convolution fusion | flops 34401681408 | bytes 41943040 | tf_op jit(solution)/shard_map/dot_general | solution.py:30
  1116.4 29.0 %collective-permute-done.33 = bf16[1,2048,384]{2,1,0:T(8,128)(2,1)S(1)} collective-permute-done((bf16[1,2048,384]{2,1,0:T(8,128)(2,1)S(1)}, bf16[1,2048,384]{2,1,0:T(8,128)(2,1)S(1)}, u32[]{:S(2)}, u32[]{:S(2)}) %collective-permute-start.33) | collective-permute-done | bytes 1572896 | tf_op jit(solution)/shard_map/ppermute | solution.py:41
  1160.4 52.6 %collective-permute-done.34 = bf16[2,2048,384]{2,1,0:T(8,128)(2,1)} collective-permute-done((bf16[2,2048,384]{2,1,0:T(8,128)(2,1)}, bf16[2,2048,384]{2,1,0:T(8,128)(2,1)}, u32[]{:S(2)}, u32[]{:S(2)}) %collective-permute-start.34) | collective-permute-done | bytes 3145760 | tf_op jit(solution)/shard_map/ppermute | solution.py:41
  1237.8 28.0 %collective-permute-done.57 = f32[8,128]{1,0:T(8,128)S(1)} collective-permute-done((f32[8,128]{1,0:T(8,128)S(1)}, f32[8,128]{1,0:T(8,128)S(1)}, u32[]{:S(2)}, u32[]{:S(2)}) %collective-permute-start.57) | collective-permute-done | bytes 4128 | tf_op jit(solution)/shard_map/ppermute | solution.py:41
  (470 shorter events, 522.8 us)
Async XLA Ops:
  7.2 119.3 %all-gather.7.cloned.1.call-start = ((), (), s32[]{:S(2)}) async-start(), calls=%async_computation.5 | async-start | bytes 2359296 | tf_op jit(solution)/shard_map/all_gather | solution.py:91
  9.2 185.4 %all-gather.5.cloned.1.call-start = ((), (), s32[]{:S(2)}) async-start(), calls=%async_computation.4 | async-start | bytes 4128768 | tf_op jit(solution)/shard_map/all_gather | solution.py:91
  13.4 476.2 %all-gather.11.cloned.1.call-start = ((), (), s32[]{:S(2)}) async-start(), calls=%async_computation.7 | async-start | bytes 9437184 | tf_op jit(solution)/shard_map/all_gather | solution.py:91
  15.7 504.2 %all-gather.9.cloned.1.call-start = ((), (), s32[]{:S(2)}) async-start(), calls=%async_computation.6 | async-start | bytes 18874368 | tf_op jit(solution)/shard_map/all_gather | solution.py:91
  24.5 67.3 %collective-permute-start.18 = (bf16[1,512,1024]{2,1,0:T(8,128)(2,1)}, bf16[1,512,1024]{2,1,0:T(8,128)(2,1)}, u32[]{:S(2)}, u32[]{:S(2)}) collective-permute-start(bf16[1,512,1024]{2,1,0:T(8,128)(2,1)} %get-tuple-element.143), channel_id=1, source_target_pairs={{0,1},{1,0},{2,3},{3,2},{4,5},{5,4},{6,7},{7,6},{8,9},{9,8},{10,11... | collective-permute-start | bytes 3145736 | tf_op jit(solution)/shard_map/ppermute | solution.py:41
  26.0 69.4 %collective-permute-start.19 = (bf16[1,512,1024]{2,1,0:T(8,128)(2,1)}, bf16[1,512,1024]{2,1,0:T(8,128)(2,1)}, u32[]{:S(2)}, u32[]{:S(2)}) collective-permute-start(bf16[1,512,1024]{2,1,0:T(8,128)(2,1)} %get-tuple-element.144), channel_id=1, source_target_pairs={{0,2},{1,3},{2,0},{3,1},{4,6},{5,7},{6,4},{7,5},{8,10},{9,11},{10,... | collective-permute-start | bytes 3145736 | tf_op jit(solution)/shard_map/ppermute | solution.py:41
  29.7 1259.5 %reduce-scatter.5.cloned.1.call-start = ((), (), s32[]{:S(2)}) async-start(), calls=%async_computation.8 | async-start | bytes 3538944 | tf_op jit(solution)/shard_map/reduce_scatter | solution.py:95
  94.9 73.4 %collective-permute-start.21 = (bf16[2,512,1024]{2,1,0:T(8,128)(2,1)}, bf16[2,512,1024]{2,1,0:T(8,128)(2,1)}, u32[]{:S(2)}, u32[]{:S(2)}) collective-permute-start(bf16[2,512,1024]{2,1,0:T(8,128)(2,1)} %pad_maximum_fusion.23), channel_id=1, source_target_pairs={{0,2},{1,3},{2,0},{3,1},{4,6},{5,7},{6,4},{7,5},{8,10},{9,11},{10,... | collective-permute-start | bytes 6291464 | tf_op jit(solution)/shard_map/ppermute | solution.py:41
  98.7 72.7 %collective-permute-start.20 = (bf16[2,512,1024]{2,1,0:T(8,128)(2,1)}, bf16[2,512,1024]{2,1,0:T(8,128)(2,1)}, u32[]{:S(2)}, u32[]{:S(2)}) collective-permute-start(bf16[2,512,1024]{2,1,0:T(8,128)(2,1)} %pad_maximum_fusion.22), channel_id=1, source_target_pairs={{0,1},{1,0},{2,3},{3,2},{4,5},{5,4},{6,7},{7,6},{8,9},{9,8},{10,11... | collective-permute-start | bytes 6291464 | tf_op jit(solution)/shard_map/ppermute | solution.py:41
  130.0 60.7 %collective-permute-start.10 = (bf16[1,2048,256]{1,2,0:T(8,128)(2,1)S(1)}, bf16[1,2048,256]{1,2,0:T(8,128)(2,1)S(1)}, u32[]{:S(2)}, u32[]{:S(2)}) collective-permute-start(bf16[1,2048,256]{1,2,0:T(8,128)(2,1)S(1)} %get-tuple-element.164), channel_id=1, source_target_pairs={{0,1},{1,0},{2,3},{3,2},{4,5},{5,4},{6,7},{7,6},{8,9},{9,8},{10,11... | collective-permute-start | bytes 3145736 | tf_op jit(solution)/shard_map/ppermute | solution.py:41
  190.0 85.7 %collective-permute-start.12 = (bf16[2,2048,256]{1,2,0:T(8,128)(2,1)}, bf16[2,2048,256]{1,2,0:T(8,128)(2,1)}, u32[]{:S(2)}, u32[]{:S(2)}) collective-permute-start(bf16[2,2048,256]{1,2,0:T(8,128)(2,1)} %pad_maximum_fusion.17), channel_id=1, source_target_pairs={{0,1},{1,0},{2,3},{3,2},{4,5},{5,4},{6,7},{7,6},{8,9},{9,8},{10,11... | collective-permute-start | bytes 6291464 | tf_op jit(solution)/shard_map/ppermute | solution.py:41
  193.2 103.7 %collective-permute-start.13 = (bf16[2,2048,256]{1,2,0:T(8,128)(2,1)}, bf16[2,2048,256]{1,2,0:T(8,128)(2,1)}, u32[]{:S(2)}, u32[]{:S(2)}) collective-permute-start(bf16[2,2048,256]{1,2,0:T(8,128)(2,1)} %pad_maximum_fusion.18), channel_id=1, source_target_pairs={{0,2},{1,3},{2,0},{3,1},{4,6},{5,7},{6,4},{7,5},{8,10},{9,11},{10,... | collective-permute-start | bytes 6291464 | tf_op jit(solution)/shard_map/ppermute | solution.py:41
  652.1 66.6 %collective-permute-start.14 = (bf16[2,512,1024]{2,1,0:T(8,128)(2,1)S(1)}, bf16[2,512,1024]{2,1,0:T(8,128)(2,1)S(1)}, u32[]{:S(2)}, u32[]{:S(2)}) collective-permute-start(bf16[2,512,1024]{2,1,0:T(8,128)(2,1)S(1)} %pad_maximum_fusion.20), channel_id=1, source_target_pairs={{0,1},{1,0},{2,3},{3,2},{4,5},{5,4},{6,7},{7,6},{8,9},{9,8},{10,11... | collective-permute-start | bytes 6291464 | tf_op jit(solution)/shard_map/ppermute | solution.py:41
  653.8 72.0 %collective-permute-start.24 = (bf16[2,512,1024]{2,1,0:T(8,128)(2,1)S(1)}, bf16[2,512,1024]{2,1,0:T(8,128)(2,1)S(1)}, u32[]{:S(2)}, u32[]{:S(2)}) collective-permute-start(bf16[2,512,1024]{2,1,0:T(8,128)(2,1)S(1)} %pad_maximum_fusion.25), channel_id=1, source_target_pairs={{0,2},{1,3},{2,0},{3,1},{4,6},{5,7},{6,4},{7,5},{8,10},{9,11},{10,... | collective-permute-start | bytes 6291464 | tf_op jit(solution)/shard_map/ppermute | solution.py:41
  654.5 118.7 %collective-permute-start.16 = (bf16[2,512,1024]{2,1,0:T(8,128)(2,1)S(1)}, bf16[2,512,1024]{2,1,0:T(8,128)(2,1)S(1)}, u32[]{:S(2)}, u32[]{:S(2)}) collective-permute-start(bf16[2,512,1024]{2,1,0:T(8,128)(2,1)S(1)} %pad_maximum_fusion.21), channel_id=1, source_target_pairs={{0,2},{1,3},{2,0},{3,1},{4,6},{5,7},{6,4},{7,5},{8,10},{9,11},{10,... | collective-permute-start | bytes 6291464 | tf_op jit(solution)/shard_map/ppermute | solution.py:41
  678.6 91.2 %collective-permute-start.23 = (bf16[1,512,1024]{2,1,0:T(8,128)(2,1)S(1)}, bf16[1,512,1024]{2,1,0:T(8,128)(2,1)S(1)}, u32[]{:S(2)}, u32[]{:S(2)}) collective-permute-start(bf16[1,512,1024]{2,1,0:T(8,128)(2,1)S(1)} %fusion.119), channel_id=1, source_target_pairs={{0,2},{1,3},{2,0},{3,1},{4,6},{5,7},{6,4},{7,5},{8,10},{9,11},{10,... | collective-permute-start | bytes 3145736 | tf_op jit(solution)/shard_map/ppermute | solution.py:41
  719.1 69.4 %collective-permute-start.15 = (bf16[1,512,1024]{2,1,0:T(8,128)(2,1)S(1)}, bf16[1,512,1024]{2,1,0:T(8,128)(2,1)S(1)}, u32[]{:S(2)}, u32[]{:S(2)}) collective-permute-start(bf16[1,512,1024]{2,1,0:T(8,128)(2,1)S(1)} %fusion.117), channel_id=1, source_target_pairs={{0,2},{1,3},{2,0},{3,1},{4,6},{5,7},{6,4},{7,5},{8,10},{9,11},{10,... | collective-permute-start | bytes 3145736 | tf_op jit(solution)/shard_map/ppermute | solution.py:41
  837.8 119.6 %collective-permute-start.40 = (bf16[1,512,1024]{2,1,0:T(8,128)(2,1)S(1)}, bf16[1,512,1024]{2,1,0:T(8,128)(2,1)}, u32[]{:S(2)}, u32[]{:S(2)}) collective-permute-start(bf16[1,512,1024]{2,1,0:T(8,128)(2,1)S(1)} %get-tuple-element.133), channel_id=1, source_target_pairs={{0,1},{1,0},{2,3},{3,2},{4,5},{5,4},{6,7},{7,6},{8,9},{9,8},{10,11... | collective-permute-start | bytes 3145736 | tf_op jit(solution)/shard_map/ppermute | solution.py:41
  955.4 345.2 %reduce-scatter.7.cloned.1.call-start = ((), (), s32[]{:S(2)}) async-start(), calls=%async_computation.9 | async-start | bytes 2359296 | tf_op jit(solution)/shard_map/reduce_scatter | solution.py:95
  958.9 60.7 %collective-permute-start.43 = (bf16[2,512,1024]{2,1,0:T(8,128)(2,1)S(1)}, bf16[2,512,1024]{2,1,0:T(8,128)(2,1)S(1)}, u32[]{:S(2)}, u32[]{:S(2)}) collective-permute-start(bf16[2,512,1024]{2,1,0:T(8,128)(2,1)S(1)} %pad_maximum_fusion.28), channel_id=1, source_target_pairs={{0,2},{1,3},{2,0},{3,1},{4,6},{5,7},{6,4},{7,5},{8,10},{9,11},{10,... | collective-permute-start | bytes 6291464 | tf_op jit(solution)/shard_map/ppermute | solution.py:41
  1036.2 285.3 %reduce-scatter.11.cloned.1.call-start = ((), (), s32[]{:S(2)}) async-start(), calls=%async_computation.11 | async-start | bytes 9437184 | tf_op jit(solution)/shard_map/reduce_scatter | solution.py:95
  1069.8 274.5 %reduce-scatter.9.cloned.1.call-start = ((), (), s32[]{:S(2)}) async-start(), calls=%async_computation.10 | async-start | bytes 18874368 | tf_op jit(solution)/shard_map/reduce_scatter | solution.py:95
  1147.4 65.6 %collective-permute-start.34 = (bf16[2,2048,384]{2,1,0:T(8,128)(2,1)}, bf16[2,2048,384]{2,1,0:T(8,128)(2,1)}, u32[]{:S(2)}, u32[]{:S(2)}) collective-permute-start(bf16[2,2048,384]{2,1,0:T(8,128)(2,1)} %pad_maximum_fusion.11), channel_id=1, source_target_pairs={{0,1},{1,0},{2,3},{3,2},{4,5},{5,4},{6,7},{7,6},{8,9},{9,8},{10,11... | collective-permute-start | bytes 9437192 | tf_op jit(solution)/shard_map/ppermute | solution.py:41
  1151.6 64.4 %collective-permute-start.35 = (bf16[2,2048,384]{2,1,0:T(8,128)(2,1)}, bf16[2,2048,384]{2,1,0:T(8,128)(2,1)}, u32[]{:S(2)}, u32[]{:S(2)}) collective-permute-start(bf16[2,2048,384]{2,1,0:T(8,128)(2,1)} %pad_maximum_fusion.12), channel_id=1, source_target_pairs={{0,2},{1,3},{2,0},{3,1},{4,6},{5,7},{6,4},{7,5},{8,10},{9,11},{10,... | collective-permute-start | bytes 9437192 | tf_op jit(solution)/shard_map/ppermute | solution.py:41
  (122 other events, 2497.7 us)
Sparse Core Ops, SparseCore 0:
  10.2 33.5 all-gather.6
  46.0 41.6 all-gather.4
  89.3 81.3 all-gather.10
  172.7 149.2 all-gather.8
  955.6 41.4 reduce-scatter.4
  1036.3 35.7 reduce-scatter.6
  1074.9 88.2 reduce-scatter.10
  1165.6 166.5 reduce-scatter.8

commit v2 on v1

--- a/solution.py
+++ b/solution.py
@@ -378,7 +378,7 @@
     return jnp.concatenate(ordered, axis=1).astype(F32)
 
 
-def body(
+def general_body(
     inputs, cotangent, segments, valid_mask, query_weight, key_weight, value_weight, out_weight,
     gate_weight, up_weight, down_weight, attn_gain, mlp_gain,
 ):
@@ -522,6 +522,793 @@
     )
 
 
+TILE = 256
+
+
+def after(value, *events):
+    return lax.optimization_barrier((value,) + events)[0]
+
+
+def to_both(block):
+    return swap(block, 1), swap(block, 2)
+
+
+def pass_on(by_x, by_y, *events):
+    half = by_x.shape[0] // 2
+    return swap(after(by_y[:half], *events), 1), swap(after(by_x[half:], *events), 2)
+
+
+def add_low(a, b):
+    return (a.astype(F32) + b.astype(F32)).astype(BF)
+
+
+def send_far(block):
+    half = block.shape[0] // 2
+    return swap(block[:half], 1), swap(block[half:], 2)
+
+
+def add_far(for_x, for_y, low, high):
+    half = for_x.shape[0] // 2
+    return (
+        jnp.concatenate([for_x[:half], add_low(for_x[half:], high)], axis=0),
+        jnp.concatenate([add_low(for_y[:half], low), for_y[half:]], axis=0),
+    )
+
+
+def call(kernel, grid, in_specs, out_specs, out_shape, args, name, flops=0, moved=0, scratch=(), prefetch=0, aliases=None):
+    return pl.pallas_call(
+        kernel,
+        grid_spec=pltpu.PrefetchScalarGridSpec(
+            num_scalar_prefetch=prefetch,
+            grid=grid,
+            in_specs=in_specs,
+            out_specs=out_specs,
+            scratch_shapes=list(scratch),
+        ),
+        out_shape=out_shape,
+        input_output_aliases=aliases or {},
+        compiler_params=params(len(grid)),
+        cost_estimate=pl.CostEstimate(flops=int(flops), bytes_accessed=int(moved), transcendentals=0),
+        name=name,
+    )(*args)
+
+
+def shape_of(shape, dtype=BF):
+    return jax.ShapeDtypeStruct(shape, dtype)
+
+
+def fixed(shape, buffers=None):
+    mode = {} if buffers is None else {"pipeline_mode": pl.Buffered(buffers)}
+    return pl.BlockSpec(shape, lambda *_: (0,) * len(shape), **mode)
+
+
+def piece_specs(pieces, tile):
+    specs, spans, start = [], [], 0
+    for piece in pieces:
+        tiles = piece.shape[0] // tile
+        specs.append(
+            pl.BlockSpec(
+                (tile, piece.shape[1]),
+                lambda i, *_, start=start, tiles=tiles: (jnp.clip(i - start, 0, tiles - 1), 0),
+            )
+        )
+        spans.append((start, start + tiles))
+        start += tiles
+    return specs, spans
+
+
+def copy_piece(refs, spans, index, target):
+    for ref, (first, last) in zip(refs, spans):
+
+        @pl.when((index >= first) & (index < last))
+        def _(ref=ref):
+            target[...] = ref[...]
+
+
+def join_kernel(spans, *refs):
+    copy_piece(refs[:-1], spans, pl.program_id(0), refs[-1])
+
+
+def join(pieces):
+    specs, spans = piece_specs(pieces, TILE)
+    rows, width = spans[-1][1] * TILE, pieces[0].shape[1]
+    return call(
+        functools.partial(join_kernel, spans), (rows // TILE,), specs,
+        pl.BlockSpec((TILE, width), lambda i: (i, 0)), shape_of((rows, width)), pieces, "join",
+        moved=4 * rows * width,
+    )
+
+
+def act_back_kernel(spans, others, *refs):
+    weight_ref = refs[len(spans)]
+    whole_ref, out_ref = refs[len(spans) + 1 + others :]
+    copy_piece(refs[: len(spans)], spans, pl.program_id(0), whole_ref)
+    out_ref[...] = dot(whole_ref[...], weight_ref[...]).astype(BF)
+
+
+def act_back(pieces, weight, first, rows, before=()):
+    specs, spans = piece_specs(pieces, TILE)
+    tiles, skip, width = spans[-1][1], first // TILE, weight.shape[1]
+    by_row = lambda w: pl.BlockSpec((TILE, w), lambda i: (skip + i, 0))
+    count = len(pieces) + 1
+    return call(
+        functools.partial(act_back_kernel, spans, len(before)), (tiles,),
+        specs + [fixed(weight.shape)] + [pl.BlockSpec(memory_space=pl.ANY)] * len(before),
+        [by_row(D), by_row(width)], [shape_of((rows, D)), shape_of((rows, width))],
+        (*pieces, weight, *before), "act_back", flops=2 * tiles * TILE * D * width, moved=tiles * TILE * D * 6,
+        aliases={count + k: k for k in range(len(before))},
+    )
+
+
+def pack_qkv_kernel(kv_local, me_ref, q_ref, k_ref, v_ref, gains_ref, out_ref):
+    width = GROUP * HEAD_DIM
+    parts = []
+    for g in range(kv_local):
+        head = slice(g * HEAD_DIM, (g + 1) * HEAD_DIM)
+        parts += [q_ref[:, g * width : (g + 1) * width], jnp.concatenate([k_ref[:, head], v_ref[:, head]], axis=1)]
+    out_ref[...] = jnp.concatenate(parts + [gains_ref[...]], axis=1)
+
+
+def pack_qkv(me_row, query_weight, key_weight, value_weight, gains, kv_local):
+    rows = query_weight.shape[0]
+    q_width, kv_width = kv_local * GROUP * HEAD_DIM, kv_local * HEAD_DIM
+    total = q_width + 2 * kv_width + LANES
+    mine = lambda width: pl.BlockSpec((rows, width), lambda i, me: (0, me[0]))
+    return call(
+        functools.partial(pack_qkv_kernel, kv_local), (1,),
+        [mine(q_width), mine(kv_width), mine(kv_width), fixed((rows, LANES))],
+        fixed((rows, total)), shape_of((rows, total)),
+        (me_row, query_weight, key_weight, value_weight, gains), "pack_qkv", moved=4 * rows * total, prefetch=1,
+    )
+
+
+def pack_rows_kernel(me_ref, in_ref, out_ref):
+    out_ref[...] = in_ref[...].astype(F32).T.astype(BF)
+
+
+def pack_rows(me_row, weight, rows):
+    tile = 512
+    tiles, columns = rows // tile, weight.shape[1]
+    return call(
+        pack_rows_kernel, (tiles,), [pl.BlockSpec((tile, columns), lambda i, me: (me[0] * tiles + i, 0))],
+        pl.BlockSpec((columns, tile), lambda i, me: (0, i)), shape_of((columns, rows)), (me_row, weight),
+        "pack_rows", moved=4 * rows * columns, prefetch=1,
+    )
+
+
+def pack_pair_kernel(me_ref, a_ref, b_ref, out_ref):
+    width = a_ref.shape[1]
+    out_ref[:, :width] = a_ref[...]
+    out_ref[:, width:] = b_ref[...]
+
+
+def pack_pair(me_row, a, b, chunks, chunk, width):
+    rows = a.shape[0]
+    spec = pl.BlockSpec((rows, width), lambda i, me: (0, me[0] * chunks + chunk))
+    return call(
+        pack_pair_kernel, (1,), [spec, spec], fixed((rows, 2 * width)), shape_of((rows, 2 * width)), (me_row, a, b),
+        "pack_pair", moved=8 * rows * width, prefetch=1,
+    )
+
+
+def enter_kernel(kv_local, spans, others, *refs):
+    pieces = refs[: len(spans)]
+    gain_ref, w_ref, cos_ref, sin_ref = refs[len(spans) : len(spans) + 4]
+    x_ref, normed_ref, q_ref, k_ref, v_ref = refs[len(spans) + 4 + others :]
+    copy_piece(pieces, spans, pl.program_id(0), x_ref)
+    x = x_ref[...].astype(F32)
+    inv = lax.rsqrt(jnp.mean(x * x, axis=-1, keepdims=True) + EPSILON)
+    normed = (x * inv * gain_ref[...]).astype(BF)
+    normed_ref[...] = normed
+    width = GROUP * HEAD_DIM
+    step = width + 2 * HEAD_DIM
+    lin = dot(normed, w_ref[:, : kv_local * step])
+    cosine, sine = cos_ref[...], sin_ref[...]
+    for g in range(kv_local):
+        for start in range(0, width, LANES):
+            part = turn(lin[:, g * step + start : g * step + start + LANES], cosine, sine) * SCALE
+            q_ref[:, g * width + start : g * width + start + LANES] = part.astype(BF)
+        pair = lin[:, g * step + width : (g + 1) * step]
+        k_ref[g] = turn(pair, cosine, sine)[:, :HEAD_DIM].astype(BF)
+        v_ref[g] = pair[:, HEAD_DIM:].astype(BF)
+
+
+def enter(pieces, gain_row, weight, cosine, sine, kv_local, first, rows, before=()):
+    specs, spans = piece_specs(pieces, TILE)
+    tiles, skip = spans[-1][1], first // TILE
+    q_width = kv_local * GROUP * HEAD_DIM
+    by_row = lambda width: pl.BlockSpec((TILE, width), lambda i: (skip + i, 0))
+    by_head = pl.BlockSpec((kv_local, TILE, HEAD_DIM), lambda i: (0, skip + i, 0))
+    heads = shape_of((kv_local, rows, HEAD_DIM))
+    count = len(pieces) + 4
+    return call(
+        functools.partial(enter_kernel, kv_local, spans, len(before)), (tiles,),
+        specs
+        + [fixed((1, D)), fixed(weight.shape), by_row(LANES), by_row(LANES)]
+        + [pl.BlockSpec(memory_space=pl.ANY)] * len(before),
+        [by_row(D), by_row(D), by_row(q_width), by_head, by_head],
+        [shape_of((rows, D)), shape_of((rows, D)), shape_of((rows, q_width)), heads, heads],
+        (*pieces, gain_row, weight, cosine, sine, *before), "enter",
+        flops=2 * tiles * TILE * D * weight.shape[1], moved=tiles * TILE * D * 8,
+        aliases={count + k: k for k in range(len(before))},
+    )
+
+
+def attend_one(me_row, q, k, v, query_row, key_col, rows, group):
+    length = k.shape[1]
+    width = GROUP * HEAD_DIM
+    head = pl.BlockSpec((1, length, HEAD_DIM), lambda g, i, me: (group, 0, 0))
+    return call(
+        functools.partial(attend_kernel, rows), (1, length // rows),
+        [
+            pl.BlockSpec((rows, width), lambda g, i, me: (i ^ me[0], group)),
+            head,
+            head,
+            pl.BlockSpec((1, rows), lambda g, i, me: (0, i ^ me[0])),
+            fixed((length, 1)),
+        ],
+        [
+            pl.BlockSpec((rows, width), lambda g, i, me: (i ^ me[0], 0)),
+            pl.BlockSpec((1, GROUP, rows), lambda g, i, me: (0, 0, i ^ me[0])),
+        ],
+        [shape_of((length, width)), shape_of((1, GROUP, length), F32)],
+        (me_row, q, k, v, query_row, key_col), "attend", flops=2.6e10, moved=1 << 22, prefetch=1,
+        scratch=[
+            pltpu.VMEM((HEAD_DIM, length), BF),
+            pltpu.VMEM((GROUP, rows), F32),
+            pltpu.VMEM((GROUP, rows), F32),
+            pltpu.VMEM((GROUP, HEAD_DIM, rows), F32),
+        ],
+    )
+
+
+def leave_kernel(groups, per, tiles, x_ref, gain_ref, *refs):
+    heads, weights, (normed_ref, attn_ref) = refs[: 5 * groups], refs[5 * groups : 5 * groups + 5], refs[5 * groups + 5 :]
+    index = pl.program_id(0)
+    attn = jnp.zeros(x_ref.shape, F32)
+    for k in range(3):
+        attn = attn + dot(jnp.concatenate([heads[5 * g + k][...] for g in range(groups)], axis=1), weights[k][...], NT)
+    stored = ((index // per) ^ 3) * per + index % per
+    is_low = stored < tiles // 2
+    far = jnp.concatenate(
+        [jnp.where(is_low, heads[5 * g + 3][...], heads[5 * g + 4][...]) for g in range(groups)], axis=1
+    )
+    attn = attn + jnp.concatenate([dot(far, weights[3][...], NT), dot(far, weights[4][...], NT)], axis=1)
+    middle = x_ref[...].astype(F32) + attn
+    inv = lax.rsqrt(jnp.mean(middle * middle, axis=-1, keepdims=True) + EPSILON)
+    normed_ref[...] = (middle * inv * gain_ref[...]).astype(BF)
+
+    @pl.when(index < per)
+    def _():
+        attn_ref[...] = attn
+
+
+def leave(x_all, gain_row, heads, weights, rows):
+    length = x_all.shape[0]
+    per, tiles = rows // TILE, length // TILE
+    by_row = pl.BlockSpec((TILE, D), lambda i: (i, 0))
+
+    def head_spec(k, low, high, width):
+        return pl.BlockSpec(
+            (TILE, width), lambda i: (jnp.clip(((i // per) ^ k) * per + i % per - low, 0, high - low - 1), 0)
+        )
+
+    specs = []
+    for pieces in heads:
+        width = pieces[0].shape[1]
+        for k in range(3):
+            specs.append(head_spec(k, 0, tiles, width))
+        specs += [head_spec(3, 0, tiles // 2, width), head_spec(3, tiles // 2, tiles, width)]
+    return call(
+        functools.partial(leave_kernel, len(heads), per, tiles), (tiles,),
+        [by_row, fixed((1, D))] + specs + [fixed(w.shape) for w in weights],
+        [by_row, pl.BlockSpec((TILE, D), lambda i: (jnp.minimum(i, per - 1), 0))],
+        [shape_of((length, D)), shape_of((rows, D), F32)],
+        (x_all, gain_row, *[p for pieces in heads for p in pieces], *weights), "leave",
+        flops=2 * length * D * D, moved=length * D * 8,
+    )
+
+
+def up_kernel(normed_ref, gate_ref, up_ref, grad_ref, act_ref, grad_gate_ref, grad_up_ref):
+    normed = normed_ref[...]
+    for start in range(0, act_ref.shape[1], 256):
+        part = slice(start, start + 256)
+        gate = dot(normed, gate_ref[:, part])
+        up = dot(normed, up_ref[:, part])
+        grad = grad_ref[:, part].astype(F32)
+        sigmoid = jax.nn.sigmoid(gate)
+        silu = gate * sigmoid
+        act_ref[:, part] = (silu * up).astype(BF)
+        grad_gate_ref[:, part] = (grad * up * (sigmoid + silu * (1.0 - sigmoid))).astype(BF)
+        grad_up_ref[:, part] = (grad * silu).astype(BF)
+
+
+def up_project(normed, gate_up, grad_act, chunk):
+    length, width = normed.shape[0], gate_up.shape[1] // 2
+    tall, wide = 1024, 512
+    across = width // wide
+    out = pl.BlockSpec((tall, wide), lambda i, j: (i, j))
+    return call(
+        up_kernel, (length // tall, across),
+        [
+            pl.BlockSpec((tall, D), lambda i, j: (i, 0)),
+            pl.BlockSpec((D, wide), lambda i, j: (0, j)),
+            pl.BlockSpec((D, wide), lambda i, j: (0, across + j)),
+            pl.BlockSpec((tall, wide), lambda i, j: (i, chunk * across + j)),
+        ],
+        [out] * 3, [shape_of((length, width))] * 3, (normed, gate_up, gate_up, grad_act), "up_project",
+        flops=4 * length * D * width, moved=length * (D + 4 * width) * 2 + 8 * D * width,
+    )
+
+
+def sum_kernel(*refs):
+    total = None
+    for i in range(0, len(refs) - 1, 2):
+        part = dot(refs[i][...], refs[i + 1][...], NT)
+        total = part if total is None else total + part
+    refs[-1][...] = total.astype(BF)
+
+
+def sum_of(terms, first, rows):
+    tall, wide = 512, 512
+    specs, args = [], []
+    for left, right, column in terms:
+        width = left.shape[1]
+        specs.append(pl.BlockSpec((tall, width), lambda i, j: (first // tall + i, 0)))
+        specs.append(pl.BlockSpec((wide, width), lambda i, j, column=column: (j, column)))
+        args += [left, right]
+    depth = sum(left.shape[1] for left, _, _ in terms)
+    return call(
+        sum_kernel, (rows // tall, D // wide), specs, pl.BlockSpec((tall, wide), lambda i, j: (i, j)),
+        shape_of((rows, D)), args, "sum_of", flops=2 * rows * D * depth, moved=2 * depth * (rows + D) + 2 * rows * D,
+    )
+
+
+def outer_kernel(across, count, left_ref, *refs):
+    for k in range(count):
+
+        @pl.when(pl.program_id(1) // across == k)
+        def _(k=k):
+            refs[-1][...] = dot(left_ref[...], refs[k][...], TN).astype(BF)
+
+
+def outer(left, rights, wide, total=None, first=0, before=()):
+    length, tall, width = left.shape[0], 1024, rights[0].shape[1]
+    across, count = width // wide, len(rights)
+    right_spec = lambda k: pl.BlockSpec((length, wide), lambda i, j: (0, jnp.clip(j - k * across, 0, across - 1)))
+    return call(
+        functools.partial(outer_kernel, across, count), (left.shape[1] // tall, across * count),
+        [pl.BlockSpec((length, tall), lambda i, j: (0, i))]
+        + [right_spec(k) for k in range(count)]
+        + [pl.BlockSpec(memory_space=pl.ANY)] * len(before),
+        pl.BlockSpec((tall, wide), lambda i, j: (i, first // wide + j)),
+        shape_of((left.shape[1], total or width * count)),
+        (left, *rights, *before), "outer", flops=2 * length * left.shape[1] * width * count,
+        moved=2 * (length + left.shape[1]) * (left.shape[1] + width * count),
+        aliases={1 + count: 0} if before else None,
+    )
+
+
+def turn_back_kernel(own_ref, by_x_ref, by_y_ref, x_ref, attn_ref, cot_ref, valid_ref, gain_ref, *refs):
+    weights, (middle_ref, low_ref, heads_ref) = refs[:5], refs[5:]
+    grad = own_ref[...].astype(F32) + by_x_ref[...].astype(F32) + by_y_ref[...].astype(F32)
+    middle = x_ref[...].astype(F32) + attn_ref[...]
+    inv = lax.rsqrt(jnp.mean(middle * middle, axis=-1, keepdims=True) + EPSILON)
+    grad_middle = cot_ref[...].astype(F32) * valid_ref[...] + norm_back(grad, middle, inv, gain_ref[...])
+    middle_ref[...] = grad_middle
+    low = grad_middle.astype(BF)
+    low_ref[...] = low
+    for k in range(3):
+        heads_ref[k] = dot(low, weights[k][...]).astype(BF)
+    heads_ref[3] = (dot(low[:, : D // 2], weights[3][...]) + dot(low[:, D // 2 :], weights[4][...])).astype(BF)
+
+
+def turn_back(terms, x, attn, cot, valid_col, gain_row, weights):
+    rows, width = x.shape[0], weights[0].shape[1]
+    by_row = lambda w: pl.BlockSpec((TILE, w), lambda i: (i, 0))
+    return call(
+        turn_back_kernel, (rows // TILE,),
+        [by_row(D)] * 6 + [by_row(1), fixed((1, D))] + [fixed(w.shape) for w in weights],
+        [by_row(D), by_row(D), pl.BlockSpec((4, TILE, width), lambda i: (0, i, 0))],
+        [shape_of((rows, D), F32), shape_of((rows, D)), shape_of((4, rows, width))],
+        (*terms, x, attn, cot, valid_col, gain_row, *weights), "turn_back",
+        flops=8 * rows * D * width, moved=rows * D * 20,
+    )
+
+
+def attend_back_one_kernel(rows, count, me_ref, *refs):
+    q, k, v, out, own, by_x, by_y, by_xy, total, query_row, key_col, cos, sin, cos_t, sin_t = refs[:15]
+    out_ref, grad, k_t, inner, dq_t, dk_acc, dv_acc = refs[15:]
+    for block, ref in enumerate((own, by_x, by_y, by_xy)):
+        grad[block * rows : (block + 1) * rows, :] = ref[...] if len(ref.shape) == 2 else ref[0]
+    width = GROUP * HEAD_DIM
+    attend_back_kernel(
+        rows, count, me_ref, q, k, v, out, grad, total, query_row, key_col, cos, sin, cos_t, sin_t,
+        out_ref.at[:, :width], LaneSlice(out_ref, width), LaneSlice(out_ref, width + HEAD_DIM),
+        k_t, inner, dq_t, dk_acc, dv_acc,
+    )
+
+
+class LaneSlice:
+    def __init__(self, ref, start):
+        self.ref, self.start = ref, start
+
+    def __setitem__(self, key, value):
+        self.ref[key[1], self.start : self.start + HEAD_DIM] = value
+
+
+def attend_back_one(me_row, q, k, v, out, grads, totals, query_row, key_col, tables, rows, group):
+    length = k.shape[1]
+    width = GROUP * HEAD_DIM
+    whole = lambda shape: fixed(shape, 1)
+    head = pl.BlockSpec((1, length, HEAD_DIM), lambda i, me: (group, 0, 0), pipeline_mode=pl.Buffered(1))
+    part = pl.BlockSpec((rows, width), lambda i, me: (0, group))
+    own = pl.BlockSpec((1, rows, width), lambda i, me: (0, 0, group))
+    out_width = width + 2 * HEAD_DIM
+    return call(
+        functools.partial(attend_back_one_kernel, rows, length // rows), (1,),
+        [
+            pl.BlockSpec((length, width), lambda i, me: (0, group)), head, head, whole((length, width)),
+            own, part, part, part, whole((1, GROUP, length)), whole((1, length)), whole((length, 1)),
+            whole((length, LANES)), whole((length, LANES)),
+            whole((HEAD_DIM // 2, length)), whole((HEAD_DIM // 2, length)),
+        ],
+        whole((length, out_width)), shape_of((length, out_width)),
+        (me_row, q, k, v, out, *grads, totals, query_row, key_col, *tables), "attend_back",
+        flops=3.4e10, moved=1 << 22, prefetch=1,
+        scratch=[
+            pltpu.VMEM((length, width), BF),
+            pltpu.VMEM((HEAD_DIM, length), BF),
+            pltpu.VMEM((GROUP, length), F32),
+            pltpu.VMEM((GROUP, HEAD_DIM, length), F32),
+            pltpu.VMEM((rows, HEAD_DIM), F32),
+            pltpu.VMEM((rows, HEAD_DIM), F32),
+        ],
+    )
+
+
+def finish_kernel(groups, step, x_ref, middle_ref, gain_ref, *refs):
+    grads, weights, out_ref = refs[: 4 * groups], refs[4 * groups : 4 * groups + 5], refs[-1]
+    columns = slice(0, groups * step)
+    grad = jnp.zeros(x_ref.shape, F32)
+    for k in range(3):
+        low = jnp.concatenate([grads[4 * g + k][...] for g in range(groups)], axis=1)
+        grad = grad + dot(low, weights[k][:, columns], NT)
+    low = jnp.concatenate([grads[4 * g + 3][...] for g in range(groups)], axis=1)
+    grad = grad + jnp.concatenate([dot(low, weights[3][:, columns], NT), dot(low, weights[4][:, columns], NT)], axis=1)
+    x = x_ref[...].astype(F32)
+    inv = lax.rsqrt(jnp.mean(x * x, axis=-1, keepdims=True) + EPSILON)
+    out_ref[...] = (middle_ref[...] + norm_back(grad, x, inv, gain_ref[...])).astype(BF)
+
+
+def finish(x, grad_middle, gain_row, grads, weights):
+    rows, step = x.shape[0], grads[0][0].shape[1]
+    by_row = lambda w: pl.BlockSpec((TILE, w), lambda i: (i, 0))
+    return call(
+        functools.partial(finish_kernel, len(grads), step), (rows // TILE,),
+        [by_row(D), by_row(D), fixed((1, D))] + [by_row(step)] * (4 * len(grads)) + [fixed(w.shape) for w in weights],
+        by_row(D), shape_of((rows, D)),
+        (x, grad_middle, gain_row, *[p for parts in grads for p in parts], *weights), "finish",
+        flops=8 * rows * D * step * len(grads), moved=rows * D * 8 + 4 * D * step * 4,
+    )
+
+
+def each_piece(refs, emit):
+    block = pl.program_id(0)
+    for k in range(3):
+
+        @pl.when(block == k)
+        def _(k=k):
+            emit(refs[k][...])
+
+    @pl.when(block == 3)
+    def _():
+        emit(jnp.concatenate([refs[3][...], refs[4][...]], axis=0))
+
+
+def fold(values):
+    return sum(values[:, at : at + LANES] for at in range(0, values.shape[1], LANES))
+
+
+def place_pair_kernel(first, me_ref, *refs):
+    pieces, weight_a, weight_b = refs[:5], refs[5], refs[6]
+    out_a, out_b, dot_ref = refs[-3:]
+    width = out_a.shape[1]
+
+    @pl.when(pl.program_id(0) == 0)
+    def _():
+        dot_ref[...] = jnp.zeros(dot_ref.shape, F32) if first else refs[9][...]
+
+    def emit(values):
+        a, b = values[:, :width].astype(F32), values[:, width:].astype(F32)
+        out_a[...], out_b[...] = a, b
+        dot_ref[...] += fold(a * weight_a[...].astype(F32)) + fold(b * weight_b[...].astype(F32))
+
+    each_piece(pieces, emit)
+
+
+def place_pair(me_row, pieces, weight_a, weight_b, chunks, chunk, before):
+    rows, total = weight_a.shape
+    width = pieces[0].shape[1] // 2
+    column = pl.BlockSpec((rows, width), lambda i, me: (0, (i ^ me[0]) * chunks + chunk))
+    any_spec = pl.BlockSpec(memory_space=pl.ANY)
+    specs = [fixed(p.shape) for p in pieces] + [column, column]
+    args = [me_row, *pieces, weight_a, weight_b]
+    aliases = {}
+    if before is not None:
+        specs += [any_spec, any_spec, fixed((rows, LANES))]
+        args += before
+        aliases = {8: 0, 9: 1}
+    return call(
+        functools.partial(place_pair_kernel, before is None), (4,), specs, [column, column, fixed((rows, LANES))],
+        [shape_of((rows, total), F32)] * 2 + [shape_of((rows, LANES), F32)], args, "place_pair",
+        moved=rows * width * 64, prefetch=1, aliases=aliases,
+    )
+
+
+def place_rows_kernel(me_ref, *refs):
+    def emit(values):
+        refs[5][...] = values.astype(F32).T
+
+    each_piece(refs[:5], emit)
+
+
+def place_rows(me_row, pieces, tall):
+    columns, rows = pieces[0].shape[0], pieces[0].shape[1]
+    across = rows // tall
+
+    def spec(k, piece):
+        return pl.BlockSpec((piece.shape[0], tall), lambda i, j, me: (0, jnp.where(i == k, j, 0)))
+
+    return call(
+        place_rows_kernel, (4, across), [spec(min(k, 3), p) for k, p in enumerate(pieces)],
+        pl.BlockSpec((tall, columns), lambda i, j, me: ((i ^ me[0]) * across + j, 0)),
+        shape_of((4 * rows, columns), F32), (me_row, *pieces), "place_rows", moved=rows * columns * 24, prefetch=1,
+    )
+
+
+def place_attn_kernel(kv_local, me_ref, *refs):
+    pieces, weights, outs, out_ref, dot_ref = refs[:5], refs[5:8], refs[8:11], refs[11], refs[12]
+    width = GROUP * HEAD_DIM
+    step = width + 2 * HEAD_DIM
+
+    @pl.when(pl.program_id(0) == 0)
+    def _():
+        dot_ref[...] = jnp.zeros(dot_ref.shape, F32)
+
+    def emit(values):
+        values = values.astype(F32)
+        take = lambda start, size: jnp.concatenate(
+            [values[:, g * step + start : g * step + start + size] for g in range(kv_local)], axis=1
+        )
+        parts = (take(0, width), take(width, HEAD_DIM), take(width + HEAD_DIM, HEAD_DIM))
+        for part, weight, out in zip(parts, weights, outs):
+            out[...] = part
+            dot_ref[...] += fold(part * weight[...].astype(F32))
+        out_ref[...] = values[:, kv_local * step :].T
+
+    each_piece(pieces, emit)
+
+
+def place_attn(me_row, pieces, query_weight, key_weight, value_weight, kv_local):
+    rows = query_weight.shape[0]
+    q_width = kv_local * GROUP * HEAD_DIM
+    column = lambda width: pl.BlockSpec((rows, width), lambda i, me: (0, i ^ me[0]))
+    columns = [column(q_width), column(kv_local * HEAD_DIM), column(kv_local * HEAD_DIM)]
+    weights = (query_weight, key_weight, value_weight)
+    return call(
+        functools.partial(place_attn_kernel, kv_local), (4,), [fixed(p.shape) for p in pieces] + columns,
+        columns + [pl.BlockSpec((q_width, rows), lambda i, me: (i ^ me[0], 0)), fixed((rows, LANES))],
+        [shape_of(w.shape, F32) for w in weights] + [shape_of((4 * q_width, rows), F32), shape_of((rows, LANES), F32)],
+        (me_row, *pieces, *weights), "place_attn", moved=rows * 5120 * 8, prefetch=1,
+    )
+
+
+CHUNKS = 2
+
+
+def square_body(
+    inputs, cotangent, segments, valid_mask, query_weight, key_weight, value_weight, out_weight,
+    gate_weight, up_weight, down_weight, attn_gain, mlp_gain,
+):
+    count = 4
+    me = lax.axis_index("seq")
+    me_row = me.reshape(1).astype(jnp.int32)
+    rows = inputs.shape[1]
+    length = rows * count
+    kv_local = KV_HEADS // count
+    q_width = kv_local * GROUP * HEAD_DIM
+    ff_local = FF // count
+    ff_chunk = ff_local // CHUNKS
+    step = (GROUP + 2) * HEAD_DIM
+
+    tokens_low, cot_low = inputs[0], cotangent[0]
+    marks = jnp.stack([segments[0], valid_mask[0]])
+    marks_all = jnp.stack([marks] + [swap(marks, k) for k in range(1, count)])
+    x_x, x_y = to_both(after(tokens_low, marks_all))
+
+    segment_all = marks_all[:, 0].reshape(length)
+    valid_all = marks_all[:, 1].reshape(length)
+    valid_col = valid_mask[0].astype(F32)[:, None]
+
+    position = (
+        (jnp.arange(count, dtype=jnp.int32) ^ me)[:, None] * rows + jnp.arange(rows, dtype=jnp.int32)[None, :]
+    ).reshape(length)
+    same = (segment_all[:, None] == segment_all[None, :]) & (position[None, :] < position[:, None])
+    places = jnp.sum(same.astype(jnp.int32), axis=1).astype(F32)
+    half = HEAD_DIM // 2
+    frequency = ROPE_BASE ** (-2.0 * jnp.arange(half, dtype=F32) / HEAD_DIM)
+    angles_t = frequency[:, None] * places[None, :]
+    cosine_t, sine_t = jnp.cos(angles_t), jnp.sin(angles_t)
+    cosine = jnp.tile(cosine_t.T, (1, LANES // half))
+    sign = jnp.tile(jnp.repeat(jnp.array([-1.0, 1.0], F32), half), LANES // HEAD_DIM)
+    sine = jnp.tile(sine_t.T, (1, LANES // half)) * sign[None, :]
+    query_row = jnp.where(valid_all == 1, segment_all, -1).reshape(1, length)
+    key_col = segment_all.reshape(length, 1)
+    tables = (cosine, sine, cosine_t, sine_t)
+
+    gains = jnp.pad(jnp.stack([attn_gain, mlp_gain], axis=1), ((0, 0), (0, LANES - 2)))
+    qkv_full = gather_fsdp(pack_qkv(me_row, query_weight, key_weight, value_weight, gains, kv_local))
+    out_slice = gather_fsdp(pack_rows(me_row, out_weight, q_width))
+    down_t = gather_fsdp(pack_rows(me_row, after(down_weight, x_x, x_y, cosine, sine), ff_local))
+    later_gate = after(gate_weight, x_x, x_y, cosine, sine)
+    gate_up = [
+        gather_fsdp(pack_pair(me_row, later_gate, up_weight, CHUNKS, c, ff_chunk)) for c in range(CHUNKS)
+    ]
+    gain_one = qkv_full[:, kv_local * step].astype(F32).reshape(1, D)
+    gain_two = qkv_full[:, kv_local * step + 1].astype(F32).reshape(1, D)
+
+    x_far = pass_on(x_x, x_y, cosine, sine)
+    entered = enter([tokens_low, x_x, x_y], gain_one, qkv_full, cosine, sine, kv_local, 0, length)
+
+    done = (*x_far, entered[0])
+    o_own = after(out_slice, *done)
+    o_x, o_y = to_both(o_own)
+    x_all, normed_one, q, k, v = enter(
+        list(x_far), gain_one, qkv_full, cosine, sine, kv_local, 3 * rows, length, tuple(entered)
+    )
+    out_0, total_0 = attend_one(me_row, q, k, v, query_row, key_col, rows, 0)
+
+    done = (o_x, o_y, out_0)
+    o_far = pass_on(o_x, o_y, *done)
+    out_pieces = [out_slice, o_x, o_y, *o_far]
+    h_x, h_y = to_both(after(out_0, *done))
+    out_1, total_1 = attend_one(me_row, after(q, *done), k, v, query_row, key_col, rows, 1)
+    heads, totals = [out_0, out_1], [total_0, total_1]
+
+    done = (*o_far, h_x, h_y, out_1)
+    h_far = pass_on(h_x, h_y, *done)
+    heads_0 = [out_0, h_x, h_y, *h_far]
+    h_x, h_y = to_both(after(out_1, *done))
+    grad_low = (after(cot_low, *done).astype(F32) * valid_col).astype(BF)
+
+    done = (*h_far, h_x, h_y, grad_low)
+    h_far = pass_on(h_x, h_y, *done)
+    heads_1 = [out_1, h_x, h_y, *h_far]
+
+    c_own = after(grad_low, *h_far)
+    c_x, c_y = to_both(c_own)
+    normed_two, attn_branch = leave(after(x_all, *h_far), gain_two, [heads_0, heads_1], out_pieces, rows)
+
+    done = (c_x, c_y, normed_two, down_t)
+    c_far = pass_on(c_x, c_y, *done)
+    acted = act_back([after(c_own, *done), c_x, c_y], down_t, 0, length)
+
+    done = (*c_far, acted[0])
+    w_own = after(qkv_full, *done)[:, : kv_local * step]
+    w_x, w_y = to_both(w_own)
+    grad_mlp, grad_act = act_back(list(c_far), down_t, 3 * rows, length, tuple(acted))
+    act_0, gate_0, up_0 = up_project(normed_two, gate_up[0], grad_act, 0)
+    grad_0 = outer(normed_two, [gate_0, up_0], 1024)
+
+    done = (w_x, w_y, grad_0)
+    gate_up_0 = scatter_fsdp(after(grad_0, *done))
+    w_far = pass_on(w_x, w_y, *done)
+    weight_pieces = [w_own, w_x, w_y, *w_far]
+    act_1, gate_1, up_1 = up_project(after(normed_two, *done), gate_up[1], grad_act, 1)
+    terms = [(gate_0, gate_up[0], 0), (up_0, gate_up[0], 1), (gate_1, gate_up[1], 0), (up_1, gate_up[1], 1)]
+    far = sum_of(terms, 3 * rows, rows)
+
+    done = (far, *w_far)
+    g_far = send_far(after(far, *done))
+    near = sum_of([(after(gate_0, *done), *terms[0][1:])] + terms[1:], rows, 2 * rows)
+
+    for_x, for_y = add_far(near[:rows], near[rows:], *g_far)
+    g_x, g_y = swap(for_x, 1), swap(for_y, 2)
+    own = sum_of([(after(gate_0, for_x, for_y), *terms[0][1:])] + terms[1:], 0, rows)
+    grad_1 = outer(after(normed_two, own), [gate_1, up_1], 1024)
+
+    grad_middle, grad_attn, grad_heads = turn_back(
+        [after(own, grad_1), g_x, g_y], tokens_low, attn_branch, cot_low, valid_col, gain_two, out_pieces
+    )
+
+    head_grads = [grad_heads] + [swap(grad_heads[k], k) for k in range(1, count)]
+    grad_down = outer(after(grad_mlp, grad_attn), [act_0, act_1], 1024)
+
+    gate_up_1 = scatter_fsdp(after(grad_1, grad_attn))
+    down_sum = scatter_fsdp(after(grad_down, *head_grads[1:]))
+
+    def attention_back(queries, group):
+        return attend_back_one(
+            me_row, queries, k, v, heads[group], head_grads, totals[group], query_row, key_col, tables, rows, group
+        )
+
+    done = (*head_grads[1:], grad_down)
+    a_own = after(grad_attn, *done)
+    a_x, a_y = to_both(a_own)
+    dqkv_0 = attention_back(after(q, *done), 0)
+
+    done = (a_x, a_y, dqkv_0)
+    a_far = pass_on(a_x, a_y, *done)
+    parts_0 = exchange_seq(blocks_of(after(dqkv_0, *done), count))
+    dqkv_1 = attention_back(after(q, *done), 1)
+
+    done = (*a_far, *parts_0[1:], dqkv_1)
+    parts_1 = exchange_seq(blocks_of(after(dqkv_1, *done), count))
+    p_own = after(gate_up_0, *done)
+    p_x, p_y = to_both(p_own)
+    total = kv_local * step + q_width
+    grad_attn_all = join([after(a_own, *done), a_x, a_y, *a_far])
+    grad_weights = outer(after(normed_one, *done), [dqkv_0, dqkv_1], step, total)
+    grad_weights = outer(
+        grad_attn_all, heads, GROUP * HEAD_DIM, total, kv_local * step, (grad_weights,)
+    )
+
+    done = (*parts_1[1:], p_x, p_y, grad_weights)
+    attn_sum = scatter_fsdp(after(grad_weights, *done))
+    p_far = pass_on(p_x, p_y, *done)
+    p_pieces = [p_own, p_x, p_y, *p_far]
+    p_own = after(gate_up_1, *done)
+    p_x, p_y = to_both(p_own)
+    mlp_part = sum_of([(after(act_0, *done), down_t, 0), (act_1, down_t, 1)], 0, length)
+
+    done = (*p_far, p_x, p_y, mlp_part)
+    mlp_blocks = blocks_of(after(mlp_part, *done), count)
+    m_far = send_far(mlp_blocks[3])
+    p_far = pass_on(p_x, p_y, *done)
+    input_grad = finish(after(tokens_low, *done), grad_middle, gain_one, [parts_0, parts_1], weight_pieces)
+    placed = place_pair(
+        me_row, [after(p_pieces[0], input_grad)] + p_pieces[1:], gate_weight, up_weight, CHUNKS, 0, None
+    )
+    input_grad = input_grad[None]
+
+    done = (*m_far, *p_far, placed[2])
+    m_x, m_y = add_far(mlp_blocks[1], mlp_blocks[2], *m_far)
+    m_x, m_y = swap(after(m_x, *done), 1), swap(m_y, 2)
+    gate_grad, up_grad, gate_up_dot = place_pair(
+        me_row, [after(p_own, *done), p_x, p_y, *p_far], gate_weight, up_weight, CHUNKS, 1, placed
+    )
+
+    done = (m_x, m_y, gate_up_dot)
+    d_x, d_y = to_both(after(down_sum, *done))
+    mlp_branch = mlp_blocks[0].astype(F32) + m_x.astype(F32) + m_y.astype(F32)
+    tokens = after(tokens_low, *done).astype(F32)
+    middle = tokens + attn_branch
+    final = middle + mlp_branch
+    outputs = final.astype(BF)[None]
+
+    done = (d_x, d_y, outputs)
+    d_far = pass_on(d_x, d_y, *done)
+    t_x, t_y = to_both(after(attn_sum, *d_far))
+    down_grad = place_rows(me_row, [down_sum, d_x, d_y, *d_far], 512)
+    query_grad, key_grad, value_grad, out_grad, qkv_dot = place_attn(
+        me_row, [attn_sum, t_x, t_y, *pass_on(t_x, t_y, down_grad)], query_weight, key_weight, value_weight, kv_local
+    )
+    attn_gain_grad = jnp.sum(qkv_dot, axis=1) / attn_gain.astype(F32)
+    mlp_gain_grad = jnp.sum(gate_up_dot, axis=1) / mlp_gain.astype(F32)
+
+    squares = [jnp.sum(valid_col * part * part) for part in (tokens, middle, final, attn_branch, mlp_branch)]
+    stats = jnp.stack([jnp.sum(valid_col)] + squares)
+    stats = jnp.broadcast_to(jnp.pad(stats, (0, LANES - 6))[None, :], (8, LANES))
+    for bit in bit_orders()[0]:
+        stats = stats + swap(stats, bit)
+    rms_stats = jnp.sqrt(stats[:1, 1:6] / (stats[:1, :1] * D))
+    return (
+        outputs, input_grad, query_grad, key_grad, value_grad, out_grad, gate_grad, up_grad, down_grad,
+        attn_gain_grad, mlp_gain_grad, rms_stats,
+    )
+
+
 def solution(mesh):
     rows_in = P("fsdp", None)
     columns_in = P(None, "fsdp")
@@ -530,7 +1317,7 @@
         rows_in, rows_in, rows_in, columns_in, rows_in, rows_in, columns_in, P("fsdp"), P("fsdp"),
     )
     return jax.shard_map(
-        body,
+        square_body if mesh.shape["seq"] == 4 else general_body,
         mesh=mesh,
         in_specs=placed,
         out_specs=(

time: 1460 us -> 902 us (0.62)
  Pallas kernels: 150 us -> 539 us
  matrix products: 367 us -> 0 us
  waiting for transfers between devices: 540 us -> 174 us
  other arithmetic: 185 us -> 33.6 us
  local copies, waits for them, and re-layouts: 131 us -> 64 us
    pallas_call x3 -> x32, Pallas kernels: 150 us -> 539 us  [call(): pl.pallas_call(kernel, grid_spec=pltpu.PrefetchScalarGridSpec(num_scalar_...]
    dot_general x15 -> x0, matrix products: 367 us -> none  [dot(): return lax.dot_general(left, right, dims, preferred_element_type=F32)]
    ppermute x58 -> x66, waiting for transfers between devices: 540 us -> 174 us  [swap(): return lax.ppermute(values, 'seq', [(i, i ^ bit) for i in range(count)])]
    concatenate x28 -> x4, other arithmetic: 60.8 us -> 4.84 us  [the longest x2 3.14 us: add_far(): jnp.concatenate([add_low(for_y[:half], low), for_y[half:]], axis=0)]
    convert_element_type x6, other arithmetic: 62.2 us -> 9.2 us  [the longest x2 5.1 us: add_low(): return (a.astype(F32) + b.astype(F32)).astype(BF)]
    unnamed x175 -> x97, local copies, waits for them, and re-layouts: 45.7 us -> 7.79 us
    slice x2 -> x27, local copies, waits for them, and re-layouts: 2.19 us -> 39 us  [the longest x11 14.2 us: pass_on(): by_x[half:]]
    squeeze x25 -> x1, local copies, waits for them, and re-layouts: 30.4 us -> 0.89 us  [square_body(): grad_heads[k]]
  transfers between devices with their start and end apart: 66 -> 75, of which waited for: 31 -> 22; matrix products, arithmetic and copies ran while one was open for 37% -> 10% of each run, Pallas kernels for 10% -> 60%
where the time goes in v2:
time: 902 us; the launch traced here: 894 us
  Pallas kernels  539 us (60%)
  waiting for transfers between devices  174 us (19%)
  starting transfers between devices  66.9 us (7%)
  local copies, waits for them, and re-layouts  64 us (7%)
  other arithmetic  33.6 us (4%)
  between operations  15.5 us (2%)
    pallas_call x32, Pallas kernels, call(): pl.pallas_call(kernel, grid_spec=pltpu.PrefetchScalarGridSpec(num_scalar_...  539 us
    ppermute x66, waiting for transfers between devices, swap(): return lax.ppermute(values, 'seq', [(i, i ^ bit) for i in range(count)])  174 us
    ppermute x66, starting transfers between devices, swap(): return lax.ppermute(values, 'seq', [(i, i ^ bit) for i in range(count)])  66.4 us
  transfers between devices with their start and end apart: 75, of which 22 were waited for; matrix products, arithmetic and copies ran while one was open for 10% of the time, Pallas kernels for 60%

profile of v2, /device:TPU:0, one launch (start us, length us, event | category | flops | bytes accessed | tf_op | source)
XLA Modules:
  0.0 893.8 jit_solution(6815075472514911799)
XLA Ops:
  32.2 36.0 %collective-permute-done.5.refs_1_ = bf16[512,2048]{1,0:T(8,128)(2,1)} collective-permute-done((bf16[512,2048]{1,0:T(8,128)(2,1)S(1)}, bf16[512,2048]{1,0:T(8,128)(2,1)}, u32[]{:S(2)}, u32[]{:S(2)}) %collective-permute-start.5) | collective-permute-done | bytes 2097184 | tf_op jit(solution)/shard_map/ppermute | solution.py:41
  88.9 15.4 %enter.2 = (bf16[2048,2048]{1,0:T(8,128)(2,1)}, bf16[2048,2048]{1,0:T(8,128)(2,1)}, bf16[2048,512]{1,0:T(8,128)(2,1)}, bf16[2,2048,64]{2,1,0:T(8,128)(2,1)}, bf16[2,2048,64]{2,1,0:T(8,128)(2,1)}) custom-call(bf16[512,2048]{1,0:T(8,128)(2,1)} %bitcast.37, bf16[512,2048]{1,0:T(8,128)(2,1)} %collective-permute-done.5.refs_1_, ...), custom_call_target="tpu_custom_call" | custom-call | flops 5637144576 | bytes 25165824 | tf_op jit(solution)/shard_map/enter/pallas_call | solution.py:559
  115.6 30.2 %attend.2 = (bf16[2048,256]{1,0:T(8,128)(2,1)}, f32[1,4,2048]{2,1,0:T(4,128)}) custom-call(s32[1]{0:T(128)} %bitcast.8.me_ref, bf16[2048,512]{1,0:T(8,128)(2,1)} %get-tuple-element.174.q_ref.refs_0_, bf16[2,2048,64]{2,1,0:T(8,128)(2,1)} %get-tuple-element.126.k_ref.refs_1_, bf16[2,2048,64]{2,1,0:T(8,128)(2,1)} %get-tuple-element.127.v_ref.refs_2_, ...), custom_call_target="tpu_custom_call" | custom-call | flops 25999998976 | bytes 4194304 | tf_op jit(solution)/shard_map/attend/pallas_call | solution.py:559
  157.2 30.2 %attend.3 = (bf16[2048,256]{1,0:T(8,128)(2,1)}, f32[1,4,2048]{2,1,0:T(4,128)}) custom-call(s32[1]{0:T(128)} %bitcast.8.me_ref, bf16[2048,512]{1,0:T(8,128)(2,1)} %get-tuple-element.174.q_ref.refs_0_, bf16[2,2048,64]{2,1,0:T(8,128)(2,1)} %get-tuple-element.126.k_ref.refs_1_, bf16[2,2048,64]{2,1,0:T(8,128)(2,1)} %get-tuple-element.127.v_ref.refs_2_, ...), custom_call_target="tpu_custom_call" | custom-call | flops 25999998976 | bytes 4194304 | tf_op jit(solution)/shard_map/attend/pallas_call | solution.py:559
  205.9 16.9 %collective-permute-done.16.refs_6_ = bf16[2048,256]{1,0:T(8,128)(2,1)S(1)} collective-permute-done((bf16[2048,256]{1,0:T(8,128)(2,1)}, bf16[2048,256]{1,0:T(8,128)(2,1)S(1)}, u32[]{:S(2)}, u32[]{:S(2)}) %collective-permute-start.16) | collective-permute-done | bytes 1048608 | tf_op jit(solution)/shard_map/ppermute | solution.py:41
  249.4 29.2 %leave.1 = (bf16[2048,2048]{1,0:T(8,128)(2,1)}, f32[512,2048]{1,0:T(8,128)}) custom-call(bf16[2048,2048]{1,0:T(8,128)(2,1)} %get-tuple-element.140.x_ref, f32[1,2048]{1,0:T(1,128)} %bitcast.51, bf16[2048,256]{1,0:T(8,128)(2,1)} %get-tuple-element.133.refs_0_.refs_3_, bf16[2048,256]{1,0:T(8,128)(2,1)} %collective-permute-done.11.refs_1_, ...), custom_call_target="tpu_custom_call" | custom-call | flops 17179869184 | bytes 33554432 | tf_op jit(solution)/shard_map/leave/pallas_call | solution.py:559
  295.0 20.1 %act_back.2 = (bf16[2048,2048]{1,0:T(8,128)(2,1)}, bf16[2048,2048]{1,0:T(8,128)(2,1)}) custom-call(bf16[512,2048]{1,0:T(8,128)(2,1)} %multiply_convert_fusion.refs_0_, bf16[512,2048]{1,0:T(8,128)(2,1)} %copy-done.23, bf16[512,2048]{1,0:T(8,128)(2,1)} %collective-permute-done.19.refs_2_, bf16[2048,2048]{1,0:T(8,128)(2,1)} %all-gather.12.cloned.1.call-done.refs_3_.refs_2_.refs_1_), custom_call_target="tpu_custom_call" | custom-call | flops 12884901888 | bytes 18874368 | tf_op jit(solution)/shard_map/act_back/pallas_call | solution.py:559
  329.4 25.2 %up_project.2 = (bf16[2048,1024]{1,0:T(8,128)(2,1)}, bf16[2048,1024]{1,0:T(8,128)(2,1)}, bf16[2048,1024]{1,0:T(8,128)(2,1)}) custom-call(bf16[2048,2048]{1,0:T(8,128)(2,1)} %get-tuple-element.163.normed_ref.left_ref, bf16[2048,2048]{1,0:T(8,128)(2,1)} %all-gather.10.cloned.1.call-done.gate_ref.up_ref.refs_1_.refs_3_, ...), custom_call_target="tpu_custom_call" | custom-call | flops 17179869184 | bytes 41943040 | tf_op jit(solution)/shard_map/up_project/pallas_call | solution.py:559
  354.6 24.3 %outer.5 = bf16[2048,2048]{1,0:T(8,128)(2,1)} custom-call(bf16[2048,2048]{1,0:T(8,128)(2,1)} %get-tuple-element.163.normed_ref.left_ref, bf16[2048,1024]{1,0:T(8,128)(2,1)} %get-tuple-element.162.refs_0_, bf16[2048,1024]{1,0:T(8,128)(2,1)} %get-tuple-element.153.refs_1_.refs_2_), custom_call_target="tpu_custom_call" | custom-call | flops 17179869184 | bytes 33554432 | tf_op jit(solution)/shard_map/outer/pallas_call | solution.py:559
  385.8 25.5 %up_project.3 = (bf16[2048,1024]{1,0:T(8,128)(2,1)}, bf16[2048,1024]{1,0:T(8,128)(2,1)}, bf16[2048,1024]{1,0:T(8,128)(2,1)}) custom-call(bf16[2048,2048]{1,0:T(8,128)(2,1)} %get-tuple-element.163.normed_ref.left_ref, bf16[2048,2048]{1,0:T(8,128)(2,1)} %all-gather.14.cloned.1.call-done.gate_ref.up_ref.refs_5_.refs_7_, ...), custom_call_target="tpu_custom_call" | custom-call | flops 17179869184 | bytes 41943040 | tf_op jit(solution)/shard_map/up_project/pallas_call | solution.py:559
  411.4 14.2 %sum_of.4 = bf16[512,2048]{1,0:T(8,128)(2,1)} custom-call(bf16[2048,1024]{1,0:T(8,128)(2,1)} %get-tuple-element.162.refs_0_, bf16[2048,2048]{1,0:T(8,128)(2,1)} %all-gather.10.cloned.1.call-done.gate_ref.up_ref.refs_1_.refs_3_, bf16[2048,1024]{1,0:T(8,128)(2,1)} %get-tuple-element.153.refs_1_.refs_2_, ...), custom_call_target="tpu_custom_call" | custom-call | flops 8589934592 | bytes 23068672 | tf_op jit(solution)/shard_map/sum_of/pallas_call | solution.py:559
  433.2 25.0 %sum_of.5 = bf16[1024,2048]{1,0:T(8,128)(2,1)} custom-call(bf16[2048,1024]{1,0:T(8,128)(2,1)} %get-tuple-element.162.refs_0_, bf16[2048,2048]{1,0:T(8,128)(2,1)} %all-gather.10.cloned.1.call-done.gate_ref.up_ref.refs_1_.refs_3_, bf16[2048,1024]{1,0:T(8,128)(2,1)} %get-tuple-element.153.refs_1_.refs_2_, ...), custom_call_target="tpu_custom_call" | custom-call | flops 17179869184 | bytes 29360128 | tf_op jit(solution)/shard_map/sum_of/pallas_call | solution.py:559
  465.9 14.2 %sum_of.6.own_ref = bf16[512,2048]{1,0:T(8,128)(2,1)} custom-call(bf16[2048,1024]{1,0:T(8,128)(2,1)} %get-tuple-element.162.refs_0_, bf16[2048,2048]{1,0:T(8,128)(2,1)} %all-gather.10.cloned.1.call-done.gate_ref.up_ref.refs_1_.refs_3_, bf16[2048,1024]{1,0:T(8,128)(2,1)} %get-tuple-element.153.refs_1_.refs_2_, ...), custom_call_target="tpu_custom_call" | custom-call | flops 8589934592 | bytes 23068672 | tf_op jit(solution)/shard_map/sum_of/pallas_call | solution.py:559
  480.1 24.5 %outer.6 = bf16[2048,2048]{1,0:T(8,128)(2,1)} custom-call(bf16[2048,2048]{1,0:T(8,128)(2,1)} %get-tuple-element.163.normed_ref.left_ref, bf16[2048,1024]{1,0:T(8,128)(2,1)} %get-tuple-element.156.refs_4_.refs_0_, bf16[2048,1024]{1,0:T(8,128)(2,1)} %get-tuple-element.157.refs_6_.refs_1_), custom_call_target="tpu_custom_call" | custom-call | flops 17179869184 | bytes 33554432 | tf_op jit(solution)/shard_map/outer/pallas_call | solution.py:559
  504.6 14.5 %turn_back.1 = (f32[512,2048]{1,0:T(8,128)}, bf16[512,2048]{1,0:T(8,128)(2,1)}, bf16[4,512,512]{2,1,0:T(8,128)(2,1)}) custom-call(bf16[512,2048]{1,0:T(8,128)(2,1)} %sum_of.6.own_ref, bf16[512,2048]{1,0:T(8,128)(2,1)} %collective-permute-done.29.by_x_ref, bf16[512,2048]{1,0:T(8,128)(2,1)} %collective-permute-done.30.by_y_ref, bf16[512,2048]{1,0:T(8,128)(2,1)} %bitcast.38, ...), custom_call_target="tpu_custom_call" | custom-call | flops 4294967296 | bytes 20971520 | tf_op jit(solution)/shard_map/turn_back/pallas_call | solution.py:559
  525.1 25.0 %outer.7 = bf16[2048,2048]{1,0:T(8,128)(2,1)} custom-call(bf16[2048,2048]{1,0:T(8,128)(2,1)} %get-tuple-element.169.left_ref, bf16[2048,1024]{1,0:T(8,128)(2,1)} %get-tuple-element.185.refs_0_, bf16[2048,1024]{1,0:T(8,128)(2,1)} %get-tuple-element.170.refs_1_.refs_2_), custom_call_target="tpu_custom_call" | custom-call | flops 17179869184 | bytes 33554432 | tf_op jit(solution)/shard_map/outer/pallas_call | solution.py:559
  556.9 40.0 %attend_back.2.refs_0_ = bf16[2048,384]{1,0:T(8,128)(2,1)} custom-call(s32[1]{0:T(128)} %bitcast.8.me_ref, bf16[2048,512]{1,0:T(8,128)(2,1)} %get-tuple-element.174.q_ref.refs_0_, bf16[2,2048,64]{2,1,0:T(8,128)(2,1)} %get-tuple-element.126.k_ref.refs_1_, bf16[2,2048,64]{2,1,0:T(8,128)(2,1)} %get-tuple-element.127.v_ref.refs_2_, ...), custom_call_target="tpu_custom_call" | custom-call | flops 33999998976 | bytes 4194304 | tf_op jit(solution)/shard_map/attend_back/pallas_call | solution.py:559
  606.1 40.0 %attend_back.3.refs_1_ = bf16[2048,384]{1,0:T(8,128)(2,1)} custom-call(s32[1]{0:T(128)} %bitcast.8.me_ref, bf16[2048,512]{1,0:T(8,128)(2,1)} %get-tuple-element.174.q_ref.refs_0_, bf16[2,2048,64]{2,1,0:T(8,128)(2,1)} %get-tuple-element.126.k_ref.refs_1_, bf16[2,2048,64]{2,1,0:T(8,128)(2,1)} %get-tuple-element.127.v_ref.refs_2_, ...), custom_call_target="tpu_custom_call" | custom-call | flops 33999998976 | bytes 4194304 | tf_op jit(solution)/shard_map/attend_back/pallas_call | solution.py:559
  665.5 14.0 %outer.8.refs_2_ = bf16[2048,1280]{1,0:T(8,128)(2,1)} custom-call(bf16[2048,2048]{1,0:T(8,128)(2,1)} %get-tuple-element.184.left_ref, bf16[2048,384]{1,0:T(8,128)(2,1)} %attend_back.2.refs_0_, bf16[2048,384]{1,0:T(8,128)(2,1)} %attend_back.3.refs_1_), custom_call_target="tpu_custom_call" | custom-call | flops 6442450944 | bytes 23068672 | tf_op jit(solution)/shard_map/outer/pallas_call | solution.py:559
  695.9 29.7 %sum_of.7 = bf16[2048,2048]{1,0:T(8,128)(2,1)} custom-call(bf16[2048,1024]{1,0:T(8,128)(2,1)} %get-tuple-element.185.refs_0_, bf16[2048,2048]{1,0:T(8,128)(2,1)} %all-gather.12.cloned.1.call-done.refs_3_.refs_2_.refs_1_, bf16[2048,1024]{1,0:T(8,128)(2,1)} %get-tuple-element.170.refs_1_.refs_2_, ...), custom_call_target="tpu_custom_call" | custom-call | flops 17179869184 | bytes 25165824 | tf_op jit(solution)/shard_map/sum_of/pallas_call | solution.py:559
  730.5 15.8 %finish.1 = bf16[512,2048]{1,0:T(8,128)(2,1)} custom-call(bf16[512,2048]{1,0:T(8,128)(2,1)} %bitcast.39, f32[512,2048]{1,0:T(8,128)} %get-tuple-element.194.middle_ref, f32[1,2048]{1,0:T(1,128)} %bitcast.50, bf16[512,384]{1,0:T(8,128)(2,1)} %get-tuple-element.245.refs_0_, bf16[512,384]{1,0:T(8,128)(2,1)} %collective-permute-done.38.refs_1_, ...), custom_call_target="tpu_custom_call" | custom-call | flops 6442450944 | bytes 20971520 | tf_op jit(solution)/shard_map/finish/pallas_call | solution.py:559
  776.7 32.4 %collective-permute-done.55 = bf16[512,2048]{1,0:T(8,128)(2,1)} collective-permute-done((bf16[512,2048]{1,0:T(8,128)(2,1)}, bf16[512,2048]{1,0:T(8,128)(2,1)}, u32[]{:S(2)}, u32[]{:S(2)}) %collective-permute-start.55) | collective-permute-done | bytes 2097184 | tf_op jit(solution)/shard_map/ppermute | solution.py:41
  819.9 13.5 %collective-permute-done.57.refs_1_ = bf16[256,2048]{1,0:T(8,128)(2,1)S(1)} collective-permute-done((bf16[256,2048]{1,0:T(8,128)(2,1)}, bf16[256,2048]{1,0:T(8,128)(2,1)S(1)}, u32[]{:S(2)}, u32[]{:S(2)}) %collective-permute-start.57) | collective-permute-done | bytes 1048608 | tf_op jit(solution)/shard_map/ppermute | solution.py:41
  858.1 12.1 %place_rows.1 = f32[8192,256]{1,0:T(8,128)} custom-call(s32[1]{0:T(128)} %bitcast.8.me_ref, bf16[256,2048]{1,0:T(8,128)(2,1)} %reduce-scatter.11.cloned.1.call-done.refs_0_, bf16[256,2048]{1,0:T(8,128)(2,1)} %copy-done.10, bf16[256,2048]{1,0:T(8,128)(2,1)} %copy-done.11, bf16[128,2048]{1,0:T(8,128)(2,1)} %copy-done.22, ...), custom_call_target="tpu_custom_call" | custom-call | bytes 12582912 | tf_op jit(solution)/shard_map/place_rows/pallas_call | solution.py:559
  (341 shorter events, 310.5 us)
Async XLA Ops:
  7.2 79.3 %all-gather.6.cloned.1.call-start = ((), (), s32[]{:S(2)}) async-start(), calls=%async_computation.4 | async-start | bytes 4128768 | tf_op jit(solution)/shard_map/all_gather | solution.py:91
  11.4 93.0 %all-gather.8.cloned.1.call-start = ((), (), s32[]{:S(2)}) async-start(), calls=%async_computation.5 | async-start | bytes 2359296 | tf_op jit(solution)/shard_map/all_gather | solution.py:91
  13.3 280.0 %all-gather.12.cloned.1.call-start = ((), (), s32[]{:S(2)}) async-start(), calls=%async_computation.7 | async-start | bytes 9437184 | tf_op jit(solution)/shard_map/all_gather | solution.py:91
  22.4 45.8 %collective-permute-start.5 = (bf16[512,2048]{1,0:T(8,128)(2,1)S(1)}, bf16[512,2048]{1,0:T(8,128)(2,1)}, u32[]{:S(2)}, u32[]{:S(2)}) collective-permute-start(bf16[512,2048]{1,0:T(8,128)(2,1)S(1)} %bitcast.40), channel_id=1, source_target_pairs={{0,1},{1,0},{2,3},{3,2},{4,5},{5,4},{6,7},{7,6},{8,9},{9,8},{10,11... | collective-permute-start | bytes 6291464 | tf_op jit(solution)/shard_map/ppermute | solution.py:41
  23.0 45.5 %collective-permute-start.3 = (bf16[512,2048]{1,0:T(8,128)(2,1)S(1)}, bf16[512,2048]{1,0:T(8,128)(2,1)}, u32[]{:S(2)}, u32[]{:S(2)}) collective-permute-start(bf16[512,2048]{1,0:T(8,128)(2,1)S(1)} %bitcast.41), channel_id=1, source_target_pairs={{0,2},{1,3},{2,0},{3,1},{4,6},{5,7},{6,4},{7,5},{8,10},{9,11},{10,... | collective-permute-start | bytes 6291464 | tf_op jit(solution)/shard_map/ppermute | solution.py:41
  72.3 257.1 %all-gather.10.cloned.1.call-start = ((), (), s32[]{:S(2)}) async-start(), calls=%async_computation.6 | async-start | bytes 9437184 | tf_op jit(solution)/shard_map/all_gather | solution.py:91
  74.6 311.3 %all-gather.14.cloned.1.call-start = ((), (), s32[]{:S(2)}) async-start(), calls=%async_computation.8 | async-start | bytes 9437184 | tf_op jit(solution)/shard_map/all_gather | solution.py:91
  76.9 570.2 %reduce-scatter.5.cloned.1.call-start = ((), (), s32[]{:S(2)}) async-start(), calls=%async_computation.9 | async-start | bytes 9437184 | tf_op jit(solution)/shard_map/reduce_scatter | solution.py:95
  104.4 45.1 %collective-permute-start.8 = (bf16[2048,512]{1,0:T(8,128)(2,1)}, bf16[2048,512]{1,0:T(8,128)(2,1)S(1)}, u32[]{:S(2)}, u32[]{:S(2)}) collective-permute-start(bf16[2048,512]{1,0:T(8,128)(2,1)} %all-gather.8.cloned.1.call-done.refs_10_.refs_0_), channel_id=1, source_target_pairs={{0,2},{1,3},{2,0},{3,1},{4,6},{5,7},{6,4},{7,5},{8,10},{9,11},{10,... | collective-permute-start | bytes 6291464 | tf_op jit(solution)/shard_map/ppermute | solution.py:41
  106.1 44.7 %collective-permute-start.7 = (bf16[2048,512]{1,0:T(8,128)(2,1)}, bf16[2048,512]{1,0:T(8,128)(2,1)}, u32[]{:S(2)}, u32[]{:S(2)}) collective-permute-start(bf16[2048,512]{1,0:T(8,128)(2,1)} %all-gather.8.cloned.1.call-done.refs_10_.refs_0_), channel_id=1, source_target_pairs={{0,1},{1,0},{2,3},{3,2},{4,5},{5,4},{6,7},{7,6},{8,9},{9,8},{10,11... | collective-permute-start | bytes 6291464 | tf_op jit(solution)/shard_map/ppermute | solution.py:41
  150.8 47.0 %collective-permute-start.12 = (bf16[2048,256]{1,0:T(8,128)(2,1)}, bf16[2048,256]{1,0:T(8,128)(2,1)}, u32[]{:S(2)}, u32[]{:S(2)}) collective-permute-start(bf16[2048,256]{1,0:T(8,128)(2,1)} %get-tuple-element.133.refs_0_.refs_3_), channel_id=1, source_target_pairs={{0,2},{1,3},{2,0},{3,1},{4,6},{5,7},{6,4},{7,5},{8,10},{9,11},{10,... | collective-permute-start | bytes 3145736 | tf_op jit(solution)/shard_map/ppermute | solution.py:41
  152.1 45.7 %collective-permute-start.11 = (bf16[2048,256]{1,0:T(8,128)(2,1)}, bf16[2048,256]{1,0:T(8,128)(2,1)}, u32[]{:S(2)}, u32[]{:S(2)}) collective-permute-start(bf16[2048,256]{1,0:T(8,128)(2,1)} %get-tuple-element.133.refs_0_.refs_3_), channel_id=1, source_target_pairs={{0,1},{1,0},{2,3},{3,2},{4,5},{5,4},{6,7},{7,6},{8,9},{9,8},{10,11... | collective-permute-start | bytes 3145736 | tf_op jit(solution)/shard_map/ppermute | solution.py:41
  317.0 63.0 %collective-permute-start.24 = (bf16[2048,768]{1,0:T(8,128)(2,1)}, bf16[2048,768]{1,0:T(8,128)(2,1)S(1)}, u32[]{:S(2)}, u32[]{:S(2)}) collective-permute-start(bf16[2048,768]{1,0:T(8,128)(2,1)} %slice.188.refs_8_), channel_id=1, source_target_pairs={{0,2},{1,3},{2,0},{3,1},{4,6},{5,7},{6,4},{7,5},{8,10},{9,11},{10,... | collective-permute-start | bytes 9437192 | tf_op jit(solution)/shard_map/ppermute | solution.py:41
  318.5 61.6 %collective-permute-start.23 = (bf16[2048,768]{1,0:T(8,128)(2,1)}, bf16[2048,768]{1,0:T(8,128)(2,1)}, u32[]{:S(2)}, u32[]{:S(2)}) collective-permute-start(bf16[2048,768]{1,0:T(8,128)(2,1)} %slice.188.refs_8_), channel_id=1, source_target_pairs={{0,1},{1,0},{2,3},{3,2},{4,5},{5,4},{6,7},{7,6},{8,9},{9,8},{10,11... | collective-permute-start | bytes 9437192 | tf_op jit(solution)/shard_map/ppermute | solution.py:41
  380.1 312.5 %reduce-scatter.7.cloned.1.call-start = ((), (), s32[]{:S(2)}) async-start(), calls=%async_computation.10 | async-start | bytes 9437184 | tf_op jit(solution)/shard_map/reduce_scatter | solution.py:95
  519.1 257.6 %reduce-scatter.11.cloned.1.call-start = ((), (), s32[]{:S(2)}) async-start(), calls=%async_computation.12 | async-start | bytes 9437184 | tf_op jit(solution)/shard_map/reduce_scatter | solution.py:95
  551.2 295.0 %reduce-scatter.9.cloned.1.call-start = ((), (), s32[]{:S(2)}) async-start(), calls=%async_computation.11 | async-start | bytes 5898240 | tf_op jit(solution)/shard_map/reduce_scatter | solution.py:95
  553.6 43.3 %collective-permute-start.35 = (bf16[512,2048]{1,0:T(8,128)(2,1)}, bf16[512,2048]{1,0:T(8,128)(2,1)S(1)}, u32[]{:S(2)}, u32[]{:S(2)}) collective-permute-start(bf16[512,2048]{1,0:T(8,128)(2,1)} %get-tuple-element.182.refs_0_), channel_id=1, source_target_pairs={{0,2},{1,3},{2,0},{3,1},{4,6},{5,7},{6,4},{7,5},{8,10},{9,11},{10,... | collective-permute-start | bytes 6291464 | tf_op jit(solution)/shard_map/ppermute | solution.py:41
  600.8 45.3 %collective-permute-start.37 = (bf16[256,2048]{1,0:T(8,128)(2,1)}, bf16[256,2048]{1,0:T(8,128)(2,1)S(1)}, u32[]{:S(2)}, u32[]{:S(2)}) collective-permute-start(bf16[256,2048]{1,0:T(8,128)(2,1)} %slice.248), channel_id=1, source_target_pairs={{0,2},{1,3},{2,0},{3,1},{4,6},{5,7},{6,4},{7,5},{8,10},{9,11},{10,... | collective-permute-start | bytes 3145736 | tf_op jit(solution)/shard_map/ppermute | solution.py:41
  601.5 44.7 %collective-permute-start.36 = (bf16[256,2048]{1,0:T(8,128)(2,1)}, bf16[256,2048]{1,0:T(8,128)(2,1)}, u32[]{:S(2)}, u32[]{:S(2)}) collective-permute-start(bf16[256,2048]{1,0:T(8,128)(2,1)} %slice.247), channel_id=1, source_target_pairs={{0,1},{1,0},{2,3},{3,2},{4,5},{5,4},{6,7},{7,6},{8,9},{9,8},{10,11... | collective-permute-start | bytes 3145736 | tf_op jit(solution)/shard_map/ppermute | solution.py:41
  602.6 43.5 %collective-permute-start.40 = (bf16[512,384]{1,0:T(8,128)(2,1)}, bf16[512,384]{1,0:T(8,128)(2,1)}, u32[]{:S(2)}, u32[]{:S(2)}) collective-permute-start(bf16[512,384]{1,0:T(8,128)(2,1)} %get-tuple-element.246), channel_id=1, source_target_pairs={{0,3},{1,2},{2,1},{3,0},{4,7},{5,6},{6,5},{7,4},{8,11},{9,10},{10,... | collective-permute-start | bytes 1179656 | tf_op jit(solution)/shard_map/ppermute | solution.py:41
  647.1 42.9 %collective-permute-start.45 = (bf16[256,2048]{1,0:T(8,128)(2,1)}, bf16[256,2048]{1,0:T(8,128)(2,1)S(1)}, u32[]{:S(2)}, u32[]{:S(2)}) collective-permute-start(bf16[256,2048]{1,0:T(8,128)(2,1)} %reduce-scatter.5.cloned.1.call-done.refs_0_), channel_id=1, source_target_pairs={{0,2},{1,3},{2,0},{3,1},{4,6},{5,7},{6,4},{7,5},{8,10},{9,11},{10,... | collective-permute-start | bytes 3145736 | tf_op jit(solution)/shard_map/ppermute | solution.py:41
  766.0 43.1 %collective-permute-start.55 = (bf16[512,2048]{1,0:T(8,128)(2,1)}, bf16[512,2048]{1,0:T(8,128)(2,1)}, u32[]{:S(2)}, u32[]{:S(2)}) collective-permute-start(bf16[512,2048]{1,0:T(8,128)(2,1)} %pad_maximum_fusion.3), channel_id=1, source_target_pairs={{0,2},{1,3},{2,0},{3,1},{4,6},{5,7},{6,4},{7,5},{8,10},{9,11},{10,... | collective-permute-start | bytes 6291464 | tf_op jit(solution)/shard_map/ppermute | solution.py:41
  767.7 43.7 %collective-permute-start.54 = (bf16[512,2048]{1,0:T(8,128)(2,1)}, bf16[512,2048]{1,0:T(8,128)(2,1)}, u32[]{:S(2)}, u32[]{:S(2)}) collective-permute-start(bf16[512,2048]{1,0:T(8,128)(2,1)} %pad_maximum_fusion.2), channel_id=1, source_target_pairs={{0,1},{1,0},{2,3},{3,2},{4,5},{5,4},{6,7},{7,6},{8,9},{9,8},{10,11... | collective-permute-start | bytes 6291464 | tf_op jit(solution)/shard_map/ppermute | solution.py:41
  (99 other events, 2102.6 us)
Sparse Core Ops, SparseCore 0:
  11.6 45.2 all-gather.5
  59.1 27.9 all-gather.7
  88.7 81.5 all-gather.11
  171.7 80.5 all-gather.9
  253.8 80.5 all-gather.13
  380.2 88.9 reduce-scatter.4
  519.2 90.8 reduce-scatter.6
  612.4 87.9 reduce-scatter.10
  702.7 58.2 reduce-scatter.8

commit v3 on v2

--- a/solution.py
+++ b/solution.py
@@ -524,7 +524,6 @@
 
 TILE = 256
 
-
 def after(value, *events):
     return lax.optimization_barrier((value,) + events)[0]
 
@@ -538,21 +537,35 @@
     return swap(after(by_y[:half], *events), 1), swap(after(by_x[half:], *events), 2)
 
 
+def swap_core(values):
+    count = lax.axis_size("fsdp")
+    return lax.ppermute(values, "fsdp", [(i, i ^ 1) for i in range(count)])
+
+
+def core_half(weight, core):
+    half = weight.shape[0] // 2
+    return lax.dynamic_slice_in_dim(weight, core * half, half, 0)
+
+
+def in_order(core, mine, other):
+    return jnp.where(core == 0, jnp.concatenate([mine, other], axis=1), jnp.concatenate([other, mine], axis=1))
+
+
 def add_low(a, b):
     return (a.astype(F32) + b.astype(F32)).astype(BF)
 
 
-def send_far(block):
-    half = block.shape[0] // 2
-    return swap(block[:half], 1), swap(block[half:], 2)
-
-
-def add_far(for_x, for_y, low, high):
-    half = for_x.shape[0] // 2
-    return (
-        jnp.concatenate([for_x[:half], add_low(for_x[half:], high)], axis=0),
-        jnp.concatenate([add_low(for_y[:half], low), for_y[half:]], axis=0),
-    )
+def send_far(low, high):
+    return swap(low, 1), swap(high, 2)
+
+
+def add_far(near, low, high):
+    x_low, x_high, y_low, y_high = near
+    return [x_low, add_low(x_high, high), add_low(y_low, low), y_high]
+
+
+def send_near(near):
+    return [swap(part, bit) for part, bit in zip(near, (1, 1, 2, 2))]
 
 
 def call(kernel, grid, in_specs, out_specs, out_shape, args, name, flops=0, moved=0, scratch=(), prefetch=0, aliases=None):
@@ -567,7 +580,9 @@
         ),
         out_shape=out_shape,
         input_output_aliases=aliases or {},
-        compiler_params=params(len(grid)),
+        compiler_params=pltpu.CompilerParams(
+            dimension_semantics=("arbitrary",) * len(grid), vmem_limit_bytes=VMEM_LIMIT
+        ),
         cost_estimate=pl.CostEstimate(flops=int(flops), bytes_accessed=int(moved), transcendentals=0),
         name=name,
     )(*args)
@@ -605,20 +620,6 @@
             target[...] = ref[...]
 
 
-def join_kernel(spans, *refs):
-    copy_piece(refs[:-1], spans, pl.program_id(0), refs[-1])
-
-
-def join(pieces):
-    specs, spans = piece_specs(pieces, TILE)
-    rows, width = spans[-1][1] * TILE, pieces[0].shape[1]
-    return call(
-        functools.partial(join_kernel, spans), (rows // TILE,), specs,
-        pl.BlockSpec((TILE, width), lambda i: (i, 0)), shape_of((rows, width)), pieces, "join",
-        moved=4 * rows * width,
-    )
-
-
 def act_back_kernel(spans, others, *refs):
     weight_ref = refs[len(spans)]
     whole_ref, out_ref = refs[len(spans) + 1 + others :]
@@ -666,12 +667,17 @@
     out_ref[...] = in_ref[...].astype(F32).T.astype(BF)
 
 
-def pack_rows(me_row, weight, rows):
+def pack_rows(me_row, weight, rows, owners=(0,)):
     tile = 512
     tiles, columns = rows // tile, weight.shape[1]
-    return call(
-        pack_rows_kernel, (tiles,), [pl.BlockSpec((tile, columns), lambda i, me: (me[0] * tiles + i, 0))],
-        pl.BlockSpec((columns, tile), lambda i, me: (0, i)), shape_of((columns, rows)), (me_row, weight),
+
+    def index(i, me):
+        owner = sum(jnp.where(i // tiles == k, owner, 0) for k, owner in enumerate(owners))
+        return ((me[0] ^ owner) * tiles + i % tiles, 0)
+
+    return call(
+        pack_rows_kernel, (tiles * len(owners),), [pl.BlockSpec((tile, columns), index)],
+        pl.BlockSpec((columns, tile), lambda i, me: (0, i)), shape_of((columns, rows * len(owners))), (me_row, weight),
         "pack_rows", moved=4 * rows * columns, prefetch=1,
     )
 
@@ -734,12 +740,64 @@
     )
 
 
+def allowed_bias(rows, size, first, query_row, key_col, diagonal):
+    allowed = key_col == query_row
+    if diagonal:
+        key_pos = lax.broadcasted_iota(jnp.int32, (size, rows - first), 0)
+        query_pos = lax.broadcasted_iota(jnp.int32, (size, rows - first), 1)
+        allowed = (allowed & (key_pos <= query_pos)) | (key_pos == query_pos)
+    return jnp.where(allowed, 0.0, NEGATIVE)
+
+
+def attend_one_kernel(rows, me_ref, q_ref, k_ref, v_ref, query_row_ref, key_col_ref, out_ref, total_ref, v_t, peak, total, acc):
+    index = pl.program_id(1)
+    me = me_ref[0]
+    half = rows // 2
+
+    @pl.when(index == 0)
+    def _():
+        v_t[...] = v_ref[0].astype(F32).T.astype(BF)
+
+    peak[...] = jnp.full(peak.shape, NEGATIVE, F32)
+    total[...] = jnp.zeros(total.shape, F32)
+    acc[...] = jnp.zeros(acc.shape, F32)
+
+    def visit(at, size, first, diagonal):
+        keys = k_ref[0, pl.ds(at, size), :]
+        values_t = v_t[:, pl.ds(at, size)]
+        bias = allowed_bias(rows, size, first, query_row_ref[:, first:], key_col_ref[pl.ds(at, size), :], diagonal)
+        for head in range(GROUP):
+            query = q_ref[first:, head * HEAD_DIM : (head + 1) * HEAD_DIM]
+            scores = dot(keys, query, NT) + bias
+            old = peak[head : head + 1, first:]
+            new = jnp.maximum(old, jnp.max(scores, axis=0, keepdims=True))
+            expo = jnp.exp(scores - new)
+            fade = jnp.exp(old - new)
+            peak[head : head + 1, first:] = new
+            total[head : head + 1, first:] = total[head : head + 1, first:] * fade + jnp.sum(expo, axis=0, keepdims=True)
+            acc[head, :, first:] = acc[head, :, first:] * fade + dot(values_t, expo.astype(BF))
+
+    here = pl.multiple_of((index ^ me) * rows, rows)
+    visit(here, half, 0, True)
+    visit(pl.multiple_of(here + half, half), half, half, True)
+
+    def step(j, _):
+        visit(pl.multiple_of((j ^ me) * rows, rows), rows, 0, False)
+        return 0
+
+    lax.fori_loop(0, index, step, 0)
+    for head in range(GROUP):
+        out = acc[head] / total[head : head + 1, :]
+        out_ref[:, head * HEAD_DIM : (head + 1) * HEAD_DIM] = out.T.astype(BF)
+    total_ref[0] = peak[...] + jnp.log(total[...])
+
+
 def attend_one(me_row, q, k, v, query_row, key_col, rows, group):
     length = k.shape[1]
     width = GROUP * HEAD_DIM
     head = pl.BlockSpec((1, length, HEAD_DIM), lambda g, i, me: (group, 0, 0))
     return call(
-        functools.partial(attend_kernel, rows), (1, length // rows),
+        functools.partial(attend_one_kernel, rows), (1, length // rows),
         [
             pl.BlockSpec((rows, width), lambda g, i, me: (i ^ me[0], group)),
             head,
@@ -762,18 +820,24 @@
     )
 
 
-def leave_kernel(groups, per, tiles, x_ref, gain_ref, *refs):
-    heads, weights, (normed_ref, attn_ref) = refs[: 5 * groups], refs[5 * groups : 5 * groups + 5], refs[5 * groups + 5 :]
+def leave_kernel(groups, per, tiles, core_ref, x_ref, gain_ref, *refs):
+    heads, weights, (normed_ref, attn_ref) = refs[: 5 * groups], refs[5 * groups : 5 * groups + 7], refs[5 * groups + 7 :]
     index = pl.program_id(0)
-    attn = jnp.zeros(x_ref.shape, F32)
-    for k in range(3):
-        attn = attn + dot(jnp.concatenate([heads[5 * g + k][...] for g in range(groups)], axis=1), weights[k][...], NT)
     stored = ((index // per) ^ 3) * per + index % per
     is_low = stored < tiles // 2
-    far = jnp.concatenate(
-        [jnp.where(is_low, heads[5 * g + 3][...], heads[5 * g + 4][...]) for g in range(groups)], axis=1
-    )
-    attn = attn + jnp.concatenate([dot(far, weights[3][...], NT), dot(far, weights[4][...], NT)], axis=1)
+    attn, mine, other = None, 0.0, 0.0
+    for k in range(4):
+        parts = [
+            heads[5 * g + k][...] if k < 3 else jnp.where(is_low, heads[5 * g + 3][...], heads[5 * g + 4][...])
+            for g in range(groups)
+        ]
+        part = jnp.concatenate(parts, axis=1)
+        if k == 0:
+            attn = dot(part, weights[0][...], NT)
+        else:
+            mine = mine + dot(part, weights[k][...], NT)
+            other = other + dot(part, weights[3 + k][...], NT)
+    attn = attn + in_order(core_ref[0], mine, other)
     middle = x_ref[...].astype(F32) + attn
     inv = lax.rsqrt(jnp.mean(middle * middle, axis=-1, keepdims=True) + EPSILON)
     normed_ref[...] = (middle * inv * gain_ref[...]).astype(BF)
@@ -783,14 +847,28 @@
         attn_ref[...] = attn
 
 
-def leave(x_all, gain_row, heads, weights, rows):
+def weight_specs(weights):
+    plain = [fixed(w.shape, 1) for w in weights if len(w.shape) == 2]
+    stacked = [w.shape[1:] for w in weights if len(w.shape) == 3]
+    return plain + [
+        pl.BlockSpec((None,) + shape, lambda *_, k=k: (k, 0, 0), pipeline_mode=pl.Buffered(1))
+        for shape in stacked
+        for k in range(3)
+    ]
+
+
+def weight_args(weights):
+    return [w for w in weights for _ in range(3 if len(w.shape) == 3 else 1)]
+
+
+def leave(core_row, x_all, gain_row, heads, weights, rows):
     length = x_all.shape[0]
     per, tiles = rows // TILE, length // TILE
-    by_row = pl.BlockSpec((TILE, D), lambda i: (i, 0))
+    by_row = pl.BlockSpec((TILE, D), lambda i, core: (i, 0))
 
     def head_spec(k, low, high, width):
         return pl.BlockSpec(
-            (TILE, width), lambda i: (jnp.clip(((i // per) ^ k) * per + i % per - low, 0, high - low - 1), 0)
+            (TILE, width), lambda i, core: (jnp.clip(((i // per) ^ k) * per + i % per - low, 0, high - low - 1), 0)
         )
 
     specs = []
@@ -801,11 +879,11 @@
         specs += [head_spec(3, 0, tiles // 2, width), head_spec(3, tiles // 2, tiles, width)]
     return call(
         functools.partial(leave_kernel, len(heads), per, tiles), (tiles,),
-        [by_row, fixed((1, D))] + specs + [fixed(w.shape) for w in weights],
-        [by_row, pl.BlockSpec((TILE, D), lambda i: (jnp.minimum(i, per - 1), 0))],
+        [by_row, fixed((1, D))] + specs + weight_specs(weights),
+        [by_row, pl.BlockSpec((TILE, D), lambda i, core: (jnp.minimum(i, per - 1), 0))],
         [shape_of((length, D)), shape_of((rows, D), F32)],
-        (x_all, gain_row, *[p for pieces in heads for p in pieces], *weights), "leave",
-        flops=2 * length * D * D, moved=length * D * 8,
+        (core_row, x_all, gain_row, *[p for pieces in heads for p in pieces], *weight_args(weights)), "leave",
+        flops=2 * length * D * D, moved=length * D * 8, prefetch=1,
     )
 
 
@@ -841,15 +919,20 @@
     )
 
 
-def sum_kernel(*refs):
+def sum_kernel(places, count, *refs):
     total = None
-    for i in range(0, len(refs) - 1, 2):
+    for i in range(0, 2 * count, 2):
         part = dot(refs[i][...], refs[i + 1][...], NT)
         total = part if total is None else total + part
-    refs[-1][...] = total.astype(BF)
-
-
-def sum_of(terms, first, rows):
+    total = total.astype(BF)
+    for (tile, start, size), ref in zip(places, refs[2 * count :]):
+
+        @pl.when(pl.program_id(0) == tile)
+        def _(start=start, size=size, ref=ref):
+            ref[...] = total[start : start + size]
+
+
+def sum_of(terms, first, rows, halves):
     tall, wide = 512, 512
     specs, args = [], []
     for left, right, column in terms:
@@ -857,10 +940,18 @@
         specs.append(pl.BlockSpec((tall, width), lambda i, j: (first // tall + i, 0)))
         specs.append(pl.BlockSpec((wide, width), lambda i, j, column=column: (j, column)))
         args += [left, right]
+    size = tall // 2 if halves else tall
+    places = [(i, start, size) for i in range(rows // tall) for start in range(0, tall, size)]
+    last = D // wide - 1
     depth = sum(left.shape[1] for left, _, _ in terms)
-    return call(
-        sum_kernel, (rows // tall, D // wide), specs, pl.BlockSpec((tall, wide), lambda i, j: (i, j)),
-        shape_of((rows, D)), args, "sum_of", flops=2 * rows * D * depth, moved=2 * depth * (rows + D) + 2 * rows * D,
+
+    def out_spec(tile):
+        return pl.BlockSpec((size, wide), lambda i, j: (0, jnp.where(i == tile, j, jnp.where(i < tile, 0, last))))
+
+    return call(
+        functools.partial(sum_kernel, places, len(terms)), (rows // tall, D // wide), specs,
+        [out_spec(tile) for tile, _, _ in places], [shape_of((size, D))] * len(places), args, "sum_of",
+        flops=2 * rows * D * depth, moved=2 * depth * (rows + D) + 2 * rows * D,
     )
 
 
@@ -872,69 +963,191 @@
             refs[-1][...] = dot(left_ref[...], refs[k][...], TN).astype(BF)
 
 
-def outer(left, rights, wide, total=None, first=0, before=()):
+def outer(left, rights, wide, total=None):
     length, tall, width = left.shape[0], 1024, rights[0].shape[1]
     across, count = width // wide, len(rights)
     right_spec = lambda k: pl.BlockSpec((length, wide), lambda i, j: (0, jnp.clip(j - k * across, 0, across - 1)))
     return call(
         functools.partial(outer_kernel, across, count), (left.shape[1] // tall, across * count),
-        [pl.BlockSpec((length, tall), lambda i, j: (0, i))]
-        + [right_spec(k) for k in range(count)]
-        + [pl.BlockSpec(memory_space=pl.ANY)] * len(before),
-        pl.BlockSpec((tall, wide), lambda i, j: (i, first // wide + j)),
-        shape_of((left.shape[1], total or width * count)),
-        (left, *rights, *before), "outer", flops=2 * length * left.shape[1] * width * count,
+        [pl.BlockSpec((length, tall), lambda i, j: (0, i))] + [right_spec(k) for k in range(count)],
+        pl.BlockSpec((tall, wide), lambda i, j: (i, j)), shape_of((left.shape[1], total or width * count)),
+        (left, *rights), "outer", flops=2 * length * left.shape[1] * width * count,
         moved=2 * (length + left.shape[1]) * (left.shape[1] + width * count),
-        aliases={1 + count: 0} if before else None,
-    )
-
-
-def turn_back_kernel(own_ref, by_x_ref, by_y_ref, x_ref, attn_ref, cot_ref, valid_ref, gain_ref, *refs):
-    weights, (middle_ref, low_ref, heads_ref) = refs[:5], refs[5:]
-    grad = own_ref[...].astype(F32) + by_x_ref[...].astype(F32) + by_y_ref[...].astype(F32)
+    )
+
+
+def outer_local_kernel(groups, left_ref, *refs):
+    for k in range(4):
+
+        @pl.when(pl.program_id(1) == k)
+        def _(k=k):
+            right = jnp.concatenate([refs[4 * g + k][...] for g in range(groups)], axis=1)
+            refs[-1][...] = dot(left_ref[...], right, TN).astype(BF)
+
+
+def outer_local(left, heads):
+    rows, width, tall = left.shape[0], heads[0][0].shape[1], 1024
+    specs, args = [], []
+    for pieces in heads:
+        for k, piece, block in ((0, pieces[0], 0), (1, pieces[1], 1), (2, pieces[2], 2), (3, pieces[4], 1)):
+            specs.append(pl.BlockSpec((rows, width), lambda i, k, block=block: (block, 0)))
+            args.append(piece)
+    across = width * len(heads)
+    return call(
+        functools.partial(outer_local_kernel, len(heads)), (D // tall, 4),
+        [pl.BlockSpec((rows, tall), lambda i, k: (0, i))] + specs, pl.BlockSpec((tall, across), lambda i, k: (i, k)),
+        shape_of((D, 4 * across)), (left, *args), "outer_local", flops=8 * rows * D * across,
+        moved=2 * D * (rows + 4 * across),
+    )
+
+
+def outer_rows_kernel(count, *refs):
+    for k in range(count):
+
+        @pl.when(pl.program_id(0) == k)
+        def _(k=k):
+            refs[-1][...] = dot(refs[k][...], refs[count][...], TN).astype(BF)
+
+
+def outer_rows(lefts, right, shard):
+    length, width = lefts[0].shape
+    count, shards = len(lefts), right.shape[1] // shard
+    return call(
+        functools.partial(outer_rows_kernel, count), (count, shards),
+        [pl.BlockSpec((length, width), lambda f, s: (0, 0))] * count + [pl.BlockSpec((length, shard), lambda f, s: (0, s))],
+        pl.BlockSpec((width, shard), lambda f, s: (s * count + f, 0)), shape_of((shards * count * width, shard)),
+        (*lefts, right), "outer_rows", flops=2 * length * right.shape[1] * width * count,
+        moved=2 * (length + right.shape[1]) * width * count,
+    )
+
+
+def two_halves(refs):
+    return jnp.where(pl.program_id(0) == 0, refs[0][...], refs[1][...]).astype(F32)
+
+
+def turn_back_kernel(core_ref, own_ref, x_low, x_high, y_low, y_high, x_ref, attn_ref, cot_ref, valid_ref, gain_ref, *refs):
+    weights, (middle_ref, low_ref, heads_ref) = refs[:7], refs[7:]
+    grad = own_ref[...].astype(F32) + two_halves((x_low, x_high)) + two_halves((y_low, y_high))
     middle = x_ref[...].astype(F32) + attn_ref[...]
     inv = lax.rsqrt(jnp.mean(middle * middle, axis=-1, keepdims=True) + EPSILON)
     grad_middle = cot_ref[...].astype(F32) * valid_ref[...] + norm_back(grad, middle, inv, gain_ref[...])
     middle_ref[...] = grad_middle
     low = grad_middle.astype(BF)
     low_ref[...] = low
-    for k in range(3):
-        heads_ref[k] = dot(low, weights[k][...]).astype(BF)
-    heads_ref[3] = (dot(low[:, : D // 2], weights[3][...]) + dot(low[:, D // 2 :], weights[4][...])).astype(BF)
-
-
-def turn_back(terms, x, attn, cot, valid_col, gain_row, weights):
+    first, second = low[:, : D // 2], low[:, D // 2 :]
+    mine = jnp.where(core_ref[0] == 0, first, second)
+    other = jnp.where(core_ref[0] == 0, second, first)
+    heads_ref[0] = dot(low, weights[0][...]).astype(BF)
+    for k in range(1, 4):
+        heads_ref[k] = (dot(mine, weights[k][...]) + dot(other, weights[3 + k][...])).astype(BF)
+
+
+def turn_back(core_row, own, terms, x, attn, cot, valid_col, gain_row, weights):
     rows, width = x.shape[0], weights[0].shape[1]
+    by_row = lambda w: pl.BlockSpec((TILE, w), lambda i, core: (i, 0))
+    return call(
+        turn_back_kernel, (rows // TILE,),
+        [by_row(D)] + [fixed((TILE, D))] * 4 + [by_row(D)] * 3 + [by_row(1), fixed((1, D))] + weight_specs(weights),
+        [by_row(D), by_row(D), pl.BlockSpec((4, TILE, width), lambda i, core: (0, i, 0))],
+        [shape_of((rows, D), F32), shape_of((rows, D)), shape_of((4, rows, width))],
+        (core_row, own, *terms, x, attn, cot, valid_col, gain_row, *weight_args(weights)), "turn_back",
+        flops=8 * rows * D * width, moved=rows * D * 20, prefetch=1,
+    )
+
+
+def last_kernel(own_ref, by_x_ref, by_y_ref, x_ref, attn_ref, valid_ref, out_ref, stats_ref):
+    mlp = own_ref[...].astype(F32) + by_x_ref[...].astype(F32) + by_y_ref[...].astype(F32)
+    x, attn, valid = x_ref[...].astype(F32), attn_ref[...], valid_ref[...]
+    middle = x + attn
+    final = middle + mlp
+    out_ref[...] = final.astype(BF)
+
+    @pl.when(pl.program_id(0) == 0)
+    def _():
+        stats_ref[...] = jnp.zeros(stats_ref.shape, F32)
+
+    for row, part in enumerate((x, middle, final, attn, mlp)):
+        stats_ref[row : row + 1, :] += fold(jnp.sum(valid * part * part, axis=0, keepdims=True))
+
+
+def last(own, by_x, by_y, x, attn, valid_col):
+    rows = x.shape[0]
     by_row = lambda w: pl.BlockSpec((TILE, w), lambda i: (i, 0))
     return call(
-        turn_back_kernel, (rows // TILE,),
-        [by_row(D)] * 6 + [by_row(1), fixed((1, D))] + [fixed(w.shape) for w in weights],
-        [by_row(D), by_row(D), pl.BlockSpec((4, TILE, width), lambda i: (0, i, 0))],
-        [shape_of((rows, D), F32), shape_of((rows, D)), shape_of((4, rows, width))],
-        (*terms, x, attn, cot, valid_col, gain_row, *weights), "turn_back",
-        flops=8 * rows * D * width, moved=rows * D * 20,
+        last_kernel, (rows // TILE,), [by_row(D)] * 5 + [by_row(1)], [by_row(D), fixed((8, LANES))],
+        [shape_of((rows, D)), shape_of((8, LANES), F32)], (own, by_x, by_y, x, attn, valid_col), "last",
+        moved=rows * D * 20,
     )
 
 
 def attend_back_one_kernel(rows, count, me_ref, *refs):
-    q, k, v, out, own, by_x, by_y, by_xy, total, query_row, key_col, cos, sin, cos_t, sin_t = refs[:15]
-    out_ref, grad, k_t, inner, dq_t, dk_acc, dv_acc = refs[15:]
+    q_ref, k_ref, v_ref, out_ref, own, by_x, by_y, by_xy, total_ref, query_row_ref, key_col_ref = refs[:11]
+    cos_ref, sin_ref, cos_t_ref, sin_t_ref, dqkv_ref, grad_ref, k_t, inner, dq_t, dk_acc, dv_acc = refs[11:]
+    me = me_ref[0]
+    half, width = HEAD_DIM // 2, GROUP * HEAD_DIM
     for block, ref in enumerate((own, by_x, by_y, by_xy)):
-        grad[block * rows : (block + 1) * rows, :] = ref[...] if len(ref.shape) == 2 else ref[0]
-    width = GROUP * HEAD_DIM
-    attend_back_kernel(
-        rows, count, me_ref, q, k, v, out, grad, total, query_row, key_col, cos, sin, cos_t, sin_t,
-        out_ref.at[:, :width], LaneSlice(out_ref, width), LaneSlice(out_ref, width + HEAD_DIM),
-        k_t, inner, dq_t, dk_acc, dv_acc,
-    )
-
-
-class LaneSlice:
-    def __init__(self, ref, start):
-        self.ref, self.start = ref, start
-
-    def __setitem__(self, key, value):
-        self.ref[key[1], self.start : self.start + HEAD_DIM] = value
+        grad_ref[block * rows : (block + 1) * rows, :] = ref[...] if len(ref.shape) == 2 else ref[0]
+    k_t[...] = k_ref[0].astype(F32).T.astype(BF)
+    dq_t[...] = jnp.zeros(dq_t.shape, F32)
+
+    def prepare(i, _):
+        here = pl.ds(pl.multiple_of(i * rows, rows), rows)
+        for head in range(GROUP):
+            cols = slice(head * HEAD_DIM, (head + 1) * HEAD_DIM)
+            both = out_ref[here, cols].astype(F32) * grad_ref[here, cols].astype(F32)
+            inner[head : head + 1, here] = jnp.sum(both.T, axis=0, keepdims=True)
+        return 0
+
+    lax.fori_loop(0, count, prepare, 0)
+
+    def visit(key_at, size, local, query_at, first, diagonal):
+        keys_here = pl.ds(key_at, size)
+        here = pl.ds(pl.multiple_of(query_at + first, rows // 2), rows - first)
+        keys, values, keys_t = k_ref[0, keys_here, :], v_ref[0, keys_here, :], k_t[:, keys_here]
+        bias = allowed_bias(rows, size, first, query_row_ref[:, here], key_col_ref[keys_here, :], diagonal)
+        for head in range(GROUP):
+            cols = slice(head * HEAD_DIM, (head + 1) * HEAD_DIM)
+            query, grad = q_ref[here, cols], grad_ref[here, cols]
+            probs = jnp.exp(dot(keys, query, NT) + bias - total_ref[0, head : head + 1, here])
+            dv_acc[local : local + size, :] += dot(probs.astype(BF), grad)
+            grad_probs = dot(values, grad, NT)
+            grad_scores = (probs * (grad_probs - inner[head : head + 1, here])).astype(BF)
+            dk_acc[local : local + size, :] += dot(grad_scores, query)
+            dq_t[head, :, here] += dot(keys_t, grad_scores)
+
+    def key_step(j, _):
+        key_start = pl.multiple_of((j ^ me) * rows, rows)
+        key_at = pl.ds(key_start, rows)
+        dk_acc[...] = jnp.zeros(dk_acc.shape, F32)
+        dv_acc[...] = jnp.zeros(dv_acc.shape, F32)
+        visit(key_start, rows // 2, 0, key_start, 0, True)
+        visit(pl.multiple_of(key_start + rows // 2, rows // 2), rows // 2, rows // 2, key_start, rows // 2, True)
+
+        def query_step(i, _):
+            visit(key_start, rows, 0, pl.multiple_of((i ^ me) * rows, rows), 0, False)
+            return 0
+
+        lax.fori_loop(j + 1, count, query_step, 0)
+        dk = dk_acc[...]
+        low, high = dk[:, :half], dk[:, half:]
+        cosine, sine = cos_ref[key_at, :half], sin_ref[key_at, half:HEAD_DIM]
+        turned = jnp.concatenate([low * cosine + high * sine, high * cosine - low * sine], axis=1)
+        dqkv_ref[key_at, width : width + HEAD_DIM] = turned.astype(BF)
+        dqkv_ref[key_at, width + HEAD_DIM :] = dv_acc[...].astype(BF)
+        return 0
+
+    lax.fori_loop(0, count, key_step, 0)
+
+    def finish_queries(i, _):
+        here = pl.ds(pl.multiple_of(i * rows, rows), rows)
+        cosine, sine = cos_t_ref[:, here], sin_t_ref[:, here]
+        for head in range(GROUP):
+            low, high = dq_t[head, :half, here], dq_t[head, half:, here]
+            turned = jnp.concatenate([low * cosine + high * sine, high * cosine - low * sine], axis=0) * SCALE
+            dqkv_ref[here, head * HEAD_DIM : (head + 1) * HEAD_DIM] = turned.T.astype(BF)
+        return 0
+
+    lax.fori_loop(0, count, finish_queries, 0)
 
 
 def attend_back_one(me_row, q, k, v, out, grads, totals, query_row, key_col, tables, rows, group):
@@ -967,29 +1180,31 @@
     )
 
 
-def finish_kernel(groups, step, x_ref, middle_ref, gain_ref, *refs):
-    grads, weights, out_ref = refs[: 4 * groups], refs[4 * groups : 4 * groups + 5], refs[-1]
-    columns = slice(0, groups * step)
-    grad = jnp.zeros(x_ref.shape, F32)
-    for k in range(3):
+def finish_kernel(groups, step, core_ref, x_ref, middle_ref, gain_ref, *refs):
+    grads, weights, out_ref = refs[: 4 * groups], refs[4 * groups : 4 * groups + 7], refs[-1]
+    grad, mine, other = None, 0.0, 0.0
+    for k in range(4):
         low = jnp.concatenate([grads[4 * g + k][...] for g in range(groups)], axis=1)
-        grad = grad + dot(low, weights[k][:, columns], NT)
-    low = jnp.concatenate([grads[4 * g + 3][...] for g in range(groups)], axis=1)
-    grad = grad + jnp.concatenate([dot(low, weights[3][:, columns], NT), dot(low, weights[4][:, columns], NT)], axis=1)
+        if k == 0:
+            grad = dot(low, weights[0][:, : groups * step], NT)
+        else:
+            mine = mine + dot(low, weights[k][...], NT)
+            other = other + dot(low, weights[3 + k][...], NT)
+    grad = grad + in_order(core_ref[0], mine, other)
     x = x_ref[...].astype(F32)
     inv = lax.rsqrt(jnp.mean(x * x, axis=-1, keepdims=True) + EPSILON)
     out_ref[...] = (middle_ref[...] + norm_back(grad, x, inv, gain_ref[...])).astype(BF)
 
 
-def finish(x, grad_middle, gain_row, grads, weights):
+def finish(core_row, x, grad_middle, gain_row, grads, weights):
     rows, step = x.shape[0], grads[0][0].shape[1]
-    by_row = lambda w: pl.BlockSpec((TILE, w), lambda i: (i, 0))
+    by_row = lambda w: pl.BlockSpec((TILE, w), lambda i, core: (i, 0))
     return call(
         functools.partial(finish_kernel, len(grads), step), (rows // TILE,),
-        [by_row(D), by_row(D), fixed((1, D))] + [by_row(step)] * (4 * len(grads)) + [fixed(w.shape) for w in weights],
+        [by_row(D), by_row(D), fixed((1, D))] + [by_row(step)] * (4 * len(grads)) + weight_specs(weights),
         by_row(D), shape_of((rows, D)),
-        (x, grad_middle, gain_row, *[p for parts in grads for p in parts], *weights), "finish",
-        flops=8 * rows * D * step * len(grads), moved=rows * D * 8 + 4 * D * step * 4,
+        (core_row, x, grad_middle, gain_row, *[p for parts in grads for p in parts], *weight_args(weights)), "finish",
+        flops=8 * rows * D * step * len(grads), moved=rows * D * 8 + 4 * D * step * 4, prefetch=1,
     )
 
 
@@ -1046,22 +1261,29 @@
     )
 
 
-def place_rows_kernel(me_ref, *refs):
-    def emit(values):
-        refs[5][...] = values.astype(F32).T
-
-    each_piece(refs[:5], emit)
+def place_rows_kernel(half, me_ref, *refs):
+    block, tile = pl.program_id(0), pl.program_id(1)
+    for k in range(5):
+        first = jnp.minimum(block, 3) == min(k, 3)
+
+        @pl.when(first if k < 3 else first & ((tile < half) == (k == 3)))
+        def _(k=k):
+            refs[5][...] = refs[k][...].astype(F32)
 
 
 def place_rows(me_row, pieces, tall):
-    columns, rows = pieces[0].shape[0], pieces[0].shape[1]
+    rows, columns = pieces[0].shape
     across = rows // tall
-
-    def spec(k, piece):
-        return pl.BlockSpec((piece.shape[0], tall), lambda i, j, me: (0, jnp.where(i == k, j, 0)))
-
-    return call(
-        place_rows_kernel, (4, across), [spec(min(k, 3), p) for k, p in enumerate(pieces)],
+    half = across // 2
+
+    def spec(k):
+        if k < 3:
+            return pl.BlockSpec((tall, columns), lambda i, j, me: (jnp.where(i == k, j, 0), 0))
+        low = (k - 3) * half
+        return pl.BlockSpec((tall, columns), lambda i, j, me: (jnp.where(i == 3, jnp.clip(j - low, 0, half - 1), 0), 0))
+
+    return call(
+        functools.partial(place_rows_kernel, half), (4, across), [spec(k) for k in range(5)],
         pl.BlockSpec((tall, columns), lambda i, j, me: ((i ^ me[0]) * across + j, 0)),
         shape_of((4 * rows, columns), F32), (me_row, *pieces), "place_rows", moved=rows * columns * 24, prefetch=1,
     )
@@ -1114,18 +1336,22 @@
     count = 4
     me = lax.axis_index("seq")
     me_row = me.reshape(1).astype(jnp.int32)
+    core = lax.axis_index("fsdp") % 2
+    core_row = core.reshape(1).astype(jnp.int32)
     rows = inputs.shape[1]
     length = rows * count
     kv_local = KV_HEADS // count
     q_width = kv_local * GROUP * HEAD_DIM
     ff_local = FF // count
     ff_chunk = ff_local // CHUNKS
+    shard_rows = gate_weight.shape[0]
     step = (GROUP + 2) * HEAD_DIM
 
     tokens_low, cot_low = inputs[0], cotangent[0]
     marks = jnp.stack([segments[0], valid_mask[0]])
     marks_all = jnp.stack([marks] + [swap(marks, k) for k in range(1, count)])
-    x_x, x_y = to_both(after(tokens_low, marks_all))
+    x_own = after(tokens_low, marks_all)
+    x_x, x_y = to_both(x_own)
 
     segment_all = marks_all[:, 0].reshape(length)
     valid_all = marks_all[:, 1].reshape(length)
@@ -1150,159 +1376,153 @@
     gains = jnp.pad(jnp.stack([attn_gain, mlp_gain], axis=1), ((0, 0), (0, LANES - 2)))
     qkv_full = gather_fsdp(pack_qkv(me_row, query_weight, key_weight, value_weight, gains, kv_local))
     out_slice = gather_fsdp(pack_rows(me_row, out_weight, q_width))
+    gain_one = qkv_full[:, kv_local * step].astype(F32).reshape(1, D)
+    gain_two = qkv_full[:, kv_local * step + 1].astype(F32).reshape(1, D)
+
+    x_far = pass_on(x_x, x_y, cosine, sine)
+    entered = enter([x_own, x_x, x_y], gain_one, qkv_full, cosine, sine, kv_local, 0, length)
+
     down_t = gather_fsdp(pack_rows(me_row, after(down_weight, x_x, x_y, cosine, sine), ff_local))
     later_gate = after(gate_weight, x_x, x_y, cosine, sine)
     gate_up = [
         gather_fsdp(pack_pair(me_row, later_gate, up_weight, CHUNKS, c, ff_chunk)) for c in range(CHUNKS)
     ]
-    gain_one = qkv_full[:, kv_local * step].astype(F32).reshape(1, D)
-    gain_two = qkv_full[:, kv_local * step + 1].astype(F32).reshape(1, D)
-
-    x_far = pass_on(x_x, x_y, cosine, sine)
-    entered = enter([tokens_low, x_x, x_y], gain_one, qkv_full, cosine, sine, kv_local, 0, length)
 
     done = (*x_far, entered[0])
-    o_own = after(out_slice, *done)
-    o_x, o_y = to_both(o_own)
+    o_mine = [swap(core_half(after(out_slice, *done), core), k) for k in range(1, count)]
+    grad_low = (cot_low.astype(F32) * valid_col).astype(BF)
     x_all, normed_one, q, k, v = enter(
         list(x_far), gain_one, qkv_full, cosine, sine, kv_local, 3 * rows, length, tuple(entered)
     )
     out_0, total_0 = attend_one(me_row, q, k, v, query_row, key_col, rows, 0)
 
-    done = (o_x, o_y, out_0)
-    o_far = pass_on(o_x, o_y, *done)
-    out_pieces = [out_slice, o_x, o_y, *o_far]
+    done = (*o_mine, out_0)
     h_x, h_y = to_both(after(out_0, *done))
+    o_other = swap_core(jnp.stack([after(w, *done) for w in o_mine]))
+    out_pieces = [out_slice, *o_mine, o_other]
     out_1, total_1 = attend_one(me_row, after(q, *done), k, v, query_row, key_col, rows, 1)
     heads, totals = [out_0, out_1], [total_0, total_1]
 
-    done = (*o_far, h_x, h_y, out_1)
+    done = (h_x, h_y, out_1, o_other)
     h_far = pass_on(h_x, h_y, *done)
     heads_0 = [out_0, h_x, h_y, *h_far]
     h_x, h_y = to_both(after(out_1, *done))
-    grad_low = (after(cot_low, *done).astype(F32) * valid_col).astype(BF)
-
-    done = (*h_far, h_x, h_y, grad_low)
+
+    done = (*h_far, h_x, h_y)
     h_far = pass_on(h_x, h_y, *done)
     heads_1 = [out_1, h_x, h_y, *h_far]
-
-    c_own = after(grad_low, *h_far)
+    c_own = after(grad_low, *done)
     c_x, c_y = to_both(c_own)
-    normed_two, attn_branch = leave(after(x_all, *h_far), gain_two, [heads_0, heads_1], out_pieces, rows)
+    normed_two, attn_branch = leave(core_row, after(x_all, *h_far), gain_two, [heads_0, heads_1], out_pieces, rows)
 
     done = (c_x, c_y, normed_two, down_t)
     c_far = pass_on(c_x, c_y, *done)
     acted = act_back([after(c_own, *done), c_x, c_y], down_t, 0, length)
 
     done = (*c_far, acted[0])
-    w_own = after(qkv_full, *done)[:, : kv_local * step]
-    w_x, w_y = to_both(w_own)
+    w_mine = [swap(core_half(after(qkv_full, *done)[:, : kv_local * step], core), k) for k in range(1, count)]
     grad_mlp, grad_act = act_back(list(c_far), down_t, 3 * rows, length, tuple(acted))
     act_0, gate_0, up_0 = up_project(normed_two, gate_up[0], grad_act, 0)
     grad_0 = outer(normed_two, [gate_0, up_0], 1024)
 
-    done = (w_x, w_y, grad_0)
+    done = (*w_mine, grad_0)
     gate_up_0 = scatter_fsdp(after(grad_0, *done))
-    w_far = pass_on(w_x, w_y, *done)
-    weight_pieces = [w_own, w_x, w_y, *w_far]
+    w_other = [swap_core(after(w, *done)) for w in w_mine]
+    weight_pieces = [qkv_full, *w_mine, *w_other]
     act_1, gate_1, up_1 = up_project(after(normed_two, *done), gate_up[1], grad_act, 1)
     terms = [(gate_0, gate_up[0], 0), (up_0, gate_up[0], 1), (gate_1, gate_up[1], 0), (up_1, gate_up[1], 1)]
-    far = sum_of(terms, 3 * rows, rows)
-
-    done = (far, *w_far)
-    g_far = send_far(after(far, *done))
-    near = sum_of([(after(gate_0, *done), *terms[0][1:])] + terms[1:], rows, 2 * rows)
-
-    for_x, for_y = add_far(near[:rows], near[rows:], *g_far)
-    g_x, g_y = swap(for_x, 1), swap(for_y, 2)
-    own = sum_of([(after(gate_0, for_x, for_y), *terms[0][1:])] + terms[1:], 0, rows)
+
+    def terms_after(*events):
+        return [(after(terms[0][0], *events), *terms[0][1:])] + terms[1:]
+
+    far = sum_of(terms, 3 * rows, rows, True)
+
+    done = (*far, *w_other)
+    g_far = send_far(*far)
+    near = sum_of(terms_after(*done), rows, 2 * rows, True)
+    near = add_far(near, *g_far)
+    g_near = send_near(near)
+    [own] = sum_of(terms_after(*near), 0, rows, False)
     grad_1 = outer(after(normed_two, own), [gate_1, up_1], 1024)
-
+    gate_up_1 = scatter_fsdp(after(grad_1, *g_near))
     grad_middle, grad_attn, grad_heads = turn_back(
-        [after(own, grad_1), g_x, g_y], tokens_low, attn_branch, cot_low, valid_col, gain_two, out_pieces
+        core_row, after(own, grad_1), g_near, tokens_low, attn_branch, cot_low, valid_col, gain_two, out_pieces
     )
 
     head_grads = [grad_heads] + [swap(grad_heads[k], k) for k in range(1, count)]
-    grad_down = outer(after(grad_mlp, grad_attn), [act_0, act_1], 1024)
-
-    gate_up_1 = scatter_fsdp(after(grad_1, grad_attn))
-    down_sum = scatter_fsdp(after(grad_down, *head_grads[1:]))
+    p_own = after(gate_up_0, grad_attn)
+    p_x, p_y = to_both(p_own)
+    grad_down = outer_rows([act_0, act_1], after(grad_mlp, grad_attn), shard_rows)
+    grad_out = outer_local(after(grad_attn, grad_down), [heads_0, heads_1])
 
     def attention_back(queries, group):
         return attend_back_one(
             me_row, queries, k, v, heads[group], head_grads, totals[group], query_row, key_col, tables, rows, group
         )
 
-    done = (*head_grads[1:], grad_down)
-    a_own = after(grad_attn, *done)
-    a_x, a_y = to_both(a_own)
+    done = (*head_grads[1:], p_x, p_y, grad_out)
+    out_sum = scatter_fsdp(after(grad_out, *done))
+    p_far = pass_on(p_x, p_y, *done)
+    p_pieces = [p_own, p_x, p_y, *p_far]
     dqkv_0 = attention_back(after(q, *done), 0)
 
-    done = (a_x, a_y, dqkv_0)
-    a_far = pass_on(a_x, a_y, *done)
+    done = (*p_far, dqkv_0)
+    down_sum = scatter_fsdp(after(grad_down, *done))
+    p_own = after(gate_up_1, *done)
+    p_x, p_y = to_both(p_own)
     parts_0 = exchange_seq(blocks_of(after(dqkv_0, *done), count))
     dqkv_1 = attention_back(after(q, *done), 1)
 
-    done = (*a_far, *parts_0[1:], dqkv_1)
+    done = (p_x, p_y, *parts_0[1:], dqkv_1)
     parts_1 = exchange_seq(blocks_of(after(dqkv_1, *done), count))
-    p_own = after(gate_up_0, *done)
-    p_x, p_y = to_both(p_own)
-    total = kv_local * step + q_width
-    grad_attn_all = join([after(a_own, *done), a_x, a_y, *a_far])
-    grad_weights = outer(after(normed_one, *done), [dqkv_0, dqkv_1], step, total)
-    grad_weights = outer(
-        grad_attn_all, heads, GROUP * HEAD_DIM, total, kv_local * step, (grad_weights,)
-    )
-
-    done = (*parts_1[1:], p_x, p_y, grad_weights)
-    attn_sum = scatter_fsdp(after(grad_weights, *done))
+    terms = [(act_0, down_t, 0), (act_1, down_t, 1)]
+    far = sum_of(terms_after(*done), 3 * rows, rows, True)
+    m_far = send_far(*far)
+    near = sum_of(terms_after(*far, *parts_1[1:]), rows, 2 * rows, True)
+
+    near = add_far(near, *m_far)
+    near = [jnp.concatenate(near[:2]), jnp.concatenate(near[2:])]
+    done = (*near, *parts_1[1:])
+    m_x, m_y = swap(near[0], 1), swap(near[1], 2)
     p_far = pass_on(p_x, p_y, *done)
-    p_pieces = [p_own, p_x, p_y, *p_far]
-    p_own = after(gate_up_1, *done)
-    p_x, p_y = to_both(p_own)
-    mlp_part = sum_of([(after(act_0, *done), down_t, 0), (act_1, down_t, 1)], 0, length)
-
-    done = (*p_far, p_x, p_y, mlp_part)
-    mlp_blocks = blocks_of(after(mlp_part, *done), count)
-    m_far = send_far(mlp_blocks[3])
-    p_far = pass_on(p_x, p_y, *done)
-    input_grad = finish(after(tokens_low, *done), grad_middle, gain_one, [parts_0, parts_1], weight_pieces)
-    placed = place_pair(
-        me_row, [after(p_pieces[0], input_grad)] + p_pieces[1:], gate_weight, up_weight, CHUNKS, 0, None
-    )
+    grad_qkv = outer(after(normed_one, *done), [dqkv_0, dqkv_1], step)
+    [own] = sum_of(terms_after(grad_qkv), 0, rows, False)
+    input_grad = finish(core_row, after(tokens_low, own), grad_middle, gain_one, [parts_0, parts_1], weight_pieces)
+
+    done = (m_x, m_y, *p_far, input_grad)
+    qkv_sum = scatter_fsdp(after(grad_qkv, *done))
     input_grad = input_grad[None]
-
-    done = (*m_far, *p_far, placed[2])
-    m_x, m_y = add_far(mlp_blocks[1], mlp_blocks[2], *m_far)
-    m_x, m_y = swap(after(m_x, *done), 1), swap(m_y, 2)
+    out_ready = after(out_sum, *done)
+    out_terms = exchange_seq([out_ready[:, k * q_width : (k + 1) * q_width] for k in range(count)])
+    outputs, stats = last(after(own, *done), m_x, m_y, tokens_low, attn_branch, valid_col)
+    outputs = outputs[None]
+    placed = place_pair(me_row, [after(p_pieces[0], stats)] + p_pieces[1:], gate_weight, up_weight, CHUNKS, 0, None)
+
+    done = (*out_terms[1:], placed[2])
+    out_sum = sum(term.astype(F32) for term in out_terms).astype(BF)
+    d_own = after(down_sum, *done)
+    d_x, d_y = to_both(d_own)
     gate_grad, up_grad, gate_up_dot = place_pair(
         me_row, [after(p_own, *done), p_x, p_y, *p_far], gate_weight, up_weight, CHUNKS, 1, placed
     )
 
-    done = (m_x, m_y, gate_up_dot)
-    d_x, d_y = to_both(after(down_sum, *done))
-    mlp_branch = mlp_blocks[0].astype(F32) + m_x.astype(F32) + m_y.astype(F32)
-    tokens = after(tokens_low, *done).astype(F32)
-    middle = tokens + attn_branch
-    final = middle + mlp_branch
-    outputs = final.astype(BF)[None]
-
-    done = (d_x, d_y, outputs)
+    done = (d_x, d_y, gate_up_dot)
     d_far = pass_on(d_x, d_y, *done)
-    t_x, t_y = to_both(after(attn_sum, *d_far))
-    down_grad = place_rows(me_row, [down_sum, d_x, d_y, *d_far], 512)
+
+    t_own = jnp.concatenate([after(qkv_sum, *d_far), out_sum], axis=1)
+    t_x, t_y = to_both(t_own)
+    stats = after(stats, *d_far)
+    down_grad = place_rows(me_row, [after(down_sum, *d_far), d_x, d_y, *d_far], 1024)
+    t_far = pass_on(t_x, t_y, t_x, t_y)
     query_grad, key_grad, value_grad, out_grad, qkv_dot = place_attn(
-        me_row, [attn_sum, t_x, t_y, *pass_on(t_x, t_y, down_grad)], query_weight, key_weight, value_weight, kv_local
+        me_row, [after(t_own, down_grad), t_x, t_y, *t_far], query_weight, key_weight, value_weight, kv_local
     )
     attn_gain_grad = jnp.sum(qkv_dot, axis=1) / attn_gain.astype(F32)
     mlp_gain_grad = jnp.sum(gate_up_dot, axis=1) / mlp_gain.astype(F32)
 
-    squares = [jnp.sum(valid_col * part * part) for part in (tokens, middle, final, attn_branch, mlp_branch)]
-    stats = jnp.stack([jnp.sum(valid_col)] + squares)
-    stats = jnp.broadcast_to(jnp.pad(stats, (0, LANES - 6))[None, :], (8, LANES))
     for bit in bit_orders()[0]:
         stats = stats + swap(stats, bit)
-    rms_stats = jnp.sqrt(stats[:1, 1:6] / (stats[:1, :1] * D))
+    rms_stats = jnp.sqrt(jnp.sum(stats[:5], axis=1)[None, :] / (jnp.sum(valid_all).astype(F32) * D))
     return (
         outputs, input_grad, query_grad, key_grad, value_grad, out_grad, gate_grad, up_grad, down_grad,
         attn_gain_grad, mlp_gain_grad, rms_stats,

time: 902 us -> 882 us (0.978)
  local copies, waits for them, and re-layouts: 64 us -> 44.3 us
    slice x5 -> x3, local copies, waits for them, and re-layouts: 12.8 us -> 2.87 us  [the longest x1 1.48 us: square_body(): out_ready[:, k * q_width:(k + 1) * q_width]]
    ppermute x66 -> x65, waiting for transfers between devices: 174 us -> 169 us  [swap(): return lax.ppermute(values, 'seq', [(i, i ^ bit) for i in range(count)])]
    pallas_call x32 -> x34, Pallas kernels: 539 us -> 542 us  [call(): pl.pallas_call(kernel, grid_spec=pltpu.PrefetchScalarGridSpec(num_scalar_...]
    ppermute x66 -> x65, starting transfers between devices: 66.4 us -> 69.3 us  [swap(): return lax.ppermute(values, 'seq', [(i, i ^ bit) for i in range(count)])]
  transfers between devices with their start and end apart: 75 -> 79, of which waited for: 22 -> 29; matrix products, arithmetic and copies ran while one was open for 10% -> 7% of each run, Pallas kernels for 60% -> 61%
where the time goes in v3:
time: 882 us; the launch traced here: 875 us
  Pallas kernels  542 us (61%)
  waiting for transfers between devices  169 us (19%)
  starting transfers between devices  70.6 us (8%)
  local copies, waits for them, and re-layouts  44.3 us (5%)
  other arithmetic  33.3 us (4%)
  between operations  15.9 us (2%)
    pallas_call x34, Pallas kernels, call(): pl.pallas_call(kernel, grid_spec=pltpu.PrefetchScalarGridSpec(num_scalar_...  542 us
    ppermute x65, waiting for transfers between devices, swap(): return lax.ppermute(values, 'seq', [(i, i ^ bit) for i in range(count)])  169 us
    ppermute x65, starting transfers between devices, swap(): return lax.ppermute(values, 'seq', [(i, i ^ bit) for i in range(count)])  69.3 us
  transfers between devices with their start and end apart: 79, of which 29 were waited for; matrix products, arithmetic and copies ran while one was open for 7% of the time, Pallas kernels for 61%

profile of v3, /device:TPU:0, one launch (start us, length us, event | category | flops | bytes accessed | tf_op | source)
XLA Modules:
  0.0 875.3 jit_solution(9505120497979370684)
XLA Ops:
  32.7 35.4 %collective-permute-done.5.refs_1_ = bf16[512,2048]{1,0:T(8,128)(2,1)} collective-permute-done((bf16[512,2048]{1,0:T(8,128)(2,1)S(1)}, bf16[512,2048]{1,0:T(8,128)(2,1)}, u32[]{:S(2)}, u32[]{:S(2)}) %collective-permute-start.5) | collective-permute-done | bytes 2097184 | tf_op jit(solution)/shard_map/ppermute | solution.py:41
  88.9 15.4 %enter.2 = (bf16[2048,2048]{1,0:T(8,128)(2,1)}, bf16[2048,2048]{1,0:T(8,128)(2,1)}, bf16[2048,512]{1,0:T(8,128)(2,1)}, bf16[2,2048,64]{2,1,0:T(8,128)(2,1)}, bf16[2,2048,64]{2,1,0:T(8,128)(2,1)}) custom-call(bf16[512,2048]{1,0:T(8,128)(2,1)} %bitcast.36, bf16[512,2048]{1,0:T(8,128)(2,1)} %collective-permute-done.5.refs_1_, ...), custom_call_target="tpu_custom_call" | custom-call | flops 5637144576 | bytes 25165824 | tf_op jit(solution)/shard_map/enter/pallas_call | solution.py:572
  118.0 29.2 %attend.2 = (bf16[2048,256]{1,0:T(8,128)(2,1)}, f32[1,4,2048]{2,1,0:T(4,128)}) custom-call(s32[1]{0:T(128)} %bitcast.9.me_ref, bf16[2048,512]{1,0:T(8,128)(2,1)} %get-tuple-element.204.q_ref.refs_0_, bf16[2,2048,64]{2,1,0:T(8,128)(2,1)} %get-tuple-element.142.k_ref.refs_1_, bf16[2,2048,64]{2,1,0:T(8,128)(2,1)} %get-tuple-element.143.v_ref.refs_2_, ...), custom_call_target="tpu_custom_call" | custom-call | flops 25999998976 | bytes 4194304 | tf_op jit(solution)/shard_map/attend/pallas_call | solution.py:572
  158.0 29.3 %attend.3 = (bf16[2048,256]{1,0:T(8,128)(2,1)}, f32[1,4,2048]{2,1,0:T(4,128)}) custom-call(s32[1]{0:T(128)} %bitcast.9.me_ref, bf16[2048,512]{1,0:T(8,128)(2,1)} %get-tuple-element.204.q_ref.refs_0_, bf16[2,2048,64]{2,1,0:T(8,128)(2,1)} %get-tuple-element.142.k_ref.refs_1_, bf16[2,2048,64]{2,1,0:T(8,128)(2,1)} %get-tuple-element.143.v_ref.refs_2_, ...), custom_call_target="tpu_custom_call" | custom-call | flops 25999998976 | bytes 4194304 | tf_op jit(solution)/shard_map/attend/pallas_call | solution.py:572
  194.2 19.4 %collective-permute-done.16.refs_6_.refs_5_ = bf16[2048,256]{1,0:T(8,128)(2,1)S(1)} collective-permute-done((bf16[2048,256]{1,0:T(8,128)(2,1)}, bf16[2048,256]{1,0:T(8,128)(2,1)S(1)}, u32[]{:S(2)}, u32[]{:S(2)}) %collective-permute-start.16) | collective-permute-done | bytes 1048608 | tf_op jit(solution)/shard_map/ppermute | solution.py:41
  241.5 29.0 %leave.1 = (bf16[2048,2048]{1,0:T(8,128)(2,1)}, f32[512,2048]{1,0:T(8,128)}) custom-call(s32[1]{0:T(128)} %bitcast.core_ref, bf16[2048,2048]{1,0:T(8,128)(2,1)} %get-tuple-element.156.x_ref, f32[1,2048]{1,0:T(1,128)} %bitcast.52, bf16[2048,256]{1,0:T(8,128)(2,1)} %get-tuple-element.147.refs_0_.refs_3_, bf16[2048,256]{1,0:T(8,128)(2,1)} %collective-permute-done.10.refs_1_, ...), custom_call_target="tpu_custom_call" | custom-call | flops 17179869184 | bytes 33554432 | tf_op jit(solution)/shard_map/leave/pallas_call | solution.py:572
  270.5 12.7 %collective-permute-done.20.refs_1_ = bf16[512,2048]{1,0:T(8,128)(2,1)} collective-permute-done((bf16[512,2048]{1,0:T(8,128)(2,1)}, bf16[512,2048]{1,0:T(8,128)(2,1)}, u32[]{:S(2)}, u32[]{:S(2)}) %collective-permute-start.20) | collective-permute-done | bytes 2097184 | tf_op jit(solution)/shard_map/ppermute | solution.py:41
  287.6 20.3 %act_back.2 = (bf16[2048,2048]{1,0:T(8,128)(2,1)}, bf16[2048,2048]{1,0:T(8,128)(2,1)}) custom-call(bf16[512,2048]{1,0:T(8,128)(2,1)} %multiply_convert_fusion.refs_0_, bf16[512,2048]{1,0:T(8,128)(2,1)} %collective-permute-done.20.refs_1_, bf16[512,2048]{1,0:T(8,128)(2,1)} %collective-permute-done.19.refs_2_, ...), custom_call_target="tpu_custom_call" | custom-call | flops 12884901888 | bytes 18874368 | tf_op jit(solution)/shard_map/act_back/pallas_call | solution.py:572
  326.5 25.3 %up_project.2 = (bf16[2048,1024]{1,0:T(8,128)(2,1)}, bf16[2048,1024]{1,0:T(8,128)(2,1)}, bf16[2048,1024]{1,0:T(8,128)(2,1)}) custom-call(bf16[2048,2048]{1,0:T(8,128)(2,1)} %get-tuple-element.186.normed_ref.left_ref, bf16[2048,2048]{1,0:T(8,128)(2,1)} %all-gather.10.cloned.1.call-done.gate_ref.up_ref.refs_1_.refs_3_, ...), custom_call_target="tpu_custom_call" | custom-call | flops 17179869184 | bytes 41943040 | tf_op jit(solution)/shard_map/up_project/pallas_call | solution.py:572
  351.8 24.3 %outer.3 = bf16[2048,2048]{1,0:T(8,128)(2,1)} custom-call(bf16[2048,2048]{1,0:T(8,128)(2,1)} %get-tuple-element.186.normed_ref.left_ref, bf16[2048,1024]{1,0:T(8,128)(2,1)} %get-tuple-element.185.refs_0_, bf16[2048,1024]{1,0:T(8,128)(2,1)} %get-tuple-element.170.refs_1_.refs_2_), custom_call_target="tpu_custom_call" | custom-call | flops 17179869184 | bytes 33554432 | tf_op jit(solution)/shard_map/outer/pallas_call | solution.py:572
  382.5 25.5 %up_project.3 = (bf16[2048,1024]{1,0:T(8,128)(2,1)}, bf16[2048,1024]{1,0:T(8,128)(2,1)}, bf16[2048,1024]{1,0:T(8,128)(2,1)}) custom-call(bf16[2048,2048]{1,0:T(8,128)(2,1)} %get-tuple-element.186.normed_ref.left_ref, bf16[2048,2048]{1,0:T(8,128)(2,1)} %all-gather.14.cloned.1.call-done.gate_ref.up_ref.refs_5_.refs_7_, ...), custom_call_target="tpu_custom_call" | custom-call | flops 17179869184 | bytes 41943040 | tf_op jit(solution)/shard_map/up_project/pallas_call | solution.py:572
  408.0 14.2 %sum_of.6 = (bf16[256,2048]{1,0:T(8,128)(2,1)}, bf16[256,2048]{1,0:T(8,128)(2,1)}) custom-call(bf16[2048,1024]{1,0:T(8,128)(2,1)} %get-tuple-element.185.refs_0_, bf16[2048,2048]{1,0:T(8,128)(2,1)} %all-gather.10.cloned.1.call-done.gate_ref.up_ref.refs_1_.refs_3_, bf16[2048,1024]{1,0:T(8,128)(2,1)} %get-tuple-element.170.refs_1_.refs_2_, ...), custom_call_target="tpu_custom_call" | custom-call | flops 8589934592 | bytes 23068672 | tf_op jit(solution)/shard_map/sum_of/pallas_call | solution.py:572
  424.2 25.6 %sum_of.7 = (bf16[256,2048]{1,0:T(8,128)(2,1)}, bf16[256,2048]{1,0:T(8,128)(2,1)}, bf16[256,2048]{1,0:T(8,128)(2,1)}, bf16[256,2048]{1,0:T(8,128)(2,1)}) custom-call(bf16[2048,1024]{1,0:T(8,128)(2,1)} %get-tuple-element.185.refs_0_, bf16[2048,2048]{1,0:T(8,128)(2,1)} %all-gather.10.cloned.1.call-done.gate_ref.up_ref.refs_1_.refs_3_, ...), custom_call_target="tpu_custom_call" | custom-call | flops 17179869184 | bytes 29360128 | tf_op jit(solution)/shard_map/sum_of/pallas_call | solution.py:572
  459.5 14.2 %sum_of.8.own_ref = bf16[512,2048]{1,0:T(8,128)(2,1)} custom-call(bf16[2048,1024]{1,0:T(8,128)(2,1)} %get-tuple-element.185.refs_0_, bf16[2048,2048]{1,0:T(8,128)(2,1)} %all-gather.10.cloned.1.call-done.gate_ref.up_ref.refs_1_.refs_3_, bf16[2048,1024]{1,0:T(8,128)(2,1)} %get-tuple-element.170.refs_1_.refs_2_, ...), custom_call_target="tpu_custom_call" | custom-call | flops 8589934592 | bytes 23068672 | tf_op jit(solution)/shard_map/sum_of/pallas_call | solution.py:572
  473.7 24.5 %outer.4 = bf16[2048,2048]{1,0:T(8,128)(2,1)} custom-call(bf16[2048,2048]{1,0:T(8,128)(2,1)} %get-tuple-element.186.normed_ref.left_ref, bf16[2048,1024]{1,0:T(8,128)(2,1)} %get-tuple-element.173.refs_4_.refs_0_, bf16[2048,1024]{1,0:T(8,128)(2,1)} %get-tuple-element.174.refs_6_.refs_1_), custom_call_target="tpu_custom_call" | custom-call | flops 17179869184 | bytes 33554432 | tf_op jit(solution)/shard_map/outer/pallas_call | solution.py:572
  505.3 16.0 %turn_back.1 = (f32[512,2048]{1,0:T(8,128)}, bf16[512,2048]{1,0:T(8,128)(2,1)}, bf16[4,512,512]{2,1,0:T(8,128)(2,1)}) custom-call(s32[1]{0:T(128)} %bitcast.core_ref, bf16[512,2048]{1,0:T(8,128)(2,1)} %sum_of.8.own_ref, bf16[256,2048]{1,0:T(8,128)(2,1)} %copy-done.23, bf16[256,2048]{1,0:T(8,128)(2,1)} %copy-done.22, bf16[256,2048]{1,0:T(8,128)(2,1)} %copy-done.21, ...), custom_call_target="tpu_custom_call" | custom-call | flops 4294967296 | bytes 20971520 | tf_op jit(solution)/shard_map/turn_back/pallas_call | solution.py:572
  528.9 27.0 %outer_rows.1 = bf16[16384,256]{1,0:T(8,128)(2,1)} custom-call(bf16[2048,1024]{1,0:T(8,128)(2,1)} %get-tuple-element.216.refs_0_, bf16[2048,1024]{1,0:T(8,128)(2,1)} %get-tuple-element.194.refs_1_.refs_2_, bf16[2048,2048]{1,0:T(8,128)(2,1)} %get-tuple-element.196.refs_2_), custom_call_target="tpu_custom_call" | custom-call | flops 17179869184 | bytes 16777216 | tf_op jit(solution)/shard_map/outer_rows/pallas_call | solution.py:572
  574.1 40.4 %attend_back.2.refs_0_ = bf16[2048,384]{1,0:T(8,128)(2,1)} custom-call(s32[1]{0:T(128)} %bitcast.9.me_ref, bf16[2048,512]{1,0:T(8,128)(2,1)} %get-tuple-element.204.q_ref.refs_0_, bf16[2,2048,64]{2,1,0:T(8,128)(2,1)} %get-tuple-element.142.k_ref.refs_1_, bf16[2,2048,64]{2,1,0:T(8,128)(2,1)} %get-tuple-element.143.v_ref.refs_2_, ...), custom_call_target="tpu_custom_call" | custom-call | flops 33999998976 | bytes 4194304 | tf_op jit(solution)/shard_map/attend_back/pallas_call | solution.py:572
  622.4 40.6 %attend_back.3.refs_1_ = bf16[2048,384]{1,0:T(8,128)(2,1)} custom-call(s32[1]{0:T(128)} %bitcast.9.me_ref, bf16[2048,512]{1,0:T(8,128)(2,1)} %get-tuple-element.204.q_ref.refs_0_, bf16[2,2048,64]{2,1,0:T(8,128)(2,1)} %get-tuple-element.142.k_ref.refs_1_, bf16[2,2048,64]{2,1,0:T(8,128)(2,1)} %get-tuple-element.143.v_ref.refs_2_, ...), custom_call_target="tpu_custom_call" | custom-call | flops 33999998976 | bytes 4194304 | tf_op jit(solution)/shard_map/attend_back/pallas_call | solution.py:572
  688.0 15.9 %sum_of.10 = (bf16[256,2048]{1,0:T(8,128)(2,1)}, bf16[256,2048]{1,0:T(8,128)(2,1)}, bf16[256,2048]{1,0:T(8,128)(2,1)}, bf16[256,2048]{1,0:T(8,128)(2,1)}) custom-call(bf16[2048,1024]{1,0:T(8,128)(2,1)} %get-tuple-element.216.refs_0_, bf16[2048,2048]{1,0:T(8,128)(2,1)} %all-gather.12.cloned.1.call-done.refs_3_.refs_2_.refs_1_, ...), custom_call_target="tpu_custom_call" | custom-call | flops 8589934592 | bytes 16777216 | tf_op jit(solution)/shard_map/sum_of/pallas_call | solution.py:572
  715.1 14.0 %outer.5 = bf16[2048,768]{1,0:T(8,128)(2,1)} custom-call(bf16[2048,2048]{1,0:T(8,128)(2,1)} %get-tuple-element.215.left_ref, bf16[2048,384]{1,0:T(8,128)(2,1)} %attend_back.2.refs_0_, bf16[2048,384]{1,0:T(8,128)(2,1)} %attend_back.3.refs_1_), custom_call_target="tpu_custom_call" | custom-call | flops 6442450944 | bytes 23068672 | tf_op jit(solution)/shard_map/outer/pallas_call | solution.py:572
  739.7 16.2 %finish.1 = bf16[512,2048]{1,0:T(8,128)(2,1)} custom-call(s32[1]{0:T(128)} %bitcast.core_ref, bf16[512,2048]{1,0:T(8,128)(2,1)} %bitcast.38, f32[512,2048]{1,0:T(8,128)} %get-tuple-element.220.middle_ref, f32[1,2048]{1,0:T(1,128)} %bitcast.51, bf16[512,384]{1,0:T(8,128)(2,1)} %get-tuple-element.259.refs_0_, ...), custom_call_target="tpu_custom_call" | custom-call | flops 6442450944 | bytes 20971520 | tf_op jit(solution)/shard_map/finish/pallas_call | solution.py:572
  755.9 13.4 %collective-permute-done.54.refs_3_ = bf16[128,2048]{1,0:T(8,128)(2,1)S(1)} collective-permute-done((bf16[128,2048]{1,0:T(8,128)(2,1)S(1)}, bf16[128,2048]{1,0:T(8,128)(2,1)S(1)}, u32[]{:S(2)}, u32[]{:S(2)}) %collective-permute-start.54) | collective-permute-done | bytes 524320 | tf_op jit(solution)/shard_map/ppermute | solution.py:41
  802.7 10.7 %collective-permute-done.60.refs_1_ = bf16[2048,256]{1,0:T(8,128)(2,1)S(1)} collective-permute-done((bf16[2048,256]{1,0:T(8,128)(2,1)}, bf16[2048,256]{1,0:T(8,128)(2,1)S(1)}, u32[]{:S(2)}, u32[]{:S(2)}) %collective-permute-start.60) | collective-permute-done | bytes 1048608 | tf_op jit(solution)/shard_map/ppermute | solution.py:41
  (347 shorter events, 321.1 us)
Async XLA Ops:
  7.2 79.2 %all-gather.6.cloned.1.call-start = ((), (), s32[]{:S(2)}) async-start(), calls=%async_computation.5 | async-start | bytes 4128768 | tf_op jit(solution)/shard_map/all_gather | solution.py:91
  11.4 92.9 %all-gather.8.cloned.1.call-start = ((), (), s32[]{:S(2)}) async-start(), calls=%async_computation.6 | async-start | bytes 2359296 | tf_op jit(solution)/shard_map/all_gather | solution.py:91
  13.3 272.6 %all-gather.12.cloned.1.call-start = ((), (), s32[]{:S(2)}) async-start(), calls=%async_computation.8 | async-start | bytes 9437184 | tf_op jit(solution)/shard_map/all_gather | solution.py:91
  22.4 45.8 %collective-permute-start.5 = (bf16[512,2048]{1,0:T(8,128)(2,1)S(1)}, bf16[512,2048]{1,0:T(8,128)(2,1)}, u32[]{:S(2)}, u32[]{:S(2)}) collective-permute-start(bf16[512,2048]{1,0:T(8,128)(2,1)S(1)} %bitcast.40), channel_id=1, source_target_pairs={{0,1},{1,0},{2,3},{3,2},{4,5},{5,4},{6,7},{7,6},{8,9},{9,8},{10,11... | collective-permute-start | bytes 6291464 | tf_op jit(solution)/shard_map/ppermute | solution.py:41
  23.0 45.5 %collective-permute-start.3 = (bf16[512,2048]{1,0:T(8,128)(2,1)S(1)}, bf16[512,2048]{1,0:T(8,128)(2,1)}, u32[]{:S(2)}, u32[]{:S(2)}) collective-permute-start(bf16[512,2048]{1,0:T(8,128)(2,1)S(1)} %bitcast.41), channel_id=1, source_target_pairs={{0,2},{1,3},{2,0},{3,1},{4,6},{5,7},{6,4},{7,5},{8,10},{9,11},{10,... | collective-permute-start | bytes 6291464 | tf_op jit(solution)/shard_map/ppermute | solution.py:41
  72.2 254.2 %all-gather.10.cloned.1.call-start = ((), (), s32[]{:S(2)}) async-start(), calls=%async_computation.7 | async-start | bytes 9437184 | tf_op jit(solution)/shard_map/all_gather | solution.py:91
  74.6 307.9 %all-gather.14.cloned.1.call-start = ((), (), s32[]{:S(2)}) async-start(), calls=%async_computation.9 | async-start | bytes 9437184 | tf_op jit(solution)/shard_map/all_gather | solution.py:91
  86.2 440.9 %reduce-scatter.8.cloned.1.call-start = ((), (), s32[]{:S(2)}) async-start(), calls=%async_computation.11 | async-start | bytes 9437184 | tf_op jit(solution)/shard_map/reduce_scatter | solution.py:95
  228.9 54.3 %collective-permute-start.20 = (bf16[512,2048]{1,0:T(8,128)(2,1)}, bf16[512,2048]{1,0:T(8,128)(2,1)}, u32[]{:S(2)}, u32[]{:S(2)}) collective-permute-start(bf16[512,2048]{1,0:T(8,128)(2,1)} %multiply_convert_fusion.refs_0_), channel_id=1, source_target_pairs={{0,1},{1,0},{2,3},{3,2},{4,5},{5,4},{6,7},{7,6},{8,9},{9,8},{10,11... | collective-permute-start | bytes 6291464 | tf_op jit(solution)/shard_map/ppermute | solution.py:41
  230.3 54.3 %collective-permute-start.19 = (bf16[512,2048]{1,0:T(8,128)(2,1)}, bf16[512,2048]{1,0:T(8,128)(2,1)}, u32[]{:S(2)}, u32[]{:S(2)}) collective-permute-start(bf16[512,2048]{1,0:T(8,128)(2,1)} %multiply_convert_fusion.refs_0_), channel_id=1, source_target_pairs={{0,2},{1,3},{2,0},{3,1},{4,6},{5,7},{6,4},{7,5},{8,10},{9,11},{10,... | collective-permute-start | bytes 6291464 | tf_op jit(solution)/shard_map/ppermute | solution.py:41
  312.6 63.5 %collective-permute-start.25 = (bf16[1024,768]{1,0:T(8,128)(2,1)}, bf16[1024,768]{1,0:T(8,128)(2,1)S(1)}, u32[]{:S(2)}, u32[]{:S(2)}) collective-permute-start(bf16[1024,768]{1,0:T(8,128)(2,1)} %constant_dynamic-slice_fusion), channel_id=1, source_target_pairs={{0,3},{1,2},{2,1},{3,0},{4,7},{5,6},{6,5},{7,4},{8,11},{9,10},{10,... | collective-permute-start | bytes 4718600 | tf_op jit(solution)/shard_map/ppermute | solution.py:41
  314.4 66.4 %collective-permute-start.24 = (bf16[1024,768]{1,0:T(8,128)(2,1)}, bf16[1024,768]{1,0:T(8,128)(2,1)S(1)}, u32[]{:S(2)}, u32[]{:S(2)}) collective-permute-start(bf16[1024,768]{1,0:T(8,128)(2,1)} %constant_dynamic-slice_fusion), channel_id=1, source_target_pairs={{0,2},{1,3},{2,0},{3,1},{4,6},{5,7},{6,4},{7,5},{8,10},{9,11},{10,... | collective-permute-start | bytes 4718600 | tf_op jit(solution)/shard_map/ppermute | solution.py:41
  315.4 65.4 %collective-permute-start.23 = (bf16[1024,768]{1,0:T(8,128)(2,1)}, bf16[1024,768]{1,0:T(8,128)(2,1)}, u32[]{:S(2)}, u32[]{:S(2)}) collective-permute-start(bf16[1024,768]{1,0:T(8,128)(2,1)} %constant_dynamic-slice_fusion), channel_id=1, source_target_pairs={{0,1},{1,0},{2,3},{3,2},{4,5},{5,4},{6,7},{7,6},{8,9},{9,8},{10,11... | collective-permute-start | bytes 4718600 | tf_op jit(solution)/shard_map/ppermute | solution.py:41
  380.8 239.6 %reduce-scatter.6.cloned.1.call-start = ((), (), s32[]{:S(2)}) async-start(), calls=%async_computation.10 | async-start | bytes 9437184 | tf_op jit(solution)/shard_map/reduce_scatter | solution.py:95
  452.8 45.3 %collective-permute-start.33 = (bf16[256,2048]{1,0:T(8,128)(2,1)}, bf16[256,2048]{1,0:T(8,128)(2,1)S(1)}, u32[]{:S(2)}, u32[]{:S(2)}) collective-permute-start(bf16[256,2048]{1,0:T(8,128)(2,1)} %add_convert_fusion.2), channel_id=1, source_target_pairs={{0,2},{1,3},{2,0},{3,1},{4,6},{5,7},{6,4},{7,5},{8,10},{9,11},{10,... | collective-permute-start | bytes 3145736 | tf_op jit(solution)/shard_map/ppermute | solution.py:41
  457.4 46.0 %collective-permute-start.31 = (bf16[256,2048]{1,0:T(8,128)(2,1)}, bf16[256,2048]{1,0:T(8,128)(2,1)S(1)}, u32[]{:S(2)}, u32[]{:S(2)}) collective-permute-start(bf16[256,2048]{1,0:T(8,128)(2,1)} %get-tuple-element.181), channel_id=1, source_target_pairs={{0,1},{1,0},{2,3},{3,2},{4,5},{5,4},{6,7},{7,6},{8,9},{9,8},{10,11... | collective-permute-start | bytes 3145736 | tf_op jit(solution)/shard_map/ppermute | solution.py:41
  458.5 44.9 %collective-permute-start.34 = (bf16[256,2048]{1,0:T(8,128)(2,1)}, bf16[256,2048]{1,0:T(8,128)(2,1)}, u32[]{:S(2)}, u32[]{:S(2)}) collective-permute-start(bf16[256,2048]{1,0:T(8,128)(2,1)} %get-tuple-element.184), channel_id=1, source_target_pairs={{0,2},{1,3},{2,0},{3,1},{4,6},{5,7},{6,4},{7,5},{8,10},{9,11},{10,... | collective-permute-start | bytes 3145736 | tf_op jit(solution)/shard_map/ppermute | solution.py:41
  504.4 264.9 %reduce-scatter.14.cloned.1.call-start = ((), (), s32[]{:S(2)}) async-start(), calls=%async_computation.14 | async-start | bytes 9437184 | tf_op jit(solution)/shard_map/reduce_scatter | solution.py:95
  569.7 222.3 %reduce-scatter.12.cloned.1.call-start = ((), (), s32[]{:S(2)}) async-start(), calls=%async_computation.13 | async-start | bytes 9437184 | tf_op jit(solution)/shard_map/reduce_scatter | solution.py:95
  614.6 204.8 %reduce-scatter.10.cloned.1.call-start = ((), (), s32[]{:S(2)}) async-start(), calls=%async_computation.12 | async-start | bytes 3538944 | tf_op jit(solution)/shard_map/reduce_scatter | solution.py:95
  616.9 46.2 %collective-permute-start.46 = (bf16[512,384]{1,0:T(8,128)(2,1)S(1)}, bf16[512,384]{1,0:T(8,128)(2,1)}, u32[]{:S(2)}, u32[]{:S(2)}) collective-permute-start(bf16[512,384]{1,0:T(8,128)(2,1)S(1)} %get-tuple-element.260), channel_id=1, source_target_pairs={{0,3},{1,2},{2,1},{3,0},{4,7},{5,6},{6,5},{7,4},{8,11},{9,10},{10,... | collective-permute-start | bytes 1179656 | tf_op jit(solution)/shard_map/ppermute | solution.py:41
  618.4 44.7 %collective-permute-start.45 = (bf16[512,384]{1,0:T(8,128)(2,1)S(1)}, bf16[512,384]{1,0:T(8,128)(2,1)}, u32[]{:S(2)}, u32[]{:S(2)}) collective-permute-start(bf16[512,384]{1,0:T(8,128)(2,1)S(1)} %get-tuple-element.261), channel_id=1, source_target_pairs={{0,2},{1,3},{2,0},{3,1},{4,6},{5,7},{6,4},{7,5},{8,10},{9,11},{10,... | collective-permute-start | bytes 1179656 | tf_op jit(solution)/shard_map/ppermute | solution.py:41
  710.7 58.6 %collective-permute-start.53 = (bf16[512,2048]{1,0:T(8,128)(2,1)}, bf16[512,2048]{1,0:T(8,128)(2,1)}, u32[]{:S(2)}, u32[]{:S(2)}) collective-permute-start(bf16[512,2048]{1,0:T(8,128)(2,1)} %pad_maximum_fusion.2), channel_id=1, source_target_pairs={{0,2},{1,3},{2,0},{3,1},{4,6},{5,7},{6,4},{7,5},{8,10},{9,11},{10,... | collective-permute-start | bytes 6291464 | tf_op jit(solution)/shard_map/ppermute | solution.py:41
  713.3 55.9 %collective-permute-start.52 = (bf16[512,2048]{1,0:T(8,128)(2,1)}, bf16[512,2048]{1,0:T(8,128)(2,1)}, u32[]{:S(2)}, u32[]{:S(2)}) collective-permute-start(bf16[512,2048]{1,0:T(8,128)(2,1)} %pad_maximum_fusion.1), channel_id=1, source_target_pairs={{0,1},{1,0},{2,3},{3,2},{4,5},{5,4},{6,7},{7,6},{8,9},{9,8},{10,11... | collective-permute-start | bytes 6291464 | tf_op jit(solution)/shard_map/ppermute | solution.py:41
  (105 other events, 2045.3 us)
Sparse Core Ops, SparseCore 0:
  11.6 45.2 all-gather.5
  59.1 27.9 all-gather.7
  88.7 81.5 all-gather.11
  171.7 80.5 all-gather.9
  253.8 80.5 all-gather.13
  380.9 89.3 reduce-scatter.7
  503.6 89.3 reduce-scatter.5
  595.8 87.9 reduce-scatter.13
  686.1 87.9 reduce-scatter.11
  776.3 38.6 reduce-scatter.9

commit v4 on v3

--- a/solution.py
+++ b/solution.py
@@ -1494,14 +1494,13 @@
     input_grad = input_grad[None]
     out_ready = after(out_sum, *done)
     out_terms = exchange_seq([out_ready[:, k * q_width : (k + 1) * q_width] for k in range(count)])
+    d_x, d_y = to_both(after(down_sum, out_ready))
     outputs, stats = last(after(own, *done), m_x, m_y, tokens_low, attn_branch, valid_col)
     outputs = outputs[None]
     placed = place_pair(me_row, [after(p_pieces[0], stats)] + p_pieces[1:], gate_weight, up_weight, CHUNKS, 0, None)
 
     done = (*out_terms[1:], placed[2])
     out_sum = sum(term.astype(F32) for term in out_terms).astype(BF)
-    d_own = after(down_sum, *done)
-    d_x, d_y = to_both(d_own)
     gate_grad, up_grad, gate_up_dot = place_pair(
         me_row, [after(p_own, *done), p_x, p_y, *p_far], gate_weight, up_weight, CHUNKS, 1, placed
     )
@@ -1512,16 +1511,17 @@
     t_own = jnp.concatenate([after(qkv_sum, *d_far), out_sum], axis=1)
     t_x, t_y = to_both(t_own)
     stats = after(stats, *d_far)
+    stats = stats + swap(stats, 1)
     down_grad = place_rows(me_row, [after(down_sum, *d_far), d_x, d_y, *d_far], 1024)
-    t_far = pass_on(t_x, t_y, t_x, t_y)
+    t_far = pass_on(t_x, t_y, t_x, t_y, down_grad)
+    stats = after(stats, t_x, t_y, down_grad)
+    stats = stats + swap(stats, 2)
     query_grad, key_grad, value_grad, out_grad, qkv_dot = place_attn(
         me_row, [after(t_own, down_grad), t_x, t_y, *t_far], query_weight, key_weight, value_weight, kv_local
     )
     attn_gain_grad = jnp.sum(qkv_dot, axis=1) / attn_gain.astype(F32)
     mlp_gain_grad = jnp.sum(gate_up_dot, axis=1) / mlp_gain.astype(F32)
 
-    for bit in bit_orders()[0]:
-        stats = stats + swap(stats, bit)
     rms_stats = jnp.sqrt(jnp.sum(stats[:5], axis=1)[None, :] / (jnp.sum(valid_all).astype(F32) * D))
     return (
         outputs, input_grad, query_grad, key_grad, value_grad, out_grad, gate_grad, up_grad, down_grad,

time: 882 us -> 885 us (level)
  transfers between devices with their start and end apart: 79 -> 79, of which waited for: 29 -> 31; matrix products, arithmetic and copies ran while one was open for 7% -> 7% of each run, Pallas kernels for 61% -> 61%
where the time goes in v4:
time: 885 us; the launch traced here: 874 us
  Pallas kernels  543 us (61%)
  waiting for transfers between devices  166 us (19%)
  starting transfers between devices  71 us (8%)
  local copies, waits for them, and re-layouts  44.6 us (5%)
  other arithmetic  33.2 us (4%)
  between operations  15.8 us (2%)
    pallas_call x34, Pallas kernels, call(): pl.pallas_call(kernel, grid_spec=pltpu.PrefetchScalarGridSpec(num_scalar_...  543 us
    ppermute x65, waiting for transfers between devices, swap(): return lax.ppermute(values, 'seq', [(i, i ^ bit) for i in range(count)])  161 us
    ppermute x65, starting transfers between devices, swap(): return lax.ppermute(values, 'seq', [(i, i ^ bit) for i in range(count)])  69.8 us
  transfers between devices with their start and end apart: 79, of which 31 were waited for; matrix products, arithmetic and copies ran while one was open for 7% of the time, Pallas kernels for 61%

profile of v4, /device:TPU:0, one launch (start us, length us, event | category | flops | bytes accessed | tf_op | source)
XLA Modules:
  0.0 873.7 jit_solution(8196396519077672612)
XLA Ops:
  32.7 35.4 %collective-permute-done.5.refs_1_ = bf16[512,2048]{1,0:T(8,128)(2,1)} collective-permute-done((bf16[512,2048]{1,0:T(8,128)(2,1)S(1)}, bf16[512,2048]{1,0:T(8,128)(2,1)}, u32[]{:S(2)}, u32[]{:S(2)}) %collective-permute-start.5) | collective-permute-done | bytes 2097184 | tf_op jit(solution)/shard_map/ppermute | solution.py:41
  88.9 15.4 %enter.2 = (bf16[2048,2048]{1,0:T(8,128)(2,1)}, bf16[2048,2048]{1,0:T(8,128)(2,1)}, bf16[2048,512]{1,0:T(8,128)(2,1)}, bf16[2,2048,64]{2,1,0:T(8,128)(2,1)}, bf16[2,2048,64]{2,1,0:T(8,128)(2,1)}) custom-call(bf16[512,2048]{1,0:T(8,128)(2,1)} %bitcast.36, bf16[512,2048]{1,0:T(8,128)(2,1)} %collective-permute-done.5.refs_1_, ...), custom_call_target="tpu_custom_call" | custom-call | flops 5637144576 | bytes 25165824 | tf_op jit(solution)/shard_map/enter/pallas_call | solution.py:572
  118.0 29.2 %attend.2 = (bf16[2048,256]{1,0:T(8,128)(2,1)}, f32[1,4,2048]{2,1,0:T(4,128)}) custom-call(s32[1]{0:T(128)} %bitcast.9.me_ref, bf16[2048,512]{1,0:T(8,128)(2,1)} %get-tuple-element.205.q_ref.refs_0_, bf16[2,2048,64]{2,1,0:T(8,128)(2,1)} %get-tuple-element.143.k_ref.refs_1_, bf16[2,2048,64]{2,1,0:T(8,128)(2,1)} %get-tuple-element.144.v_ref.refs_2_, ...), custom_call_target="tpu_custom_call" | custom-call | flops 25999998976 | bytes 4194304 | tf_op jit(solution)/shard_map/attend/pallas_call | solution.py:572
  158.0 29.3 %attend.3 = (bf16[2048,256]{1,0:T(8,128)(2,1)}, f32[1,4,2048]{2,1,0:T(4,128)}) custom-call(s32[1]{0:T(128)} %bitcast.9.me_ref, bf16[2048,512]{1,0:T(8,128)(2,1)} %get-tuple-element.205.q_ref.refs_0_, bf16[2,2048,64]{2,1,0:T(8,128)(2,1)} %get-tuple-element.143.k_ref.refs_1_, bf16[2,2048,64]{2,1,0:T(8,128)(2,1)} %get-tuple-element.144.v_ref.refs_2_, ...), custom_call_target="tpu_custom_call" | custom-call | flops 25999998976 | bytes 4194304 | tf_op jit(solution)/shard_map/attend/pallas_call | solution.py:572
  194.3 19.4 %collective-permute-done.16.refs_6_.refs_5_ = bf16[2048,256]{1,0:T(8,128)(2,1)S(1)} collective-permute-done((bf16[2048,256]{1,0:T(8,128)(2,1)}, bf16[2048,256]{1,0:T(8,128)(2,1)S(1)}, u32[]{:S(2)}, u32[]{:S(2)}) %collective-permute-start.16) | collective-permute-done | bytes 1048608 | tf_op jit(solution)/shard_map/ppermute | solution.py:41
  241.5 29.0 %leave.1 = (bf16[2048,2048]{1,0:T(8,128)(2,1)}, f32[512,2048]{1,0:T(8,128)}) custom-call(s32[1]{0:T(128)} %bitcast.core_ref, bf16[2048,2048]{1,0:T(8,128)(2,1)} %get-tuple-element.157.x_ref, f32[1,2048]{1,0:T(1,128)} %bitcast.52, bf16[2048,256]{1,0:T(8,128)(2,1)} %get-tuple-element.148.refs_0_.refs_3_, bf16[2048,256]{1,0:T(8,128)(2,1)} %collective-permute-done.10.refs_1_, ...), custom_call_target="tpu_custom_call" | custom-call | flops 17179869184 | bytes 33554432 | tf_op jit(solution)/shard_map/leave/pallas_call | solution.py:572
  270.5 12.7 %collective-permute-done.20.refs_1_ = bf16[512,2048]{1,0:T(8,128)(2,1)} collective-permute-done((bf16[512,2048]{1,0:T(8,128)(2,1)}, bf16[512,2048]{1,0:T(8,128)(2,1)}, u32[]{:S(2)}, u32[]{:S(2)}) %collective-permute-start.20) | collective-permute-done | bytes 2097184 | tf_op jit(solution)/shard_map/ppermute | solution.py:41
  287.6 20.3 %act_back.2 = (bf16[2048,2048]{1,0:T(8,128)(2,1)}, bf16[2048,2048]{1,0:T(8,128)(2,1)}) custom-call(bf16[512,2048]{1,0:T(8,128)(2,1)} %multiply_convert_fusion.refs_0_, bf16[512,2048]{1,0:T(8,128)(2,1)} %collective-permute-done.20.refs_1_, bf16[512,2048]{1,0:T(8,128)(2,1)} %collective-permute-done.19.refs_2_, ...), custom_call_target="tpu_custom_call" | custom-call | flops 12884901888 | bytes 18874368 | tf_op jit(solution)/shard_map/act_back/pallas_call | solution.py:572
  316.0 10.4 %act_back.3 = (bf16[2048,2048]{1,0:T(8,128)(2,1)}, bf16[2048,2048]{1,0:T(8,128)(2,1)}) custom-call(bf16[256,2048]{1,0:T(8,128)(2,1)} %copy-done.28, bf16[256,2048]{1,0:T(8,128)(2,1)} %collective-permute-done.22.refs_1_, bf16[2048,2048]{1,0:T(8,128)(2,1)} %all-gather.12.cloned.1.call-done.refs_3_.refs_2_.refs_1_, ...), custom_call_target="tpu_custom_call", output_to_operand_aliasing={{0}: (3, {}), {1}: (4, {})} | custom-call | flops 4294967296 | bytes 6291456 | tf_op jit(solution)/shard_map/act_back/pallas_call | solution.py:572
  326.4 25.3 %up_project.2 = (bf16[2048,1024]{1,0:T(8,128)(2,1)}, bf16[2048,1024]{1,0:T(8,128)(2,1)}, bf16[2048,1024]{1,0:T(8,128)(2,1)}) custom-call(bf16[2048,2048]{1,0:T(8,128)(2,1)} %get-tuple-element.187.normed_ref.left_ref, bf16[2048,2048]{1,0:T(8,128)(2,1)} %all-gather.10.cloned.1.call-done.gate_ref.up_ref.refs_1_.refs_3_, ...), custom_call_target="tpu_custom_call" | custom-call | flops 17179869184 | bytes 41943040 | tf_op jit(solution)/shard_map/up_project/pallas_call | solution.py:572
  351.7 24.3 %outer.3 = bf16[2048,2048]{1,0:T(8,128)(2,1)} custom-call(bf16[2048,2048]{1,0:T(8,128)(2,1)} %get-tuple-element.187.normed_ref.left_ref, bf16[2048,1024]{1,0:T(8,128)(2,1)} %get-tuple-element.186.refs_0_, bf16[2048,1024]{1,0:T(8,128)(2,1)} %get-tuple-element.171.refs_1_.refs_2_), custom_call_target="tpu_custom_call" | custom-call | flops 17179869184 | bytes 33554432 | tf_op jit(solution)/shard_map/outer/pallas_call | solution.py:572
  382.5 25.6 %up_project.3 = (bf16[2048,1024]{1,0:T(8,128)(2,1)}, bf16[2048,1024]{1,0:T(8,128)(2,1)}, bf16[2048,1024]{1,0:T(8,128)(2,1)}) custom-call(bf16[2048,2048]{1,0:T(8,128)(2,1)} %get-tuple-element.187.normed_ref.left_ref, bf16[2048,2048]{1,0:T(8,128)(2,1)} %all-gather.14.cloned.1.call-done.gate_ref.up_ref.refs_5_.refs_7_, ...), custom_call_target="tpu_custom_call" | custom-call | flops 17179869184 | bytes 41943040 | tf_op jit(solution)/shard_map/up_project/pallas_call | solution.py:572
  408.0 14.1 %sum_of.6 = (bf16[256,2048]{1,0:T(8,128)(2,1)}, bf16[256,2048]{1,0:T(8,128)(2,1)}) custom-call(bf16[2048,1024]{1,0:T(8,128)(2,1)} %get-tuple-element.186.refs_0_, bf16[2048,2048]{1,0:T(8,128)(2,1)} %all-gather.10.cloned.1.call-done.gate_ref.up_ref.refs_1_.refs_3_, bf16[2048,1024]{1,0:T(8,128)(2,1)} %get-tuple-element.171.refs_1_.refs_2_, ...), custom_call_target="tpu_custom_call" | custom-call | flops 8589934592 | bytes 23068672 | tf_op jit(solution)/shard_map/sum_of/pallas_call | solution.py:572
  424.3 25.6 %sum_of.7 = (bf16[256,2048]{1,0:T(8,128)(2,1)}, bf16[256,2048]{1,0:T(8,128)(2,1)}, bf16[256,2048]{1,0:T(8,128)(2,1)}, bf16[256,2048]{1,0:T(8,128)(2,1)}) custom-call(bf16[2048,1024]{1,0:T(8,128)(2,1)} %get-tuple-element.186.refs_0_, bf16[2048,2048]{1,0:T(8,128)(2,1)} %all-gather.10.cloned.1.call-done.gate_ref.up_ref.refs_1_.refs_3_, ...), custom_call_target="tpu_custom_call" | custom-call | flops 17179869184 | bytes 29360128 | tf_op jit(solution)/shard_map/sum_of/pallas_call | solution.py:572
  459.6 14.2 %sum_of.8.own_ref = bf16[512,2048]{1,0:T(8,128)(2,1)} custom-call(bf16[2048,1024]{1,0:T(8,128)(2,1)} %get-tuple-element.186.refs_0_, bf16[2048,2048]{1,0:T(8,128)(2,1)} %all-gather.10.cloned.1.call-done.gate_ref.up_ref.refs_1_.refs_3_, bf16[2048,1024]{1,0:T(8,128)(2,1)} %get-tuple-element.171.refs_1_.refs_2_, ...), custom_call_target="tpu_custom_call" | custom-call | flops 8589934592 | bytes 23068672 | tf_op jit(solution)/shard_map/sum_of/pallas_call | solution.py:572
  473.8 24.5 %outer.4 = bf16[2048,2048]{1,0:T(8,128)(2,1)} custom-call(bf16[2048,2048]{1,0:T(8,128)(2,1)} %get-tuple-element.187.normed_ref.left_ref, bf16[2048,1024]{1,0:T(8,128)(2,1)} %get-tuple-element.174.refs_4_.refs_0_, bf16[2048,1024]{1,0:T(8,128)(2,1)} %get-tuple-element.175.refs_6_.refs_1_), custom_call_target="tpu_custom_call" | custom-call | flops 17179869184 | bytes 33554432 | tf_op jit(solution)/shard_map/outer/pallas_call | solution.py:572
  505.4 16.0 %turn_back.1 = (f32[512,2048]{1,0:T(8,128)}, bf16[512,2048]{1,0:T(8,128)(2,1)}, bf16[4,512,512]{2,1,0:T(8,128)(2,1)}) custom-call(s32[1]{0:T(128)} %bitcast.core_ref, bf16[512,2048]{1,0:T(8,128)(2,1)} %sum_of.8.own_ref, bf16[256,2048]{1,0:T(8,128)(2,1)} %copy-done.23, bf16[256,2048]{1,0:T(8,128)(2,1)} %copy-done.22, bf16[256,2048]{1,0:T(8,128)(2,1)} %copy-done.21, ...), custom_call_target="tpu_custom_call" | custom-call | flops 4294967296 | bytes 20971520 | tf_op jit(solution)/shard_map/turn_back/pallas_call | solution.py:572
  529.0 27.0 %outer_rows.1 = bf16[16384,256]{1,0:T(8,128)(2,1)} custom-call(bf16[2048,1024]{1,0:T(8,128)(2,1)} %get-tuple-element.217.refs_0_, bf16[2048,1024]{1,0:T(8,128)(2,1)} %get-tuple-element.195.refs_1_.refs_2_, bf16[2048,2048]{1,0:T(8,128)(2,1)} %get-tuple-element.197.refs_2_), custom_call_target="tpu_custom_call" | custom-call | flops 17179869184 | bytes 16777216 | tf_op jit(solution)/shard_map/outer_rows/pallas_call | solution.py:572
  574.3 40.4 %attend_back.2.refs_0_ = bf16[2048,384]{1,0:T(8,128)(2,1)} custom-call(s32[1]{0:T(128)} %bitcast.9.me_ref, bf16[2048,512]{1,0:T(8,128)(2,1)} %get-tuple-element.205.q_ref.refs_0_, bf16[2,2048,64]{2,1,0:T(8,128)(2,1)} %get-tuple-element.143.k_ref.refs_1_, bf16[2,2048,64]{2,1,0:T(8,128)(2,1)} %get-tuple-element.144.v_ref.refs_2_, ...), custom_call_target="tpu_custom_call" | custom-call | flops 33999998976 | bytes 4194304 | tf_op jit(solution)/shard_map/attend_back/pallas_call | solution.py:572
  622.6 40.7 %attend_back.3.refs_1_ = bf16[2048,384]{1,0:T(8,128)(2,1)} custom-call(s32[1]{0:T(128)} %bitcast.9.me_ref, bf16[2048,512]{1,0:T(8,128)(2,1)} %get-tuple-element.205.q_ref.refs_0_, bf16[2,2048,64]{2,1,0:T(8,128)(2,1)} %get-tuple-element.143.k_ref.refs_1_, bf16[2,2048,64]{2,1,0:T(8,128)(2,1)} %get-tuple-element.144.v_ref.refs_2_, ...), custom_call_target="tpu_custom_call" | custom-call | flops 33999998976 | bytes 4194304 | tf_op jit(solution)/shard_map/attend_back/pallas_call | solution.py:572
  688.1 15.9 %sum_of.10 = (bf16[256,2048]{1,0:T(8,128)(2,1)}, bf16[256,2048]{1,0:T(8,128)(2,1)}, bf16[256,2048]{1,0:T(8,128)(2,1)}, bf16[256,2048]{1,0:T(8,128)(2,1)}) custom-call(bf16[2048,1024]{1,0:T(8,128)(2,1)} %get-tuple-element.217.refs_0_, bf16[2048,2048]{1,0:T(8,128)(2,1)} %all-gather.12.cloned.1.call-done.refs_3_.refs_2_.refs_1_, ...), custom_call_target="tpu_custom_call" | custom-call | flops 8589934592 | bytes 16777216 | tf_op jit(solution)/shard_map/sum_of/pallas_call | solution.py:572
  715.3 14.0 %outer.5 = bf16[2048,768]{1,0:T(8,128)(2,1)} custom-call(bf16[2048,2048]{1,0:T(8,128)(2,1)} %get-tuple-element.216.left_ref, bf16[2048,384]{1,0:T(8,128)(2,1)} %attend_back.2.refs_0_, bf16[2048,384]{1,0:T(8,128)(2,1)} %attend_back.3.refs_1_), custom_call_target="tpu_custom_call" | custom-call | flops 6442450944 | bytes 23068672 | tf_op jit(solution)/shard_map/outer/pallas_call | solution.py:572
  739.8 16.2 %finish.1 = bf16[512,2048]{1,0:T(8,128)(2,1)} custom-call(s32[1]{0:T(128)} %bitcast.core_ref, bf16[512,2048]{1,0:T(8,128)(2,1)} %bitcast.38, f32[512,2048]{1,0:T(8,128)} %get-tuple-element.221.middle_ref, f32[1,2048]{1,0:T(1,128)} %bitcast.51, bf16[512,384]{1,0:T(8,128)(2,1)} %get-tuple-element.261.refs_0_, ...), custom_call_target="tpu_custom_call" | custom-call | flops 6442450944 | bytes 20971520 | tf_op jit(solution)/shard_map/finish/pallas_call | solution.py:572
  756.0 13.4 %collective-permute-done.54.refs_3_ = bf16[128,2048]{1,0:T(8,128)(2,1)S(1)} collective-permute-done((bf16[128,2048]{1,0:T(8,128)(2,1)S(1)}, bf16[128,2048]{1,0:T(8,128)(2,1)S(1)}, u32[]{:S(2)}, u32[]{:S(2)}) %collective-permute-start.54) | collective-permute-done | bytes 524320 | tf_op jit(solution)/shard_map/ppermute | solution.py:41
  (349 shorter events, 319.8 us)
Async XLA Ops:
  7.2 79.2 %all-gather.6.cloned.1.call-start = ((), (), s32[]{:S(2)}) async-start(), calls=%async_computation.5 | async-start | bytes 4128768 | tf_op jit(solution)/shard_map/all_gather | solution.py:91
  11.4 92.9 %all-gather.8.cloned.1.call-start = ((), (), s32[]{:S(2)}) async-start(), calls=%async_computation.6 | async-start | bytes 2359296 | tf_op jit(solution)/shard_map/all_gather | solution.py:91
  13.3 272.6 %all-gather.12.cloned.1.call-start = ((), (), s32[]{:S(2)}) async-start(), calls=%async_computation.8 | async-start | bytes 9437184 | tf_op jit(solution)/shard_map/all_gather | solution.py:91
  22.4 45.8 %collective-permute-start.5 = (bf16[512,2048]{1,0:T(8,128)(2,1)S(1)}, bf16[512,2048]{1,0:T(8,128)(2,1)}, u32[]{:S(2)}, u32[]{:S(2)}) collective-permute-start(bf16[512,2048]{1,0:T(8,128)(2,1)S(1)} %bitcast.40), channel_id=1, source_target_pairs={{0,1},{1,0},{2,3},{3,2},{4,5},{5,4},{6,7},{7,6},{8,9},{9,8},{10,11... | collective-permute-start | bytes 6291464 | tf_op jit(solution)/shard_map/ppermute | solution.py:41
  23.0 45.5 %collective-permute-start.3 = (bf16[512,2048]{1,0:T(8,128)(2,1)S(1)}, bf16[512,2048]{1,0:T(8,128)(2,1)}, u32[]{:S(2)}, u32[]{:S(2)}) collective-permute-start(bf16[512,2048]{1,0:T(8,128)(2,1)S(1)} %bitcast.41), channel_id=1, source_target_pairs={{0,2},{1,3},{2,0},{3,1},{4,6},{5,7},{6,4},{7,5},{8,10},{9,11},{10,... | collective-permute-start | bytes 6291464 | tf_op jit(solution)/shard_map/ppermute | solution.py:41
  72.3 254.1 %all-gather.10.cloned.1.call-start = ((), (), s32[]{:S(2)}) async-start(), calls=%async_computation.7 | async-start | bytes 9437184 | tf_op jit(solution)/shard_map/all_gather | solution.py:91
  74.6 307.8 %all-gather.14.cloned.1.call-start = ((), (), s32[]{:S(2)}) async-start(), calls=%async_computation.9 | async-start | bytes 9437184 | tf_op jit(solution)/shard_map/all_gather | solution.py:91
  86.2 440.9 %reduce-scatter.8.cloned.1.call-start = ((), (), s32[]{:S(2)}) async-start(), calls=%async_computation.11 | async-start | bytes 9437184 | tf_op jit(solution)/shard_map/reduce_scatter | solution.py:95
  228.9 54.3 %collective-permute-start.20 = (bf16[512,2048]{1,0:T(8,128)(2,1)}, bf16[512,2048]{1,0:T(8,128)(2,1)}, u32[]{:S(2)}, u32[]{:S(2)}) collective-permute-start(bf16[512,2048]{1,0:T(8,128)(2,1)} %multiply_convert_fusion.refs_0_), channel_id=1, source_target_pairs={{0,1},{1,0},{2,3},{3,2},{4,5},{5,4},{6,7},{7,6},{8,9},{9,8},{10,11... | collective-permute-start | bytes 6291464 | tf_op jit(solution)/shard_map/ppermute | solution.py:41
  230.3 54.2 %collective-permute-start.19 = (bf16[512,2048]{1,0:T(8,128)(2,1)}, bf16[512,2048]{1,0:T(8,128)(2,1)}, u32[]{:S(2)}, u32[]{:S(2)}) collective-permute-start(bf16[512,2048]{1,0:T(8,128)(2,1)} %multiply_convert_fusion.refs_0_), channel_id=1, source_target_pairs={{0,2},{1,3},{2,0},{3,1},{4,6},{5,7},{6,4},{7,5},{8,10},{9,11},{10,... | collective-permute-start | bytes 6291464 | tf_op jit(solution)/shard_map/ppermute | solution.py:41
  312.5 63.4 %collective-permute-start.25 = (bf16[1024,768]{1,0:T(8,128)(2,1)}, bf16[1024,768]{1,0:T(8,128)(2,1)S(1)}, u32[]{:S(2)}, u32[]{:S(2)}) collective-permute-start(bf16[1024,768]{1,0:T(8,128)(2,1)} %constant_dynamic-slice_fusion), channel_id=1, source_target_pairs={{0,3},{1,2},{2,1},{3,0},{4,7},{5,6},{6,5},{7,4},{8,11},{9,10},{10,... | collective-permute-start | bytes 4718600 | tf_op jit(solution)/shard_map/ppermute | solution.py:41
  314.4 66.4 %collective-permute-start.24 = (bf16[1024,768]{1,0:T(8,128)(2,1)}, bf16[1024,768]{1,0:T(8,128)(2,1)S(1)}, u32[]{:S(2)}, u32[]{:S(2)}) collective-permute-start(bf16[1024,768]{1,0:T(8,128)(2,1)} %constant_dynamic-slice_fusion), channel_id=1, source_target_pairs={{0,2},{1,3},{2,0},{3,1},{4,6},{5,7},{6,4},{7,5},{8,10},{9,11},{10,... | collective-permute-start | bytes 4718600 | tf_op jit(solution)/shard_map/ppermute | solution.py:41
  315.4 65.4 %collective-permute-start.23 = (bf16[1024,768]{1,0:T(8,128)(2,1)}, bf16[1024,768]{1,0:T(8,128)(2,1)}, u32[]{:S(2)}, u32[]{:S(2)}) collective-permute-start(bf16[1024,768]{1,0:T(8,128)(2,1)} %constant_dynamic-slice_fusion), channel_id=1, source_target_pairs={{0,1},{1,0},{2,3},{3,2},{4,5},{5,4},{6,7},{7,6},{8,9},{9,8},{10,11... | collective-permute-start | bytes 4718600 | tf_op jit(solution)/shard_map/ppermute | solution.py:41
  380.8 239.7 %reduce-scatter.6.cloned.1.call-start = ((), (), s32[]{:S(2)}) async-start(), calls=%async_computation.10 | async-start | bytes 9437184 | tf_op jit(solution)/shard_map/reduce_scatter | solution.py:95
  452.9 45.4 %collective-permute-start.33 = (bf16[256,2048]{1,0:T(8,128)(2,1)}, bf16[256,2048]{1,0:T(8,128)(2,1)S(1)}, u32[]{:S(2)}, u32[]{:S(2)}) collective-permute-start(bf16[256,2048]{1,0:T(8,128)(2,1)} %add_convert_fusion.2), channel_id=1, source_target_pairs={{0,2},{1,3},{2,0},{3,1},{4,6},{5,7},{6,4},{7,5},{8,10},{9,11},{10,... | collective-permute-start | bytes 3145736 | tf_op jit(solution)/shard_map/ppermute | solution.py:41
  457.4 46.1 %collective-permute-start.31 = (bf16[256,2048]{1,0:T(8,128)(2,1)}, bf16[256,2048]{1,0:T(8,128)(2,1)S(1)}, u32[]{:S(2)}, u32[]{:S(2)}) collective-permute-start(bf16[256,2048]{1,0:T(8,128)(2,1)} %get-tuple-element.182), channel_id=1, source_target_pairs={{0,1},{1,0},{2,3},{3,2},{4,5},{5,4},{6,7},{7,6},{8,9},{9,8},{10,11... | collective-permute-start | bytes 3145736 | tf_op jit(solution)/shard_map/ppermute | solution.py:41
  458.6 44.9 %collective-permute-start.34 = (bf16[256,2048]{1,0:T(8,128)(2,1)}, bf16[256,2048]{1,0:T(8,128)(2,1)}, u32[]{:S(2)}, u32[]{:S(2)}) collective-permute-start(bf16[256,2048]{1,0:T(8,128)(2,1)} %get-tuple-element.185), channel_id=1, source_target_pairs={{0,2},{1,3},{2,0},{3,1},{4,6},{5,7},{6,4},{7,5},{8,10},{9,11},{10,... | collective-permute-start | bytes 3145736 | tf_op jit(solution)/shard_map/ppermute | solution.py:41
  504.5 264.9 %reduce-scatter.14.cloned.1.call-start = ((), (), s32[]{:S(2)}) async-start(), calls=%async_computation.14 | async-start | bytes 9437184 | tf_op jit(solution)/shard_map/reduce_scatter | solution.py:95
  569.8 205.0 %reduce-scatter.12.cloned.1.call-start = ((), (), s32[]{:S(2)}) async-start(), calls=%async_computation.13 | async-start | bytes 9437184 | tf_op jit(solution)/shard_map/reduce_scatter | solution.py:95
  614.8 208.4 %reduce-scatter.10.cloned.1.call-start = ((), (), s32[]{:S(2)}) async-start(), calls=%async_computation.12 | async-start | bytes 3538944 | tf_op jit(solution)/shard_map/reduce_scatter | solution.py:95
  617.0 46.2 %collective-permute-start.46 = (bf16[512,384]{1,0:T(8,128)(2,1)S(1)}, bf16[512,384]{1,0:T(8,128)(2,1)}, u32[]{:S(2)}, u32[]{:S(2)}) collective-permute-start(bf16[512,384]{1,0:T(8,128)(2,1)S(1)} %get-tuple-element.262), channel_id=1, source_target_pairs={{0,3},{1,2},{2,1},{3,0},{4,7},{5,6},{6,5},{7,4},{8,11},{9,10},{10,... | collective-permute-start | bytes 1179656 | tf_op jit(solution)/shard_map/ppermute | solution.py:41
  618.5 44.7 %collective-permute-start.45 = (bf16[512,384]{1,0:T(8,128)(2,1)S(1)}, bf16[512,384]{1,0:T(8,128)(2,1)}, u32[]{:S(2)}, u32[]{:S(2)}) collective-permute-start(bf16[512,384]{1,0:T(8,128)(2,1)S(1)} %get-tuple-element.263), channel_id=1, source_target_pairs={{0,2},{1,3},{2,0},{3,1},{4,6},{5,7},{6,4},{7,5},{8,10},{9,11},{10,... | collective-permute-start | bytes 1179656 | tf_op jit(solution)/shard_map/ppermute | solution.py:41
  710.8 58.6 %collective-permute-start.53 = (bf16[512,2048]{1,0:T(8,128)(2,1)}, bf16[512,2048]{1,0:T(8,128)(2,1)}, u32[]{:S(2)}, u32[]{:S(2)}) collective-permute-start(bf16[512,2048]{1,0:T(8,128)(2,1)} %pad_maximum_fusion.2), channel_id=1, source_target_pairs={{0,2},{1,3},{2,0},{3,1},{4,6},{5,7},{6,4},{7,5},{8,10},{9,11},{10,... | collective-permute-start | bytes 6291464 | tf_op jit(solution)/shard_map/ppermute | solution.py:41
  713.4 55.9 %collective-permute-start.52 = (bf16[512,2048]{1,0:T(8,128)(2,1)}, bf16[512,2048]{1,0:T(8,128)(2,1)}, u32[]{:S(2)}, u32[]{:S(2)}) collective-permute-start(bf16[512,2048]{1,0:T(8,128)(2,1)} %pad_maximum_fusion.1), channel_id=1, source_target_pairs={{0,1},{1,0},{2,3},{3,2},{4,5},{5,4},{6,7},{7,6},{8,9},{9,8},{10,11... | collective-permute-start | bytes 6291464 | tf_op jit(solution)/shard_map/ppermute | solution.py:41
  (106 other events, 2058.7 us)
Sparse Core Ops, SparseCore 0:
  11.6 45.2 all-gather.5
  59.1 27.9 all-gather.7
  88.7 81.5 all-gather.11
  171.7 80.5 all-gather.9
  253.8 80.5 all-gather.13
  380.9 89.4 reduce-scatter.7
  503.7 89.3 reduce-scatter.5
  596.0 87.9 reduce-scatter.13
  686.8 87.9 reduce-scatter.11
  777.0 38.6 reduce-scatter.9

commit v5 on v3

--- a/solution.py
+++ b/solution.py
@@ -964,7 +964,7 @@
 
 
 def outer(left, rights, wide, total=None):
-    length, tall, width = left.shape[0], 1024, rights[0].shape[1]
+    length, tall, width = left.shape[0], left.shape[1], rights[0].shape[1]
     across, count = width // wide, len(rights)
     right_spec = lambda k: pl.BlockSpec((length, wide), lambda i, j: (0, jnp.clip(j - k * across, 0, across - 1)))
     return call(
@@ -1423,7 +1423,7 @@
     w_mine = [swap(core_half(after(qkv_full, *done)[:, : kv_local * step], core), k) for k in range(1, count)]
     grad_mlp, grad_act = act_back(list(c_far), down_t, 3 * rows, length, tuple(acted))
     act_0, gate_0, up_0 = up_project(normed_two, gate_up[0], grad_act, 0)
-    grad_0 = outer(normed_two, [gate_0, up_0], 1024)
+    grad_0 = outer(normed_two, [gate_0, up_0], 512)
 
     done = (*w_mine, grad_0)
     gate_up_0 = scatter_fsdp(after(grad_0, *done))
@@ -1443,7 +1443,7 @@
     near = add_far(near, *g_far)
     g_near = send_near(near)
     [own] = sum_of(terms_after(*near), 0, rows, False)
-    grad_1 = outer(after(normed_two, own), [gate_1, up_1], 1024)
+    grad_1 = outer(after(normed_two, own), [gate_1, up_1], 512)
     gate_up_1 = scatter_fsdp(after(grad_1, *g_near))
     grad_middle, grad_attn, grad_heads = turn_back(
         core_row, after(own, grad_1), g_near, tokens_low, attn_branch, cot_low, valid_col, gain_two, out_pieces

time: 882 us -> 881 us (level)
  no operation moved by 1% of the time
where the time goes in v5:
time: 881 us; the launch traced here: 875 us
  Pallas kernels  544 us (62%)
  waiting for transfers between devices  168 us (19%)
  starting transfers between devices  70.4 us (8%)
  local copies, waits for them, and re-layouts  44.3 us (5%)
  other arithmetic  33 us (4%)
  between operations  15.8 us (2%)
    pallas_call x34, Pallas kernels, call(): pl.pallas_call(kernel, grid_spec=pltpu.PrefetchScalarGridSpec(num_scalar_...  544 us
    ppermute x65, waiting for transfers between devices, swap(): return lax.ppermute(values, 'seq', [(i, i ^ bit) for i in range(count)])  167 us
    ppermute x65, starting transfers between devices, swap(): return lax.ppermute(values, 'seq', [(i, i ^ bit) for i in range(count)])  69.1 us
  transfers between devices with their start and end apart: 79, of which 29 were waited for; matrix products, arithmetic and copies ran while one was open for 7% of the time, Pallas kernels for 61%

profile of v5, /device:TPU:0, one launch (start us, length us, event | category | flops | bytes accessed | tf_op | source)
XLA Modules:
  0.0 875.3 jit_solution(3939362096316405626)
XLA Ops:
  32.7 35.4 %collective-permute-done.5.refs_1_ = bf16[512,2048]{1,0:T(8,128)(2,1)} collective-permute-done((bf16[512,2048]{1,0:T(8,128)(2,1)S(1)}, bf16[512,2048]{1,0:T(8,128)(2,1)}, u32[]{:S(2)}, u32[]{:S(2)}) %collective-permute-start.5) | collective-permute-done | bytes 2097184 | tf_op jit(solution)/shard_map/ppermute | solution.py:41
  88.9 15.4 %enter.2 = (bf16[2048,2048]{1,0:T(8,128)(2,1)}, bf16[2048,2048]{1,0:T(8,128)(2,1)}, bf16[2048,512]{1,0:T(8,128)(2,1)}, bf16[2,2048,64]{2,1,0:T(8,128)(2,1)}, bf16[2,2048,64]{2,1,0:T(8,128)(2,1)}) custom-call(bf16[512,2048]{1,0:T(8,128)(2,1)} %bitcast.36, bf16[512,2048]{1,0:T(8,128)(2,1)} %collective-permute-done.5.refs_1_, ...), custom_call_target="tpu_custom_call" | custom-call | flops 5637144576 | bytes 25165824 | tf_op jit(solution)/shard_map/enter/pallas_call | solution.py:572
  118.0 29.2 %attend.2 = (bf16[2048,256]{1,0:T(8,128)(2,1)}, f32[1,4,2048]{2,1,0:T(4,128)}) custom-call(s32[1]{0:T(128)} %bitcast.9.me_ref, bf16[2048,512]{1,0:T(8,128)(2,1)} %get-tuple-element.204.q_ref.refs_0_, bf16[2,2048,64]{2,1,0:T(8,128)(2,1)} %get-tuple-element.142.k_ref.refs_1_, bf16[2,2048,64]{2,1,0:T(8,128)(2,1)} %get-tuple-element.143.v_ref.refs_2_, ...), custom_call_target="tpu_custom_call" | custom-call | flops 25999998976 | bytes 4194304 | tf_op jit(solution)/shard_map/attend/pallas_call | solution.py:572
  158.0 29.5 %attend.3 = (bf16[2048,256]{1,0:T(8,128)(2,1)}, f32[1,4,2048]{2,1,0:T(4,128)}) custom-call(s32[1]{0:T(128)} %bitcast.9.me_ref, bf16[2048,512]{1,0:T(8,128)(2,1)} %get-tuple-element.204.q_ref.refs_0_, bf16[2,2048,64]{2,1,0:T(8,128)(2,1)} %get-tuple-element.142.k_ref.refs_1_, bf16[2,2048,64]{2,1,0:T(8,128)(2,1)} %get-tuple-element.143.v_ref.refs_2_, ...), custom_call_target="tpu_custom_call" | custom-call | flops 25999998976 | bytes 4194304 | tf_op jit(solution)/shard_map/attend/pallas_call | solution.py:572
  194.4 19.4 %collective-permute-done.16.refs_6_.refs_5_ = bf16[2048,256]{1,0:T(8,128)(2,1)S(1)} collective-permute-done((bf16[2048,256]{1,0:T(8,128)(2,1)}, bf16[2048,256]{1,0:T(8,128)(2,1)S(1)}, u32[]{:S(2)}, u32[]{:S(2)}) %collective-permute-start.16) | collective-permute-done | bytes 1048608 | tf_op jit(solution)/shard_map/ppermute | solution.py:41
  241.8 29.0 %leave.1 = (bf16[2048,2048]{1,0:T(8,128)(2,1)}, f32[512,2048]{1,0:T(8,128)}) custom-call(s32[1]{0:T(128)} %bitcast.core_ref, bf16[2048,2048]{1,0:T(8,128)(2,1)} %get-tuple-element.156.x_ref, f32[1,2048]{1,0:T(1,128)} %bitcast.52, bf16[2048,256]{1,0:T(8,128)(2,1)} %get-tuple-element.147.refs_0_.refs_3_, bf16[2048,256]{1,0:T(8,128)(2,1)} %collective-permute-done.10.refs_1_, ...), custom_call_target="tpu_custom_call" | custom-call | flops 17179869184 | bytes 33554432 | tf_op jit(solution)/shard_map/leave/pallas_call | solution.py:572
  270.8 12.6 %collective-permute-done.20.refs_1_ = bf16[512,2048]{1,0:T(8,128)(2,1)} collective-permute-done((bf16[512,2048]{1,0:T(8,128)(2,1)}, bf16[512,2048]{1,0:T(8,128)(2,1)}, u32[]{:S(2)}, u32[]{:S(2)}) %collective-permute-start.20) | collective-permute-done | bytes 2097184 | tf_op jit(solution)/shard_map/ppermute | solution.py:41
  287.7 20.3 %act_back.2 = (bf16[2048,2048]{1,0:T(8,128)(2,1)}, bf16[2048,2048]{1,0:T(8,128)(2,1)}) custom-call(bf16[512,2048]{1,0:T(8,128)(2,1)} %multiply_convert_fusion.refs_0_, bf16[512,2048]{1,0:T(8,128)(2,1)} %collective-permute-done.20.refs_1_, bf16[512,2048]{1,0:T(8,128)(2,1)} %collective-permute-done.19.refs_2_, ...), custom_call_target="tpu_custom_call" | custom-call | flops 12884901888 | bytes 18874368 | tf_op jit(solution)/shard_map/act_back/pallas_call | solution.py:572
  326.6 25.3 %up_project.2 = (bf16[2048,1024]{1,0:T(8,128)(2,1)}, bf16[2048,1024]{1,0:T(8,128)(2,1)}, bf16[2048,1024]{1,0:T(8,128)(2,1)}) custom-call(bf16[2048,2048]{1,0:T(8,128)(2,1)} %get-tuple-element.186.normed_ref.left_ref, bf16[2048,2048]{1,0:T(8,128)(2,1)} %all-gather.10.cloned.1.call-done.gate_ref.up_ref.refs_1_.refs_3_, ...), custom_call_target="tpu_custom_call" | custom-call | flops 17179869184 | bytes 41943040 | tf_op jit(solution)/shard_map/up_project/pallas_call | solution.py:572
  351.9 24.5 %outer.3 = bf16[2048,2048]{1,0:T(8,128)(2,1)} custom-call(bf16[2048,2048]{1,0:T(8,128)(2,1)} %get-tuple-element.186.normed_ref.left_ref, bf16[2048,1024]{1,0:T(8,128)(2,1)} %get-tuple-element.185.refs_0_, bf16[2048,1024]{1,0:T(8,128)(2,1)} %get-tuple-element.170.refs_1_.refs_2_), custom_call_target="tpu_custom_call" | custom-call | flops 17179869184 | bytes 33554432 | tf_op jit(solution)/shard_map/outer/pallas_call | solution.py:572
  382.6 25.5 %up_project.3 = (bf16[2048,1024]{1,0:T(8,128)(2,1)}, bf16[2048,1024]{1,0:T(8,128)(2,1)}, bf16[2048,1024]{1,0:T(8,128)(2,1)}) custom-call(bf16[2048,2048]{1,0:T(8,128)(2,1)} %get-tuple-element.186.normed_ref.left_ref, bf16[2048,2048]{1,0:T(8,128)(2,1)} %all-gather.14.cloned.1.call-done.gate_ref.up_ref.refs_5_.refs_7_, ...), custom_call_target="tpu_custom_call" | custom-call | flops 17179869184 | bytes 41943040 | tf_op jit(solution)/shard_map/up_project/pallas_call | solution.py:572
  408.1 14.2 %sum_of.6 = (bf16[256,2048]{1,0:T(8,128)(2,1)}, bf16[256,2048]{1,0:T(8,128)(2,1)}) custom-call(bf16[2048,1024]{1,0:T(8,128)(2,1)} %get-tuple-element.185.refs_0_, bf16[2048,2048]{1,0:T(8,128)(2,1)} %all-gather.10.cloned.1.call-done.gate_ref.up_ref.refs_1_.refs_3_, bf16[2048,1024]{1,0:T(8,128)(2,1)} %get-tuple-element.170.refs_1_.refs_2_, ...), custom_call_target="tpu_custom_call" | custom-call | flops 8589934592 | bytes 23068672 | tf_op jit(solution)/shard_map/sum_of/pallas_call | solution.py:572
  424.2 25.6 %sum_of.7 = (bf16[256,2048]{1,0:T(8,128)(2,1)}, bf16[256,2048]{1,0:T(8,128)(2,1)}, bf16[256,2048]{1,0:T(8,128)(2,1)}, bf16[256,2048]{1,0:T(8,128)(2,1)}) custom-call(bf16[2048,1024]{1,0:T(8,128)(2,1)} %get-tuple-element.185.refs_0_, bf16[2048,2048]{1,0:T(8,128)(2,1)} %all-gather.10.cloned.1.call-done.gate_ref.up_ref.refs_1_.refs_3_, ...), custom_call_target="tpu_custom_call" | custom-call | flops 17179869184 | bytes 29360128 | tf_op jit(solution)/shard_map/sum_of/pallas_call | solution.py:572
  459.5 14.2 %sum_of.8.own_ref = bf16[512,2048]{1,0:T(8,128)(2,1)} custom-call(bf16[2048,1024]{1,0:T(8,128)(2,1)} %get-tuple-element.185.refs_0_, bf16[2048,2048]{1,0:T(8,128)(2,1)} %all-gather.10.cloned.1.call-done.gate_ref.up_ref.refs_1_.refs_3_, bf16[2048,1024]{1,0:T(8,128)(2,1)} %get-tuple-element.170.refs_1_.refs_2_, ...), custom_call_target="tpu_custom_call" | custom-call | flops 8589934592 | bytes 23068672 | tf_op jit(solution)/shard_map/sum_of/pallas_call | solution.py:572
  473.6 24.9 %outer.4 = bf16[2048,2048]{1,0:T(8,128)(2,1)} custom-call(bf16[2048,2048]{1,0:T(8,128)(2,1)} %get-tuple-element.186.normed_ref.left_ref, bf16[2048,1024]{1,0:T(8,128)(2,1)} %get-tuple-element.173.refs_4_.refs_0_, bf16[2048,1024]{1,0:T(8,128)(2,1)} %get-tuple-element.174.refs_6_.refs_1_), custom_call_target="tpu_custom_call" | custom-call | flops 17179869184 | bytes 33554432 | tf_op jit(solution)/shard_map/outer/pallas_call | solution.py:572
  505.4 15.9 %turn_back.1 = (f32[512,2048]{1,0:T(8,128)}, bf16[512,2048]{1,0:T(8,128)(2,1)}, bf16[4,512,512]{2,1,0:T(8,128)(2,1)}) custom-call(s32[1]{0:T(128)} %bitcast.core_ref, bf16[512,2048]{1,0:T(8,128)(2,1)} %sum_of.8.own_ref, bf16[256,2048]{1,0:T(8,128)(2,1)} %copy-done.23, bf16[256,2048]{1,0:T(8,128)(2,1)} %copy-done.22, bf16[256,2048]{1,0:T(8,128)(2,1)} %copy-done.21, ...), custom_call_target="tpu_custom_call" | custom-call | flops 4294967296 | bytes 20971520 | tf_op jit(solution)/shard_map/turn_back/pallas_call | solution.py:572
  528.9 26.9 %outer_rows.1 = bf16[16384,256]{1,0:T(8,128)(2,1)} custom-call(bf16[2048,1024]{1,0:T(8,128)(2,1)} %get-tuple-element.216.refs_0_, bf16[2048,1024]{1,0:T(8,128)(2,1)} %get-tuple-element.194.refs_1_.refs_2_, bf16[2048,2048]{1,0:T(8,128)(2,1)} %get-tuple-element.196.refs_2_), custom_call_target="tpu_custom_call" | custom-call | flops 17179869184 | bytes 16777216 | tf_op jit(solution)/shard_map/outer_rows/pallas_call | solution.py:572
  573.9 40.5 %attend_back.2.refs_0_ = bf16[2048,384]{1,0:T(8,128)(2,1)} custom-call(s32[1]{0:T(128)} %bitcast.9.me_ref, bf16[2048,512]{1,0:T(8,128)(2,1)} %get-tuple-element.204.q_ref.refs_0_, bf16[2,2048,64]{2,1,0:T(8,128)(2,1)} %get-tuple-element.142.k_ref.refs_1_, bf16[2,2048,64]{2,1,0:T(8,128)(2,1)} %get-tuple-element.143.v_ref.refs_2_, ...), custom_call_target="tpu_custom_call" | custom-call | flops 33999998976 | bytes 4194304 | tf_op jit(solution)/shard_map/attend_back/pallas_call | solution.py:572
  622.2 40.8 %attend_back.3.refs_1_ = bf16[2048,384]{1,0:T(8,128)(2,1)} custom-call(s32[1]{0:T(128)} %bitcast.9.me_ref, bf16[2048,512]{1,0:T(8,128)(2,1)} %get-tuple-element.204.q_ref.refs_0_, bf16[2,2048,64]{2,1,0:T(8,128)(2,1)} %get-tuple-element.142.k_ref.refs_1_, bf16[2,2048,64]{2,1,0:T(8,128)(2,1)} %get-tuple-element.143.v_ref.refs_2_, ...), custom_call_target="tpu_custom_call" | custom-call | flops 33999998976 | bytes 4194304 | tf_op jit(solution)/shard_map/attend_back/pallas_call | solution.py:572
  688.0 15.9 %sum_of.10 = (bf16[256,2048]{1,0:T(8,128)(2,1)}, bf16[256,2048]{1,0:T(8,128)(2,1)}, bf16[256,2048]{1,0:T(8,128)(2,1)}, bf16[256,2048]{1,0:T(8,128)(2,1)}) custom-call(bf16[2048,1024]{1,0:T(8,128)(2,1)} %get-tuple-element.216.refs_0_, bf16[2048,2048]{1,0:T(8,128)(2,1)} %all-gather.12.cloned.1.call-done.refs_3_.refs_2_.refs_1_, ...), custom_call_target="tpu_custom_call" | custom-call | flops 8589934592 | bytes 16777216 | tf_op jit(solution)/shard_map/sum_of/pallas_call | solution.py:572
  715.0 15.0 %outer.5 = bf16[2048,768]{1,0:T(8,128)(2,1)} custom-call(bf16[2048,2048]{1,0:T(8,128)(2,1)} %get-tuple-element.215.left_ref, bf16[2048,384]{1,0:T(8,128)(2,1)} %attend_back.2.refs_0_, bf16[2048,384]{1,0:T(8,128)(2,1)} %attend_back.3.refs_1_), custom_call_target="tpu_custom_call" | custom-call | flops 6442450944 | bytes 23068672 | tf_op jit(solution)/shard_map/outer/pallas_call | solution.py:572
  740.5 16.4 %finish.1 = bf16[512,2048]{1,0:T(8,128)(2,1)} custom-call(s32[1]{0:T(128)} %bitcast.core_ref, bf16[512,2048]{1,0:T(8,128)(2,1)} %bitcast.38, f32[512,2048]{1,0:T(8,128)} %get-tuple-element.220.middle_ref, f32[1,2048]{1,0:T(1,128)} %bitcast.51, bf16[512,384]{1,0:T(8,128)(2,1)} %get-tuple-element.259.refs_0_, ...), custom_call_target="tpu_custom_call" | custom-call | flops 6442450944 | bytes 20971520 | tf_op jit(solution)/shard_map/finish/pallas_call | solution.py:572
  756.9 12.3 %collective-permute-done.54.refs_3_ = bf16[128,2048]{1,0:T(8,128)(2,1)S(1)} collective-permute-done((bf16[128,2048]{1,0:T(8,128)(2,1)S(1)}, bf16[128,2048]{1,0:T(8,128)(2,1)S(1)}, u32[]{:S(2)}, u32[]{:S(2)}) %collective-permute-start.54) | collective-permute-done | bytes 524320 | tf_op jit(solution)/shard_map/ppermute | solution.py:41
  802.3 10.8 %collective-permute-done.60.refs_1_ = bf16[2048,256]{1,0:T(8,128)(2,1)S(1)} collective-permute-done((bf16[2048,256]{1,0:T(8,128)(2,1)}, bf16[2048,256]{1,0:T(8,128)(2,1)S(1)}, u32[]{:S(2)}, u32[]{:S(2)}) %collective-permute-start.60) | collective-permute-done | bytes 1048608 | tf_op jit(solution)/shard_map/ppermute | solution.py:41
  (347 shorter events, 320.1 us)
Async XLA Ops:
  7.2 79.2 %all-gather.6.cloned.1.call-start = ((), (), s32[]{:S(2)}) async-start(), calls=%async_computation.5 | async-start | bytes 4128768 | tf_op jit(solution)/shard_map/all_gather | solution.py:91
  11.4 92.9 %all-gather.8.cloned.1.call-start = ((), (), s32[]{:S(2)}) async-start(), calls=%async_computation.6 | async-start | bytes 2359296 | tf_op jit(solution)/shard_map/all_gather | solution.py:91
  13.3 272.8 %all-gather.12.cloned.1.call-start = ((), (), s32[]{:S(2)}) async-start(), calls=%async_computation.8 | async-start | bytes 9437184 | tf_op jit(solution)/shard_map/all_gather | solution.py:91
  22.4 45.8 %collective-permute-start.5 = (bf16[512,2048]{1,0:T(8,128)(2,1)S(1)}, bf16[512,2048]{1,0:T(8,128)(2,1)}, u32[]{:S(2)}, u32[]{:S(2)}) collective-permute-start(bf16[512,2048]{1,0:T(8,128)(2,1)S(1)} %bitcast.40), channel_id=1, source_target_pairs={{0,1},{1,0},{2,3},{3,2},{4,5},{5,4},{6,7},{7,6},{8,9},{9,8},{10,11... | collective-permute-start | bytes 6291464 | tf_op jit(solution)/shard_map/ppermute | solution.py:41
  23.0 45.5 %collective-permute-start.3 = (bf16[512,2048]{1,0:T(8,128)(2,1)S(1)}, bf16[512,2048]{1,0:T(8,128)(2,1)}, u32[]{:S(2)}, u32[]{:S(2)}) collective-permute-start(bf16[512,2048]{1,0:T(8,128)(2,1)S(1)} %bitcast.41), channel_id=1, source_target_pairs={{0,2},{1,3},{2,0},{3,1},{4,6},{5,7},{6,4},{7,5},{8,10},{9,11},{10,... | collective-permute-start | bytes 6291464 | tf_op jit(solution)/shard_map/ppermute | solution.py:41
  72.2 254.4 %all-gather.10.cloned.1.call-start = ((), (), s32[]{:S(2)}) async-start(), calls=%async_computation.7 | async-start | bytes 9437184 | tf_op jit(solution)/shard_map/all_gather | solution.py:91
  74.6 308.0 %all-gather.14.cloned.1.call-start = ((), (), s32[]{:S(2)}) async-start(), calls=%async_computation.9 | async-start | bytes 9437184 | tf_op jit(solution)/shard_map/all_gather | solution.py:91
  86.2 440.9 %reduce-scatter.8.cloned.1.call-start = ((), (), s32[]{:S(2)}) async-start(), calls=%async_computation.11 | async-start | bytes 9437184 | tf_op jit(solution)/shard_map/reduce_scatter | solution.py:95
  229.1 54.3 %collective-permute-start.20 = (bf16[512,2048]{1,0:T(8,128)(2,1)}, bf16[512,2048]{1,0:T(8,128)(2,1)}, u32[]{:S(2)}, u32[]{:S(2)}) collective-permute-start(bf16[512,2048]{1,0:T(8,128)(2,1)} %multiply_convert_fusion.refs_0_), channel_id=1, source_target_pairs={{0,1},{1,0},{2,3},{3,2},{4,5},{5,4},{6,7},{7,6},{8,9},{9,8},{10,11... | collective-permute-start | bytes 6291464 | tf_op jit(solution)/shard_map/ppermute | solution.py:41
  230.5 54.2 %collective-permute-start.19 = (bf16[512,2048]{1,0:T(8,128)(2,1)}, bf16[512,2048]{1,0:T(8,128)(2,1)}, u32[]{:S(2)}, u32[]{:S(2)}) collective-permute-start(bf16[512,2048]{1,0:T(8,128)(2,1)} %multiply_convert_fusion.refs_0_), channel_id=1, source_target_pairs={{0,2},{1,3},{2,0},{3,1},{4,6},{5,7},{6,4},{7,5},{8,10},{9,11},{10,... | collective-permute-start | bytes 6291464 | tf_op jit(solution)/shard_map/ppermute | solution.py:41
  313.0 63.5 %collective-permute-start.25 = (bf16[1024,768]{1,0:T(8,128)(2,1)}, bf16[1024,768]{1,0:T(8,128)(2,1)S(1)}, u32[]{:S(2)}, u32[]{:S(2)}) collective-permute-start(bf16[1024,768]{1,0:T(8,128)(2,1)} %constant_dynamic-slice_fusion), channel_id=1, source_target_pairs={{0,3},{1,2},{2,1},{3,0},{4,7},{5,6},{6,5},{7,4},{8,11},{9,10},{10,... | collective-permute-start | bytes 4718600 | tf_op jit(solution)/shard_map/ppermute | solution.py:41
  314.4 66.5 %collective-permute-start.24 = (bf16[1024,768]{1,0:T(8,128)(2,1)}, bf16[1024,768]{1,0:T(8,128)(2,1)S(1)}, u32[]{:S(2)}, u32[]{:S(2)}) collective-permute-start(bf16[1024,768]{1,0:T(8,128)(2,1)} %constant_dynamic-slice_fusion), channel_id=1, source_target_pairs={{0,2},{1,3},{2,0},{3,1},{4,6},{5,7},{6,4},{7,5},{8,10},{9,11},{10,... | collective-permute-start | bytes 4718600 | tf_op jit(solution)/shard_map/ppermute | solution.py:41
  315.5 65.3 %collective-permute-start.23 = (bf16[1024,768]{1,0:T(8,128)(2,1)}, bf16[1024,768]{1,0:T(8,128)(2,1)}, u32[]{:S(2)}, u32[]{:S(2)}) collective-permute-start(bf16[1024,768]{1,0:T(8,128)(2,1)} %constant_dynamic-slice_fusion), channel_id=1, source_target_pairs={{0,1},{1,0},{2,3},{3,2},{4,5},{5,4},{6,7},{7,6},{8,9},{9,8},{10,11... | collective-permute-start | bytes 4718600 | tf_op jit(solution)/shard_map/ppermute | solution.py:41
  380.9 239.2 %reduce-scatter.6.cloned.1.call-start = ((), (), s32[]{:S(2)}) async-start(), calls=%async_computation.10 | async-start | bytes 9437184 | tf_op jit(solution)/shard_map/reduce_scatter | solution.py:95
  452.8 45.8 %collective-permute-start.33 = (bf16[256,2048]{1,0:T(8,128)(2,1)}, bf16[256,2048]{1,0:T(8,128)(2,1)S(1)}, u32[]{:S(2)}, u32[]{:S(2)}) collective-permute-start(bf16[256,2048]{1,0:T(8,128)(2,1)} %add_convert_fusion.2), channel_id=1, source_target_pairs={{0,2},{1,3},{2,0},{3,1},{4,6},{5,7},{6,4},{7,5},{8,10},{9,11},{10,... | collective-permute-start | bytes 3145736 | tf_op jit(solution)/shard_map/ppermute | solution.py:41
  457.5 46.0 %collective-permute-start.31 = (bf16[256,2048]{1,0:T(8,128)(2,1)}, bf16[256,2048]{1,0:T(8,128)(2,1)S(1)}, u32[]{:S(2)}, u32[]{:S(2)}) collective-permute-start(bf16[256,2048]{1,0:T(8,128)(2,1)} %get-tuple-element.181), channel_id=1, source_target_pairs={{0,1},{1,0},{2,3},{3,2},{4,5},{5,4},{6,7},{7,6},{8,9},{9,8},{10,11... | collective-permute-start | bytes 3145736 | tf_op jit(solution)/shard_map/ppermute | solution.py:41
  458.6 44.9 %collective-permute-start.34 = (bf16[256,2048]{1,0:T(8,128)(2,1)}, bf16[256,2048]{1,0:T(8,128)(2,1)}, u32[]{:S(2)}, u32[]{:S(2)}) collective-permute-start(bf16[256,2048]{1,0:T(8,128)(2,1)} %get-tuple-element.184), channel_id=1, source_target_pairs={{0,2},{1,3},{2,0},{3,1},{4,6},{5,7},{6,4},{7,5},{8,10},{9,11},{10,... | collective-permute-start | bytes 3145736 | tf_op jit(solution)/shard_map/ppermute | solution.py:41
  504.5 264.8 %reduce-scatter.14.cloned.1.call-start = ((), (), s32[]{:S(2)}) async-start(), calls=%async_computation.14 | async-start | bytes 9437184 | tf_op jit(solution)/shard_map/reduce_scatter | solution.py:95
  569.7 222.0 %reduce-scatter.12.cloned.1.call-start = ((), (), s32[]{:S(2)}) async-start(), calls=%async_computation.13 | async-start | bytes 9437184 | tf_op jit(solution)/shard_map/reduce_scatter | solution.py:95
  614.4 204.6 %reduce-scatter.10.cloned.1.call-start = ((), (), s32[]{:S(2)}) async-start(), calls=%async_computation.12 | async-start | bytes 3538944 | tf_op jit(solution)/shard_map/reduce_scatter | solution.py:95
  616.7 46.4 %collective-permute-start.46 = (bf16[512,384]{1,0:T(8,128)(2,1)S(1)}, bf16[512,384]{1,0:T(8,128)(2,1)}, u32[]{:S(2)}, u32[]{:S(2)}) collective-permute-start(bf16[512,384]{1,0:T(8,128)(2,1)S(1)} %get-tuple-element.260), channel_id=1, source_target_pairs={{0,3},{1,2},{2,1},{3,0},{4,7},{5,6},{6,5},{7,4},{8,11},{9,10},{10,... | collective-permute-start | bytes 1179656 | tf_op jit(solution)/shard_map/ppermute | solution.py:41
  618.1 44.9 %collective-permute-start.45 = (bf16[512,384]{1,0:T(8,128)(2,1)S(1)}, bf16[512,384]{1,0:T(8,128)(2,1)}, u32[]{:S(2)}, u32[]{:S(2)}) collective-permute-start(bf16[512,384]{1,0:T(8,128)(2,1)S(1)} %get-tuple-element.261), channel_id=1, source_target_pairs={{0,2},{1,3},{2,0},{3,1},{4,6},{5,7},{6,4},{7,5},{8,10},{9,11},{10,... | collective-permute-start | bytes 1179656 | tf_op jit(solution)/shard_map/ppermute | solution.py:41
  710.6 58.6 %collective-permute-start.53 = (bf16[512,2048]{1,0:T(8,128)(2,1)}, bf16[512,2048]{1,0:T(8,128)(2,1)}, u32[]{:S(2)}, u32[]{:S(2)}) collective-permute-start(bf16[512,2048]{1,0:T(8,128)(2,1)} %pad_maximum_fusion.2), channel_id=1, source_target_pairs={{0,2},{1,3},{2,0},{3,1},{4,6},{5,7},{6,4},{7,5},{8,10},{9,11},{10,... | collective-permute-start | bytes 6291464 | tf_op jit(solution)/shard_map/ppermute | solution.py:41
  713.2 56.0 %collective-permute-start.52 = (bf16[512,2048]{1,0:T(8,128)(2,1)}, bf16[512,2048]{1,0:T(8,128)(2,1)}, u32[]{:S(2)}, u32[]{:S(2)}) collective-permute-start(bf16[512,2048]{1,0:T(8,128)(2,1)} %pad_maximum_fusion.1), channel_id=1, source_target_pairs={{0,1},{1,0},{2,3},{3,2},{4,5},{5,4},{6,7},{7,6},{8,9},{9,8},{10,11... | collective-permute-start | bytes 6291464 | tf_op jit(solution)/shard_map/ppermute | solution.py:41
  (105 other events, 2043.5 us)
Sparse Core Ops, SparseCore 0:
  11.6 45.2 all-gather.5
  59.1 27.9 all-gather.7
  88.7 81.5 all-gather.11
  171.7 80.5 all-gather.9
  253.8 80.6 all-gather.13
  381.0 89.5 reduce-scatter.7
  503.7 89.4 reduce-scatter.5
  596.0 87.9 reduce-scatter.13
  686.3 87.9 reduce-scatter.11
  776.5 38.6 reduce-scatter.9
